TPU v7x, 32 devices: a whole 2x2x4 slice. The times are simulated.
32 devices in a mesh: groups: 2 (over y), dp: 4 (over z), tensor: 4 (over x, core).
Axes of the slice: x: 2, y: 2, z: 4, core: 2. Of those that a mesh axis runs over, the one named last changes fastest.
Arguments:
- queries: bfloat16 [1024, 8192], P(('groups', 'dp'), 'tensor'), parts along dimension 0, may hold values from -36 to 36
- new_keys: bfloat16 [1024, 1024], P(('groups', 'dp'), 'tensor'), parts along dimension 0, may hold values from -6 to 6
- new_values: bfloat16 [1024, 1024], P(('groups', 'dp'), 'tensor'), parts along dimension 0, may hold values from -6 to 6
- key_cache: bfloat16 [1024, 96, 1024], P(('groups', 'dp'), None, 'tensor'), parts along dimension 0, may hold values from -6 to 6
- value_cache: bfloat16 [1024, 96, 1024], P(('groups', 'dp'), None, 'tensor'), parts along dimension 0, may hold values from -6 to 6
- lengths: int32 [1024], P(('groups', 'dp')), parts along dimension 0, may hold values from 2 to 96, as said below
- out_weight: bfloat16 [8192, 4096], P('tensor'), may hold values from -0.0625 to 0.0625
- down_factors: bfloat16 [12, 8192, 64], P('dp', 'tensor'), may hold values from -0.0625 to 0.0625
- up_factors: bfloat16 [12, 64, 4096], P('dp', None, 'tensor'), may hold values from -0.75 to 0.75
- assignment: int32 [1024], P(('groups', 'dp')), parts along dimension 0, may hold values from 0 to 11, as said below
- home_index: int32 [12], replicated, may hold values from 0 to 11, each once
Outputs:
- mixed: bfloat16 [1024, 4096], P(('groups', 'dp')), parts along dimension 0
There are 2 independent parts, one for each index of `groups`. A program takes and returns all parts, laid end to end along the dimension named above; an argument that names none is the same for every part. Nothing has to cross between parts.
Inputs may be any that keep to these rules, and one draw needn't show every extreme that they name: `assignment`: among the 128 requests of one index of dp no variant appears more than 26 times, and one variant appears exactly 26 times among the requests of every index of dp. `home_index`: each storage position once. `lengths`: some request of every index of dp has all 96 positions valid.
All inputs are finite; a program needn't handle non-finite values.
Results may differ from a plain program's by a relative error of at most 0.0085.
Values may be sent and summed in bfloat16 or wider, within the bound.
No kernel may reach another device: no remote copies, remote signals or barrier semaphores. Data moves between devices by JAX's collectives and lax.ppermute only.
A program may use at most 128 MiB of HBM per device.

v0:
```python
import math

import jax
import jax.numpy as jnp
from jax import lax
from jax.sharding import PartitionSpec as P

HEAD_DIM = 128


def attend(queries, new_keys, new_values, key_cache, value_cache, lengths):
    row_count = queries.shape[0]
    cache_len = key_cache.shape[1]
    kv_local = new_keys.shape[1] // HEAD_DIM
    per_group = queries.shape[1] // new_keys.shape[1]
    grouped = queries.reshape(row_count, kv_local, per_group, HEAD_DIM)
    cache_keys = key_cache.reshape(row_count, cache_len, kv_local, HEAD_DIM)
    cache_values = value_cache.reshape(row_count, cache_len, kv_local, HEAD_DIM)
    fresh_key = new_keys.reshape(row_count, kv_local, HEAD_DIM)
    fresh_value = new_values.reshape(row_count, kv_local, HEAD_DIM)
    score_scale = 1.0 / math.sqrt(HEAD_DIM)
    scores = (
        jnp.einsum("rkgd,rckd->rkgc", grouped, cache_keys, preferred_element_type=jnp.float32)
        * score_scale
    )
    usable = jnp.arange(cache_len, dtype=jnp.int32)[None, :] < lengths[:, None]
    scores = jnp.where(usable[:, None, None, :], scores, -1e30)
    own_score = (
        jnp.einsum("rkgd,rkd->rkg", grouped, fresh_key, preferred_element_type=jnp.float32)
        * score_scale
    )
    highest = jnp.maximum(jnp.max(scores, axis=-1), own_score)
    weights_raw = jnp.exp(scores - highest[..., None])
    own_raw = jnp.exp(own_score - highest)
    denominator = jnp.sum(weights_raw, axis=-1) + own_raw
    weights = (weights_raw / denominator[..., None]).astype(jnp.bfloat16)
    own_weight = (own_raw / denominator).astype(jnp.bfloat16)
    result = jnp.einsum(
        "rkgc,rckd->rkgd", weights, cache_values, preferred_element_type=jnp.float32
    )
    result = (
        result
        + own_weight.astype(jnp.float32)[..., None] * fresh_value.astype(jnp.float32)[:, :, None, :]
    )
    return result.reshape(row_count, queries.shape[1]).astype(jnp.bfloat16)


def per_device(
    queries,
    new_keys,
    new_values,
    key_cache,
    value_cache,
    lengths,
    out_weight,
    down_factors,
    up_factors,
    assignment,
    home_index,
):
    attended = attend(queries, new_keys, new_values, key_cache, value_cache, lengths)
    row_count = attended.shape[0]
    feature_width = attended.shape[1]
    dp_count = lax.axis_size("dp")
    var_local = down_factors.shape[0]
    variants = var_local * dp_count
    out_local = up_factors.shape[2]
    labels = jnp.arange(variants, dtype=jnp.int32)
    chosen = assignment[:, None] == labels[None, :]
    position = jnp.sum(jnp.where(chosen, home_index[None, :], 0), axis=1)
    capacity = max(2, 5 * row_count // (2 * variants))
    chosen_count = chosen.astype(jnp.int32)
    before = jnp.cumsum(chosen_count, axis=0) - chosen_count
    offset = jnp.sum(jnp.where(chosen, before, 0), axis=1)
    target = position * capacity + offset
    outgoing = (
        jnp.zeros((variants * capacity, feature_width), jnp.bfloat16).at[target].set(attended)
    )
    outgoing = outgoing.reshape(dp_count, var_local * capacity, feature_width)
    received = lax.all_to_all(outgoing, "dp", split_axis=0, concat_axis=0, tiled=True)
    received = received.reshape(dp_count, var_local, capacity, feature_width)
    low_rank = jnp.einsum(
        "slcf,lfk->slck", received, down_factors, preferred_element_type=jnp.float32
    )
    low_rank = lax.psum(low_rank, "tensor").astype(jnp.bfloat16)
    delta_part = jnp.einsum(
        "slck,lkd->slcd", low_rank, up_factors, preferred_element_type=jnp.float32
    )
    delta_part = delta_part.astype(jnp.bfloat16).reshape(dp_count, var_local * capacity, out_local)
    returned = lax.all_to_all(delta_part, "dp", split_axis=0, concat_axis=0, tiled=True)
    delta_rows = returned.reshape(variants * capacity, out_local)[target]
    partial_sum = jnp.dot(attended, out_weight, preferred_element_type=jnp.float32)
    summed = lax.psum(partial_sum, "tensor")
    delta_whole = lax.all_gather(delta_rows, "tensor", axis=1, tiled=True)
    return (summed + delta_whole.astype(jnp.float32)).astype(jnp.bfloat16)


def solution(mesh):
    placed = (
        P(("groups", "dp"), "tensor"),
        P(("groups", "dp"), "tensor"),
        P(("groups", "dp"), "tensor"),
        P(("groups", "dp"), None, "tensor"),
        P(("groups", "dp"), None, "tensor"),
        P(("groups", "dp")),
        P("tensor", None),
        P("dp", "tensor", None),
        P("dp", None, "tensor"),
        P(("groups", "dp")),
        P(),
    )
    return jax.shard_map(
        per_device, mesh=mesh, in_specs=placed, out_specs=P(("groups", "dp"), None), check_vma=False
    )
```

profile of v0, /device:TPU:0, one launch (start us, length us, event | category | flops | bytes accessed | tf_op | source)
XLA Modules:
  0.0 127.6 jit_solution(16861784316777538480)
XLA Ops:
  6.5 1.2 copy.51
  7.8 0.7 iota_compare_fusion.1
  8.5 0.9 reshape.90
  9.4 5.6 %fusion.42 = (f32[128,2,8]{2,1,0:T(2,128)S(1)}, f32[128,2,8,96]{3,2,1,0:T(8,128)S(1)}) fusion(bf16[128,2,8,128]{3,2,1,0:T(8,128)(2,1)S(1)} %bitcast.78, pred[128,96]{1,0:T(8,128)(4,1)S(1)} %iota_compare_fusion.1, bf16[128,96,256]{2,1,0:T(8,128)(2,1)} %param.14), kind=kOutput, calls=%fused_computation.47 | convolution fusion | flops 50919424 | bytes 7622656 | tf_op jit(solution)/shard_map/rkgd,rckd->rkgc/dot_general | solution.py:23
  15.2 0.4 fusion.43
  15.8 0.8 fusion.24
  17.3 0.2 select_reduce_fusion.1
  17.5 4.0 %fusion.14 = bf16[128,2,8,128]{3,2,1,0:T(8,128)(2,1)S(1)} fusion(f32[128,2,8,96]{3,2,1,0:T(8,128)S(1)} %get-tuple-element.10, f32[128,2,128]{2,1,0:T(2,128)S(1)} %reshape.90, f32[128,2,8]{2,1,0:T(2,128)S(1)} %copy.40, f32[128,2,8]{2,1,0:T(2,128)S(1)} %copy.38, f32[128,2,8]{2,1,0:T(2,128)S(1)} %copy.36, bf16[128,96,256]{2,1,0:T(8,128)(2,1)} %param.15), kind=kOutput, calls=%fused_computation.14 | convolution fusion | flops 51707904 | bytes 7757824 | tf_op jit(solution)/shard_map/rkgc,rckd->rkgd/dot_general | solution.py:38
  21.5 1.8 %scatter_custom_fusion = bf16[312,2048]{1,0:T(8,128)(2,1)S(1)} fusion(s32[128]{0:T(128)S(1)} %fusion.41, bf16[]{:T(256)} %constant.3.clone.1, bf16[16,8,16,128]{3,2,1,0:T(8,128)(2,1)S(1)} %bitcast.75), kind=kCustom, calls=%fused_computation.22 | custom fusion | bytes 1802242 | tf_op jit(solution)/shard_map/scatter | solution.py:77
  23.3 1.4 %reshape.86 = bf16[4,78,2048]{2,1,0:T(8,128)(2,1)} reshape(bf16[312,2048]{1,0:T(8,128)(2,1)S(1)} %scatter_custom_fusion) | data formatting | bytes 2555904 | tf_op jit(solution)/shard_map/reshape | solution.py:79
  24.7 6.3 %all-to-all-start = ((bf16[4,78,2048]{2,1,0:T(8,128)(2,1)}), bf16[4,78,2048]{2,1,0:T(8,128)(2,1)S(1)}, u32[]{:S(2)}, u32[]{:S(2)}) async-start(bf16[4,78,2048]{2,1,0:T(8,128)(2,1)} %reshape.86), calls=%async_computation | async-start | bytes 2621440 | tf_op jit(solution)/shard_map/all_to_all | solution.py:80
  31.0 9.4 %fusion.29 = f32[128,4096]{1,0:T(8,128)} fusion(bf16[2048,4096]{1,0:T(8,128)(2,1)} %param.17, bf16[16,8,16,128]{3,2,1,0:T(8,128)(2,1)S(1)} %bitcast.76), kind=kOutput, calls=%fused_computation.25 | convolution fusion | flops 2147483648 | bytes 19398656 | tf_op jit(solution)/shard_map/dot_general | solution.py:92
  40.5 21.9 %all-to-all-done = bf16[4,78,2048]{2,1,0:T(8,128)(2,1)S(1)} async-done(((bf16[4,78,2048]{2,1,0:T(8,128)(2,1)}), bf16[4,78,2048]{2,1,0:T(8,128)(2,1)S(1)}, u32[]{:S(2)}, u32[]{:S(2)}) %all-to-all-start) | async-done | bytes 1277984 | tf_op jit(solution)/shard_map/all_to_all | solution.py:80
  62.4 1.0 copy.41
  63.4 1.0 fusion.21
  64.4 12.4 %psum.15 = bf16[4,3,26,64]{3,2,0,1:T(8,128)(2,1)S(1)} all-reduce(f32[4,3,26,64]{3,2,0,1:T(8,128)S(1)} %fusion.21), channel_id=1, replica_groups=mesh['groups'=2,'dp'=4,'tensor'=4] {'tensor'}, use_global_device_ids=true, to_apply=%region_7.8 | all-reduce | flops 19968 | bytes 119808 | tf_op jit(solution)/shard_map/psum | solution.py:85
  76.9 0.3 fusion.17
  77.2 0.5 copy.43
  77.7 1.0 copy.44
  78.8 3.5 %all-to-all-start.1 = ((bf16[4,78,1024]{2,1,0:T(8,128)(2,1)}), bf16[4,78,1024]{2,1,0:T(8,128)(2,1)S(1)}, u32[]{:S(2)}, u32[]{:S(2)}) async-start(bf16[4,78,1024]{2,1,0:T(8,128)(2,1)} %copy.44), calls=%async_computation.1 | async-start | bytes 1310720 | tf_op jit(solution)/shard_map/all_to_all | solution.py:90
  82.3 18.6 %all-to-all-done.1 = bf16[4,78,1024]{2,1,0:T(8,128)(2,1)S(1)} async-done(((bf16[4,78,1024]{2,1,0:T(8,128)(2,1)}), bf16[4,78,1024]{2,1,0:T(8,128)(2,1)S(1)}, u32[]{:S(2)}, u32[]{:S(2)}) %all-to-all-start.1) | async-done | bytes 639008 | tf_op jit(solution)/shard_map/all_to_all | solution.py:90
  101.1 1.6 %gather_fusion = bf16[128,1024]{1,0:T(8,128)(2,1)} fusion(bf16[312,1024]{1,0:T(8,128)(2,1)S(1)} %reshape.89, s32[1024]{0:T(1024)S(1)} %pad_clamp_fusion), kind=kCustom, calls=%fused_computation | custom fusion | bytes 524800 | tf_op jit(solution)/shard_map/gather | solution.py:91
  102.7 15.0 %all-gather.3.cloned.1.call-done = bf16[128,4096]{1,0:T(8,128)(2,1)} async-done(((bf16[128,1024]{1,0:T(8,128)(2,1)}), bf16[128,4096]{1,0:T(8,128)(2,1)}) %all-gather.3.cloned.1.call-update) | async-done | bytes 1048592 | tf_op jit(solution)/shard_map/all_gather | solution.py:94
  117.7 3.0 %add_convert_fusion = bf16[128,4096]{1,0:T(8,128)(2,1)} fusion(f32[128,4096]{1,0:T(8,128)} %all-reduce.2.cloned.1.call-done, bf16[128,4096]{1,0:T(8,128)(2,1)} %all-gather.3.cloned.1.call-done), kind=kLoop, calls=%fused_computation.8 | loop fusion | flops 1572864 | bytes 4194304 | tf_op jit(solution)/shard_map/convert_element_type | solution.py:95
  (29 shorter events, 1.3 us)
Async XLA Ops:
  6.5 56.8 %copy-start = (bf16[3,2048,64]{1,2,0:T(8,128)(2,1)S(1)}, bf16[3,2048,64]{1,2,0:T(8,128)(2,1)}, u32[]{:S(2)}) copy-start(bf16[3,2048,64]{1,2,0:T(8,128)(2,1)} %param.18) | copy-start | bytes 2359300
  9.4 5.7 %copy-start.2 = (bf16[128,256]{1,0:T(8,128)(2,1)S(1)}, bf16[128,256]{1,0:T(8,128)(2,1)}, u32[]{:S(2)}) copy-start(bf16[128,256]{1,0:T(8,128)(2,1)} %param.12) | copy-start | bytes 196612
  15.0 2.0 %copy-start.3 = (s32[128]{0:T(128)S(1)}, s32[128]{0:T(128)}, u32[]{:S(2)}) copy-start(s32[128]{0:T(128)} %param.20) | copy-start | bytes 1540
  15.1 2.2 %copy-start.4 = (s32[12]{0:T(128)S(1)}, s32[12]{0:T(128)}, u32[]{:S(2)}) copy-start(s32[12]{0:T(128)} %param.21) | copy-start | bytes 148
  24.7 37.7 %all-to-all-start = ((bf16[4,78,2048]{2,1,0:T(8,128)(2,1)}), bf16[4,78,2048]{2,1,0:T(8,128)(2,1)S(1)}, u32[]{:S(2)}, u32[]{:S(2)}) async-start(bf16[4,78,2048]{2,1,0:T(8,128)(2,1)} %reshape.86), calls=%async_computation | async-start | bytes 2621440 | tf_op jit(solution)/shard_map/all_to_all | solution.py:80
  31.0 71.7 %all-reduce.2.cloned.1.call-start = ((), (), s32[]{:S(2)}) async-start(), calls=%async_computation.2 | async-start | bytes 4194304 | tf_op jit(solution)/shard_map/psum | solution.py:93
  63.4 13.5 %copy-start.1 = (bf16[3,64,1024]{2,1,0:T(8,128)(2,1)S(1)}, bf16[3,64,1024]{2,1,0:T(8,128)(2,1)}, u32[]{:S(2)}) copy-start(bf16[3,64,1024]{2,1,0:T(8,128)(2,1)} %param.19) | copy-start | bytes 1179652
  78.8 22.1 %all-to-all-start.1 = ((bf16[4,78,1024]{2,1,0:T(8,128)(2,1)}), bf16[4,78,1024]{2,1,0:T(8,128)(2,1)S(1)}, u32[]{:S(2)}, u32[]{:S(2)}) async-start(bf16[4,78,1024]{2,1,0:T(8,128)(2,1)} %copy.44), calls=%async_computation.1 | async-start | bytes 1310720 | tf_op jit(solution)/shard_map/all_to_all | solution.py:90
  82.2 35.4 %all-gather.3.cloned.1.call-start = ((), (), s32[]{:S(2)}) async-start(), calls=%async_computation.3 | async-start | bytes 1310720 | tf_op jit(solution)/shard_map/all_gather | solution.py:94
Sparse Core Ops, SparseCore 0:
  40.6 53.2 all-reduce.1
  102.8 14.8 all-gather.2
where the time goes:
time: 128 us
  waiting for transfers between devices  55.5 us (43%)
  matrix products  20.7 us (16%)
  between operations  13.6 us (11%)
  blocking collectives  12.4 us (10%)
  local copies, waits for them, and re-layouts  10.3 us (8%)
  starting transfers between devices  9.85 us (8%)
  other arithmetic  5.02 us (4%)
    all_to_all x1, waiting for transfers between devices, per_device(): lax.all_to_all(outgoing, 'dp', split_axis=0, concat_axis=0, tiled=True)  21.9 us
    all_to_all x1, waiting for transfers between devices, per_device(): lax.all_to_all(delta_part, 'dp', split_axis=0, concat_axis=0, tiled=True)  18.6 us
    all_gather x1, waiting for transfers between devices, per_device(): delta_whole = lax.all_gather(delta_rows, 'tensor', axis=1, tiled=True)  15 us
    psum x1, blocking collectives, per_device(): low_rank = lax.psum(low_rank, 'tensor').astype(jnp.bfloat16)  12.4 us
    dot_general x1, matrix products, per_device(): jnp.dot(attended, out_weight, preferred_element_type=jnp.float32)  9.41 us
    all_to_all x1, starting transfers between devices, per_device(): lax.all_to_all(outgoing, 'dp', split_axis=0, concat_axis=0, tiled=True)  6.32 us
    dot_general x1, matrix products, attend(): jnp.einsum('rkgd,rckd->rkgc', grouped, cache_keys, preferred_element_type...  5.6 us
    dot_general x1, matrix products, attend(): jnp.einsum('rkgc,rckd->rkgd', weights, cache_values, preferred_element_ty...  3.97 us
  transfers between devices with their start and end apart: 4, of which 3 were waited for; matrix products, arithmetic and copies ran while one was open for 12% of the time, Pallas kernels for 0%

commit v1 on v0

v1 whole, which is shorter than its diff:
```python
import functools
import math

import jax
import jax.numpy as jnp
from jax import lax
from jax.experimental import pallas as pl
from jax.experimental.pallas import tpu as pltpu
from jax.sharding import PartitionSpec as P

HEAD_DIM = 128
BLOCK = 16
VMEM_BYTES = 48 * 1024 * 1024


def row_index(assign_row, home_col, var_local, dp_count):
    rows = assign_row.shape[1]
    variants = home_col.shape[0]
    labels = lax.broadcasted_iota(jnp.int32, (variants, rows), 0)
    position = jnp.sum(
        jnp.where(labels == assign_row, home_col, 0).astype(jnp.float32), axis=0, keepdims=True
    )
    home = jnp.zeros((1, rows), jnp.int32)
    for d in range(1, dp_count):
        home = home + (position >= d * var_local - 0.5).astype(jnp.int32)
    padded = max(16, dp_count)
    same = lax.broadcasted_iota(jnp.int32, (padded, rows), 0) == home
    earlier = lax.broadcasted_iota(jnp.int32, (rows, rows), 0) < lax.broadcasted_iota(
        jnp.int32, (rows, rows), 1
    )
    before = jnp.dot(
        same.astype(jnp.float32).astype(jnp.bfloat16),
        earlier.astype(jnp.float32).astype(jnp.bfloat16),
        preferred_element_type=jnp.float32,
    )
    rank = jnp.sum(jnp.where(same, before, 0.0), axis=0, keepdims=True)
    return home, rank.astype(jnp.int32)


def column_index(assign_col, home_row, var_local, dp_count):
    rows = assign_col.shape[0]
    variants = home_row.shape[1]
    labels = lax.broadcasted_iota(jnp.int32, (rows, variants), 1)
    position = jnp.sum(
        jnp.where(labels == assign_col, home_row, 0).astype(jnp.float32), axis=1, keepdims=True
    )
    home = jnp.zeros((rows, 1), jnp.int32)
    for d in range(1, dp_count):
        home = home + (position >= d * var_local - 0.5).astype(jnp.int32)
    same = lax.broadcasted_iota(jnp.int32, (rows, 128), 1) == home
    earlier = lax.broadcasted_iota(jnp.int32, (rows, rows), 1) < lax.broadcasted_iota(
        jnp.int32, (rows, rows), 0
    )
    before = jnp.dot(
        earlier.astype(jnp.float32).astype(jnp.bfloat16),
        same.astype(jnp.float32).astype(jnp.bfloat16),
        preferred_element_type=jnp.float32,
    )
    rank = jnp.sum(jnp.where(same, before, 0.0), axis=1, keepdims=True)
    return position.astype(jnp.int32), home, rank.astype(jnp.int32)


def attend_kernel(
    heads, kv_local, cache_len, var_local, dp_count, slots,
    info_ref, q_ref, nk_ref, nv_ref, k_ref, v_ref, assign_ref, home_ref, *rest
):
    att_ref = rest[0]
    slot_refs = rest[1 : 1 + dp_count]
    q_scr, o_scr = rest[1 + dp_count :]
    step = pl.program_id(0)
    group = heads // kv_local
    scale = 1.0 / math.sqrt(HEAD_DIM)
    q = q_ref[...].astype(jnp.float32) * scale
    for h in range(heads):
        q_scr[pl.ds(h, BLOCK, stride=heads), :] = q[:, h * HEAD_DIM : (h + 1) * HEAD_DIM]
    total = BLOCK * heads
    head = lax.broadcasted_iota(jnp.int32, (total, 1), 0) % heads
    q_all = q_scr[...]
    parts = [
        jnp.where((head >= k * group) & (head < (k + 1) * group), q_all, 0.0)
        for k in range(kv_local)
    ]
    q_bd = (parts[0] if kv_local == 1 else jnp.concatenate(parts, axis=1)).astype(jnp.bfloat16)
    nt = (((1,), (1,)), ((), ()))
    own_all = lax.dot_general(q_bd, nk_ref[...], nt, preferred_element_type=jnp.float32)
    own_req = lax.broadcasted_iota(jnp.int32, (total, BLOCK), 0) // heads
    own_valid = own_req == lax.broadcasted_iota(jnp.int32, (total, BLOCK), 1)
    own_all = jnp.where(own_valid, own_all, -1e30)
    wide = 2 * cache_len
    tall = 2 * heads
    row = lax.broadcasted_iota(jnp.int32, (tall, wide), 0)
    lane = lax.broadcasted_iota(jnp.int32, (tall, wide), 1)
    first = row < heads
    lane_in = lane - jnp.where(first, 0, cache_len)
    for p in range(BLOCK // 2):
        keys = k_ref[2 * p : 2 * p + 2].reshape(wide, kv_local * HEAD_DIM)
        values = v_ref[2 * p : 2 * p + 2].reshape(wide, kv_local * HEAD_DIM)
        scores = lax.dot_general(
            q_bd[p * tall : (p + 1) * tall], keys, nt, preferred_element_type=jnp.float32
        )
        len_a = info_ref[1 + step * BLOCK + 2 * p]
        len_b = info_ref[1 + step * BLOCK + 2 * p + 1]
        valid = (lane_in >= 0) & (lane_in < jnp.where(first, jnp.minimum(len_a, cache_len), len_b))
        scores = jnp.where(valid, scores, -1e30)
        own = own_all[p * tall : (p + 1) * tall]
        highest = jnp.maximum(
            jnp.max(scores, axis=1, keepdims=True), jnp.max(own, axis=1, keepdims=True)
        )
        weights = jnp.exp(scores - highest)
        own_weights = jnp.exp(own - highest)
        denominator = jnp.sum(weights, axis=1, keepdims=True) + jnp.sum(
            own_weights, axis=1, keepdims=True
        )
        result = jnp.dot(
            weights.astype(jnp.bfloat16), values, preferred_element_type=jnp.float32
        ) + jnp.dot(
            own_weights.astype(jnp.bfloat16), nv_ref[...], preferred_element_type=jnp.float32
        )
        result = result * (1.0 / denominator)
        picked = result[:, :HEAD_DIM]
        for k in range(1, kv_local):
            picked = jnp.where(
                head[:tall] >= k * group, result[:, k * HEAD_DIM : (k + 1) * HEAD_DIM], picked
            )
        o_scr[p * tall : (p + 1) * tall, :] = picked
    where = pl.ds(pl.multiple_of(step * BLOCK, BLOCK), BLOCK)
    for h in range(heads):
        att_ref[where, h * HEAD_DIM : (h + 1) * HEAD_DIM] = o_scr[
            pl.ds(h, BLOCK, stride=heads), :
        ].astype(jnp.bfloat16)

    @pl.when(step == pl.num_programs(0) - 1)
    def _():
        rows = att_ref.shape[0]
        home, rank = row_index(assign_ref[...], home_ref[...], var_local, dp_count)
        slot = lax.broadcasted_iota(jnp.int32, (slots, rows), 0)
        attended = att_ref[...]
        for shift in range(dp_count):
            target = lax.rem(info_ref[0] + shift, dp_count)
            pick = (slot == rank) & (home == target)
            slot_refs[shift][...] = jnp.dot(
                pick.astype(jnp.float32).astype(jnp.bfloat16),
                attended,
                preferred_element_type=jnp.float32,
            ).astype(jnp.bfloat16)


def attend(
    info, queries, new_keys, new_values, key_cache, value_cache, assign_row, home_col,
    var_local, dp_count, slots,
):
    rows, width = queries.shape
    kv_width = new_keys.shape[1]
    cache_len = key_cache.shape[1]
    heads, kv_local = width // HEAD_DIM, kv_width // HEAD_DIM
    spec = pltpu.PrefetchScalarGridSpec(
        num_scalar_prefetch=1,
        grid=(rows // BLOCK,),
        in_specs=[
            pl.BlockSpec((BLOCK, width), lambda i, _: (i, 0)),
            pl.BlockSpec((BLOCK, kv_width), lambda i, _: (i, 0)),
            pl.BlockSpec((BLOCK, kv_width), lambda i, _: (i, 0)),
            pl.BlockSpec((BLOCK, cache_len, kv_width), lambda i, _: (i, 0, 0)),
            pl.BlockSpec((BLOCK, cache_len, kv_width), lambda i, _: (i, 0, 0)),
            pl.BlockSpec(assign_row.shape, lambda i, _: (0, 0)),
            pl.BlockSpec(home_col.shape, lambda i, _: (0, 0)),
        ],
        out_specs=[pl.BlockSpec((rows, width), lambda i, _: (0, 0))]
        + [pl.BlockSpec((slots, width), lambda i, _: (0, 0))] * dp_count,
        scratch_shapes=[
            pltpu.VMEM((BLOCK * heads, HEAD_DIM), jnp.float32),
            pltpu.VMEM((BLOCK * heads, HEAD_DIM), jnp.float32),
        ],
    )
    return pl.pallas_call(
        functools.partial(
            attend_kernel, heads, kv_local, cache_len, var_local, dp_count, slots
        ),
        grid_spec=spec,
        out_shape=[jax.ShapeDtypeStruct((rows, width), jnp.bfloat16)]
        + [jax.ShapeDtypeStruct((slots, width), jnp.bfloat16)] * dp_count,
        compiler_params=pltpu.CompilerParams(vmem_limit_bytes=VMEM_BYTES),
        name="attend",
    )(info, queries, new_keys, new_values, key_cache, value_cache, assign_row, home_col)


def project_kernel(ids_ref, a_ref, *refs):
    count = len(refs) // 2
    for w_ref, o_ref in zip(refs[:count], refs[count:]):
        o_ref[...] = jnp.dot(
            a_ref[...], w_ref[...], preferred_element_type=jnp.float32
        ).astype(jnp.bfloat16)


def project(ids, attended, out_weight, which, out_local):
    rows, width = attended.shape
    tile = min(256, out_local)
    tiles = out_local // tile

    def column(w):
        return lambda i, ids: (0, ids[w] * tiles + i)

    spec = pltpu.PrefetchScalarGridSpec(
        num_scalar_prefetch=1,
        grid=(tiles,),
        in_specs=[pl.BlockSpec((rows, width), lambda i, _: (0, 0))]
        + [pl.BlockSpec((width, tile), column(w)) for w in which],
        out_specs=[pl.BlockSpec((rows, tile), lambda i, _: (0, i)) for _ in which],
    )
    return pl.pallas_call(
        project_kernel,
        grid_spec=spec,
        out_shape=[jax.ShapeDtypeStruct((rows, out_local), jnp.bfloat16) for _ in which],
        compiler_params=pltpu.CompilerParams(vmem_limit_bytes=VMEM_BYTES),
        name="project",
    )(ids, attended, *([out_weight] * len(which)))


def reduce_kernel(rows_ref, down_ref, o_ref):
    for v in range(down_ref.shape[0]):
        o_ref[v] = jnp.dot(
            rows_ref[...], down_ref[v], preferred_element_type=jnp.float32
        ).astype(o_ref.dtype)


def reduce_rows(rows, down):
    return pl.pallas_call(
        reduce_kernel,
        out_shape=jax.ShapeDtypeStruct((down.shape[0], rows.shape[0], down.shape[2]), jnp.bfloat16),
        compiler_params=pltpu.CompilerParams(vmem_limit_bytes=VMEM_BYTES),
        name="reduce_rows",
    )(rows, down)


def combine_kernel(var_local, dp_count, info_ref, assign_ref, home_ref, *refs):
    o_ref = refs[-1]
    position, home, rank = column_index(assign_ref[...], home_ref[...], var_local, dp_count)
    local = position - home * var_local
    rows = assign_ref.shape[0]
    slots = refs[0].shape[1]
    slot = lax.broadcasted_iota(jnp.int32, (rows, slots), 1)
    total = jnp.zeros(o_ref.shape, jnp.float32)
    for shift in range(dp_count):
        target = lax.rem(info_ref[0] + shift, dp_count)
        mine = (slot == rank) & (home == target)
        for v in range(var_local):
            pick = (mine & (local == v)).astype(jnp.float32).astype(jnp.bfloat16)
            total = total + jnp.dot(pick, refs[shift][v], preferred_element_type=jnp.float32)
    o_ref[...] = total


def combine(info, assign_col, home_row, parts, var_local, dp_count):
    rows = assign_col.shape[0]
    rank_width = parts[0].shape[2]
    vmem = pl.BlockSpec(memory_space=pltpu.VMEM)
    return pl.pallas_call(
        functools.partial(combine_kernel, var_local, dp_count),
        in_specs=[pl.BlockSpec(memory_space=pltpu.SMEM)] + [vmem] * (2 + len(parts)),
        out_specs=vmem,
        out_shape=jax.ShapeDtypeStruct((rows, rank_width), jnp.float32),
        compiler_params=pltpu.CompilerParams(vmem_limit_bytes=VMEM_BYTES),
        name="combine",
    )(info, assign_col, home_row, *parts)


def delta_kernel(
    var_local, dp_count, info_ref, assign_ref, home_ref, low_ref, base_ref, up_ref, *refs
):
    o_ref = refs[-1]
    position, home, _ = column_index(assign_ref[...], home_ref[...], var_local, dp_count)
    low = low_ref[...].astype(jnp.bfloat16)
    rows = low.shape[0]
    half = refs[0].shape[2]

    def picked(target, v):
        return jnp.where(position == target * var_local + v, low.astype(jnp.float32), 0.0).astype(
            jnp.bfloat16
        )

    own = [picked(info_ref[0], v) for v in range(var_local)]
    others = [
        [picked(lax.rem(info_ref[0] + dp_count - shift, dp_count), v) for v in range(var_local)]
        for shift in range(1, dp_count)
    ]
    for side in range(2):
        place = lax.rem(info_ref[1] + side, 2)
        columns = pl.ds(pl.multiple_of(place * half, half), half)
        total = jnp.zeros((rows, half), jnp.float32)
        for v in range(var_local):
            total = total + jnp.dot(own[v], up_ref[v, :, columns], preferred_element_type=jnp.float32)
            for shift in range(1, dp_count):
                total = total + jnp.dot(
                    others[shift - 1][v],
                    refs[side * (dp_count - 1) + shift - 1][v],
                    preferred_element_type=jnp.float32,
                )
        o_ref[:, columns] = (base_ref[:, columns].astype(jnp.float32) + total).astype(jnp.bfloat16)


def add_delta(info, assign_col, home_row, low, base, up, near, far, var_local, dp_count):
    vmem = pl.BlockSpec(memory_space=pltpu.VMEM)
    return pl.pallas_call(
        functools.partial(delta_kernel, var_local, dp_count),
        in_specs=[pl.BlockSpec(memory_space=pltpu.SMEM)] + [vmem] * (5 + len(near) + len(far)),
        out_specs=vmem,
        out_shape=jax.ShapeDtypeStruct(base.shape, jnp.bfloat16),
        compiler_params=pltpu.CompilerParams(vmem_limit_bytes=VMEM_BYTES),
        name="add_delta",
    )(info, assign_col, home_row, low, base, up, *near, *far)


def per_device(
    queries, new_keys, new_values, key_cache, value_cache, lengths,
    out_weight, down_factors, up_factors, assignment, home_index,
):
    dp_count = lax.axis_size("dp")
    tensor_count = lax.axis_size("tensor")
    group_count = lax.axis_size("groups")
    z = lax.axis_index("dp").astype(jnp.int32)
    t = lax.axis_index("tensor").astype(jnp.int32)
    y = lax.axis_index("groups").astype(jnp.int32)
    rows = queries.shape[0]
    var_local = down_factors.shape[0]
    variants = var_local * dp_count
    out_local = up_factors.shape[2]
    capacity = max(2, 5 * rows // (2 * variants))
    slots = min(rows, -(-var_local * capacity // 16) * 16)
    bits = tensor_count.bit_length() - 1

    def along(values, axis, count, shift):
        return lax.ppermute(values, axis, [(i, (i + shift) % count) for i in range(count)])

    def across(values, bit):
        return lax.ppermute(
            values, "tensor", [(i, i ^ (1 << bit)) for i in range(tensor_count)]
        )

    half = out_local // 2
    piece = lax.dynamic_slice_in_dim(up_factors, y * half, half, axis=2)
    near, far = [], []
    for shift in range(1, dp_count):
        piece = along(piece, "dp", dp_count, 1)
        near.append(piece)
        far.append(along(piece, "groups", group_count, 1))

    assign_row, assign_col = assignment[None, :], assignment[:, None]
    home_row, home_col = home_index[None, :], home_index[:, None]
    place = jnp.stack([z, y])
    attended, *outgoing = attend(
        jnp.concatenate([z[None], lengths]), queries, new_keys, new_values, key_cache, value_cache,
        assign_row, home_col, var_local, dp_count, slots,
    )
    arrived = [outgoing[0]] + [
        along(outgoing[shift], "dp", dp_count, shift) for shift in range(1, dp_count)
    ]

    ids = t ^ jnp.arange(tensor_count, dtype=jnp.int32)
    held = {}
    order = [w for w in range(tensor_count) if w & 1] + [
        w for w in range(tensor_count) if not w & 1
    ]
    middle = tensor_count // 2
    for which in (order[:middle], order[middle:]):
        for w, product in zip(which, project(ids, attended, out_weight, which, out_local)):
            held[w] = product
    for bit in range(bits):
        kept = {}
        for w in list(held):
            if w & (1 << bit):
                continue
            got = across(held[w | (1 << bit)], bit)
            kept[w] = held[w].astype(jnp.float32) + got.astype(jnp.float32)
            if bit < bits - 1 and w:
                kept[w] = kept[w].astype(jnp.bfloat16)
        held = kept
    base = held[0]

    returned = []
    for shift in range(dp_count):
        part = reduce_rows(arrived[shift], down_factors)
        returned.append(part if shift == 0 else along(part, "dp", dp_count, dp_count - shift))
    low = combine(place, assign_col, home_row, returned, var_local, dp_count)
    for bit in range(bits):
        low = low + across(low, bit)
    mixed = add_delta(
        place, assign_col, home_row, low, base, up_factors, near, far, var_local, dp_count
    )

    pieces = {0: mixed}
    for bit in reversed(range(bits)):
        for w in list(pieces):
            pieces[w | (1 << bit)] = across(pieces[w], bit)
    whole = jnp.zeros((rows, tensor_count * out_local), jnp.bfloat16)
    for w, value in pieces.items():
        whole = lax.dynamic_update_slice(whole, value, (jnp.int32(0), (t ^ w) * out_local))
    return whole


def solution(mesh):
    placed = (
        P(("groups", "dp"), "tensor"),
        P(("groups", "dp"), "tensor"),
        P(("groups", "dp"), "tensor"),
        P(("groups", "dp"), None, "tensor"),
        P(("groups", "dp"), None, "tensor"),
        P(("groups", "dp")),
        P("tensor", None),
        P("dp", "tensor", None),
        P("dp", None, "tensor"),
        P(("groups", "dp")),
        P(),
    )
    return jax.shard_map(
        per_device, mesh=mesh, in_specs=placed, out_specs=P(("groups", "dp"), None), check_vma=False
    )
```

time: 128 us -> 114 us (0.89)
  Pallas kernels: 0 us -> 35.8 us
  matrix products: 20.7 us -> 0 us
  starting transfers between devices: 9.85 us -> 29.4 us
  waiting for transfers between devices: 55.5 us -> 38.3 us
  between operations: 13.6 us -> 0.21 us
  blocking collectives: 12.4 us -> 0 us
  local copies, waits for them, and re-layouts: 10.3 us -> 6.93 us
  other arithmetic: 5.02 us -> 2.73 us
    all_to_all x2 -> x0, waiting for transfers between devices: 40.5 us -> none  [the longest x1 21.9 us: per_device(): lax.all_to_all(outgoing, 'dp', split_axis=0, concat_axis=0, tiled=True)]
    ppermute x0 -> x20, waiting for transfers between devices: none -> 38.3 us  [the longest x12 27.8 us: along(): lax.ppermute(values, axis, [(i, (i + shift) % count) for i in range(count)])]
    pallas_call x0 -> x9, Pallas kernels: none -> 35.8 us  [the longest x1 18.7 us: attend(): pl.pallas_call(functools.partial(attend_kernel, heads, kv_local, cache_le...]
    ppermute x0 -> x20, starting transfers between devices: none -> 29.4 us  [the longest x12 25 us: along(): lax.ppermute(values, axis, [(i, (i + shift) % count) for i in range(count)])]
    dot_general x6 -> x0, matrix products: 20.7 us -> none  [the longest x1 9.41 us: per_device(): jnp.dot(attended, out_weight, preferred_element_type=jnp.float32)]
    all_gather x1 -> x0, waiting for transfers between devices: 15 us -> none  [per_device(): delta_whole = lax.all_gather(delta_rows, 'tensor', axis=1, tiled=True)]
    psum x1 -> x0, blocking collectives: 12.4 us -> none  [per_device(): low_rank = lax.psum(low_rank, 'tensor').astype(jnp.bfloat16)]
    all_to_all x2 -> x0, starting transfers between devices: 9.8 us -> none  [the longest x1 6.32 us: per_device(): lax.all_to_all(outgoing, 'dp', split_axis=0, concat_axis=0, tiled=True)]
  transfers between devices with their start and end apart: 4 -> 20, of which waited for: 3 -> 10; matrix products, arithmetic and copies ran while one was open for 12% -> 4% of each run, Pallas kernels for 0% -> 8%
where the time goes in v1:
time: 114 us; the launch traced here: 113 us
  waiting for transfers between devices  38.3 us (34%)
  Pallas kernels  35.8 us (31%)
  starting transfers between devices  29.4 us (26%)
  local copies, waits for them, and re-layouts  6.93 us (6%)
  other arithmetic  2.73 us (2%)
    ppermute x12, waiting for transfers between devices, along(): lax.ppermute(values, axis, [(i, (i + shift) % count) for i in range(count)])  27.8 us
    ppermute x12, starting transfers between devices, along(): lax.ppermute(values, axis, [(i, (i + shift) % count) for i in range(count)])  25 us
    pallas_call x1, Pallas kernels, attend(): pl.pallas_call(functools.partial(attend_kernel, heads, kv_local, cache_le...  18.7 us
    pallas_call x2, Pallas kernels, project(): pl.pallas_call(project_kernel, grid_spec=spec, out_shape=[jax.ShapeDtypeS...  11.5 us
    ppermute x8, waiting for transfers between devices, across(): lax.ppermute(values, 'tensor', [(i, i ^ 1 << bit) for i in range(tensor_c...  10.5 us
    unnamed x17, local copies, waits for them, and re-layouts  5.17 us
    ppermute x8, starting transfers between devices, across(): lax.ppermute(values, 'tensor', [(i, i ^ 1 << bit) for i in range(tensor_c...  4.4 us
  transfers between devices with their start and end apart: 20, of which 10 were waited for; matrix products, arithmetic and copies ran while one was open for 4% of the time, Pallas kernels for 8%

profile of v1, /device:TPU:0, one launch (start us, length us, event | category | flops | bytes accessed | tf_op | source)
XLA Modules:
  0.0 113.4 jit_solution(16604814241965525506)
XLA Ops:
  4.9 18.7 %attend.1 = (bf16[128,2048]{1,0:T(8,128)(2,1)S(1)}, bf16[80,2048]{1,0:T(8,128)(2,1)S(1)}, bf16[80,2048]{1,0:T(8,128)(2,1)S(1)}, bf16[80,2048]{1,0:T(8,128)(2,1)}, bf16[80,2048]{1,0:T(8,128)(2,1)}) custom-call(s32[129]{0:T(256)S(1)} %pad_add_fusion.info_ref, bf16[128,2048]{1,0:T(8,128)(2,1)S(1)} %copy-done.1, bf16[128,256]{1,0:T(8,128)(2,1)S(1)} %copy-done.2, ...), custom_call_target="tpu_custom_call" | custom-call | tf_op jit(solution)/shard_map/attend/pallas_call | solution.py:175
  23.5 6.1 %project.3 = (bf16[128,1024]{1,0:T(8,128)(2,1)}, bf16[128,1024]{1,0:T(8,128)(2,1)S(1)}) custom-call(s32[4]{0:T(128)S(1)} %iota_xor_fusion.ids_ref, bf16[128,2048]{1,0:T(8,128)(2,1)S(1)} %get-tuple-element.18.a_ref, bf16[2048,4096]{1,0:T(8,128)(2,1)} %refs_1_.3, bf16[2048,4096]{1,0:T(8,128)(2,1)} %refs_1_.3), custom_call_target="tpu_custom_call" | custom-call | tf_op jit(solution)/shard_map/project/pallas_call | solution.py:210
  30.1 2.6 %collective-permute-start.11 = (bf16[3,64,512]{2,1,0:T(8,128)(2,1)S(1)}, bf16[3,64,512]{2,1,0:T(8,128)(2,1)}, u32[]{:S(2)}, u32[]{:S(2)}) collective-permute-start(bf16[3,64,512]{2,1,0:T(8,128)(2,1)S(1)} %constant_dynamic-slice_fusion), channel_id=1, source_target_pairs={{0,4},{4,8},{8,12},{12,0},{1,5},{5,9},{9,13},{13,1},{2,6},{6,10},{... | collective-permute-start | bytes 589832 | tf_op jit(solution)/shard_map/ppermute | solution.py:331
  32.7 1.6 %collective-permute-start = (bf16[80,2048]{1,0:T(8,128)(2,1)S(1)}, bf16[80,2048]{1,0:T(8,128)(2,1)S(1)}, u32[]{:S(2)}, u32[]{:S(2)}) collective-permute-start(bf16[80,2048]{1,0:T(8,128)(2,1)S(1)} %get-tuple-element.15), channel_id=1, source_target_pairs={{0,4},{4,8},{8,12},{12,0},{1,5},{5,9},{9,13},{13,1},{2,6},{6,10},{... | collective-permute-start | bytes 983048 | tf_op jit(solution)/shard_map/ppermute | solution.py:331
  35.4 2.9 %collective-permute-start.4 = (bf16[80,2048]{1,0:T(8,128)(2,1)}, bf16[80,2048]{1,0:T(8,128)(2,1)S(1)}, u32[]{:S(2)}, u32[]{:S(2)}) collective-permute-start(bf16[80,2048]{1,0:T(8,128)(2,1)} %get-tuple-element.17), channel_id=1, source_target_pairs={{0,12},{4,0},{8,4},{12,8},{1,13},{5,1},{9,5},{13,9},{2,14},{6,2},{... | collective-permute-start | bytes 983048 | tf_op jit(solution)/shard_map/ppermute | solution.py:331
  38.3 5.5 %project.2 = (bf16[128,1024]{1,0:T(8,128)(2,1)S(1)}, bf16[128,1024]{1,0:T(8,128)(2,1)S(1)}) custom-call(s32[4]{0:T(128)S(1)} %iota_xor_fusion.ids_ref, bf16[128,2048]{1,0:T(8,128)(2,1)S(1)} %get-tuple-element.18.a_ref, bf16[2048,4096]{1,0:T(8,128)(2,1)} %refs_1_.3, bf16[2048,4096]{1,0:T(8,128)(2,1)} %refs_1_.3), custom_call_target="tpu_custom_call" | custom-call | tf_op jit(solution)/shard_map/project/pallas_call | solution.py:210
  44.7 3.0 %collective-permute-done.rows_ref = bf16[80,2048]{1,0:T(8,128)(2,1)S(1)} collective-permute-done((bf16[80,2048]{1,0:T(8,128)(2,1)S(1)}, bf16[80,2048]{1,0:T(8,128)(2,1)S(1)}, u32[]{:S(2)}, u32[]{:S(2)}) %collective-permute-start) | collective-permute-done | bytes 327712 | tf_op jit(solution)/shard_map/ppermute | solution.py:331
  47.7 1.6 %collective-permute-start.10 = (bf16[128,1024]{1,0:T(8,128)(2,1)}, bf16[128,1024]{1,0:T(8,128)(2,1)}, u32[]{:S(2)}, u32[]{:S(2)}) collective-permute-start(bf16[128,1024]{1,0:T(8,128)(2,1)} %add_convert_fusion), channel_id=1, source_target_pairs={{0,2},{1,3},{2,0},{3,1},{4,6},{5,7},{6,4},{7,5},{8,10},{9,11},{10,... | collective-permute-start | bytes 786440 | tf_op jit(solution)/shard_map/ppermute | solution.py:334
  49.3 1.8 %copy.13.down_ref = bf16[3,2048,64]{2,1,0:T(8,128)(2,1)S(1)} copy(bf16[3,2048,64]{1,2,0:T(8,128)(2,1)} %param.18) | data formatting | bytes 1572864 | tf_op args[7]
  51.5 10.2 %collective-permute-done.2.rows_ref = bf16[80,2048]{1,0:T(8,128)(2,1)S(1)} collective-permute-done((bf16[80,2048]{1,0:T(8,128)(2,1)}, bf16[80,2048]{1,0:T(8,128)(2,1)S(1)}, u32[]{:S(2)}, u32[]{:S(2)}) %collective-permute-start.2) | collective-permute-done | bytes 327712 | tf_op jit(solution)/shard_map/ppermute | solution.py:331
  61.7 8.7 %collective-permute-start.1 = (bf16[3,80,64]{2,1,0:T(8,128)(2,1)S(1)}, bf16[3,80,64]{2,1,0:T(8,128)(2,1)S(1)}, u32[]{:S(2)}, u32[]{:S(2)}) collective-permute-start(bf16[3,80,64]{2,1,0:T(8,128)(2,1)S(1)} %reduce_rows.5), channel_id=1, source_target_pairs={{0,12},{4,0},{8,4},{12,8},{1,13},{5,1},{9,5},{13,9},{2,14},{6,2},{... | collective-permute-start | bytes 92168 | tf_op jit(solution)/shard_map/ppermute | solution.py:331
  72.7 2.5 %collective-permute-start.3 = (bf16[3,80,64]{2,1,0:T(8,128)(2,1)}, bf16[3,80,64]{2,1,0:T(8,128)(2,1)S(1)}, u32[]{:S(2)}, u32[]{:S(2)}) collective-permute-start(bf16[3,80,64]{2,1,0:T(8,128)(2,1)} %reduce_rows.6), channel_id=1, source_target_pairs={{0,8},{4,12},{8,0},{12,4},{1,9},{5,13},{9,1},{13,5},{2,10},{6,14},... | collective-permute-start | bytes 92168 | tf_op jit(solution)/shard_map/ppermute | solution.py:331
  77.0 5.3 %collective-permute-done.3.refs_2_ = bf16[3,80,64]{2,1,0:T(8,128)(2,1)S(1)} collective-permute-done((bf16[3,80,64]{2,1,0:T(8,128)(2,1)}, bf16[3,80,64]{2,1,0:T(8,128)(2,1)S(1)}, u32[]{:S(2)}, u32[]{:S(2)}) %collective-permute-start.3) | collective-permute-done | bytes 30752 | tf_op jit(solution)/shard_map/ppermute | solution.py:331
  83.6 1.2 %collective-permute-done.6 = f32[128,64]{1,0:T(8,128)S(1)} collective-permute-done((f32[128,64]{1,0:T(8,128)S(1)}, f32[128,64]{1,0:T(8,128)S(1)}, u32[]{:S(2)}, u32[]{:S(2)}) %collective-permute-start.6) | collective-permute-done | bytes 32800 | tf_op jit(solution)/shard_map/ppermute | solution.py:334
  84.8 1.6 %collective-permute-start.7 = (f32[128,64]{1,0:T(8,128)S(1)}, f32[128,64]{1,0:T(8,128)S(1)}, u32[]{:S(2)}, u32[]{:S(2)}) collective-permute-start(f32[128,64]{1,0:T(8,128)S(1)} %add.30), channel_id=1, source_target_pairs={{0,2},{1,3},{2,0},{3,1},{4,6},{5,7},{6,4},{7,5},{8,10},{9,11},{10,... | collective-permute-start | bytes 98312 | tf_op jit(solution)/shard_map/ppermute | solution.py:334
  86.4 1.5 %collective-permute-start.14 = (bf16[3,64,512]{2,1,0:T(8,128)(2,1)}, bf16[3,64,512]{2,1,0:T(8,128)(2,1)S(1)}, u32[]{:S(2)}, u32[]{:S(2)}) collective-permute-start(bf16[3,64,512]{2,1,0:T(8,128)(2,1)} %collective-permute-done.11.refs_0_), channel_id=1, source_target_pairs={{0,16},{16,0},{1,17},{17,1},{2,18},{18,2},{3,19},{19,3},{4,20},{20... | collective-permute-start | bytes 589832 | tf_op jit(solution)/shard_map/ppermute | solution.py:331
  87.9 1.3 %collective-permute-done.7 = f32[128,64]{1,0:T(8,128)S(1)} collective-permute-done((f32[128,64]{1,0:T(8,128)S(1)}, f32[128,64]{1,0:T(8,128)S(1)}, u32[]{:S(2)}, u32[]{:S(2)}) %collective-permute-start.7) | collective-permute-done | bytes 32800 | tf_op jit(solution)/shard_map/ppermute | solution.py:334
  89.1 1.5 %collective-permute-start.15 = (bf16[3,64,512]{2,1,0:T(8,128)(2,1)}, bf16[3,64,512]{2,1,0:T(8,128)(2,1)S(1)}, u32[]{:S(2)}, u32[]{:S(2)}) collective-permute-start(bf16[3,64,512]{2,1,0:T(8,128)(2,1)} %collective-permute-done.12.refs_1_), channel_id=1, source_target_pairs={{0,16},{16,0},{1,17},{17,1},{2,18},{18,2},{3,19},{19,3},{4,20},{20... | collective-permute-start | bytes 589832 | tf_op jit(solution)/shard_map/ppermute | solution.py:331
  92.4 2.0 %collective-permute-done.14.refs_3_ = bf16[3,64,512]{2,1,0:T(8,128)(2,1)S(1)} collective-permute-done((bf16[3,64,512]{2,1,0:T(8,128)(2,1)}, bf16[3,64,512]{2,1,0:T(8,128)(2,1)S(1)}, u32[]{:S(2)}, u32[]{:S(2)}) %collective-permute-start.14) | collective-permute-done | bytes 196640 | tf_op jit(solution)/shard_map/ppermute | solution.py:331
  94.4 4.2 %collective-permute-done.15.refs_4_ = bf16[3,64,512]{2,1,0:T(8,128)(2,1)S(1)} collective-permute-done((bf16[3,64,512]{2,1,0:T(8,128)(2,1)}, bf16[3,64,512]{2,1,0:T(8,128)(2,1)S(1)}, u32[]{:S(2)}, u32[]{:S(2)}) %collective-permute-start.15) | collective-permute-done | bytes 196640 | tf_op jit(solution)/shard_map/ppermute | solution.py:331
  98.6 3.1 %collective-permute-done.16.refs_5_ = bf16[3,64,512]{2,1,0:T(8,128)(2,1)S(1)} collective-permute-done((bf16[3,64,512]{2,1,0:T(8,128)(2,1)S(1)}, bf16[3,64,512]{2,1,0:T(8,128)(2,1)S(1)}, u32[]{:S(2)}, u32[]{:S(2)}) %collective-permute-start.16) | collective-permute-done | bytes 196640 | tf_op jit(solution)/shard_map/ppermute | solution.py:331
  101.7 2.1 %add_delta.1 = bf16[128,1024]{1,0:T(8,128)(2,1)S(1)} custom-call(s32[2]{0:T(128)S(1)} %pad_add_fusion.1.info_ref, s32[128,1]{1,0:T(8,128)S(1)} %copy.18.assign_ref, s32[1,12]{1,0:T(1,128)S(1)} %bitcast.8, f32[128,64]{1,0:T(8,128)S(1)} %add.31.low_ref, f32[128,1024]{1,0:T(8,128)S(1)} %convert_add_fusion.base_ref, bf16[3,64,1024]{2,1,0:T(8,128)(2,1)S(1)} %copy-done, ...), custom_call_target="tpu_custom_call" | custom-call | tf_op jit(solution)/shard_map/add_delta/pallas_call | solution.py:302
  104.4 6.7 %collective-permute-done.17 = bf16[128,1024]{1,0:T(8,128)(2,1)S(1)} collective-permute-done((bf16[128,1024]{1,0:T(8,128)(2,1)S(1)}, bf16[128,1024]{1,0:T(8,128)(2,1)S(1)}, u32[]{:S(2)}, u32[]{:S(2)}) %collective-permute-start.17) | collective-permute-done | bytes 262176 | tf_op jit(solution)/shard_map/ppermute | solution.py:334
  111.3 1.3 %collective-permute-done.19 = bf16[128,1024]{1,0:T(8,128)(2,1)S(1)} collective-permute-done((bf16[128,1024]{1,0:T(8,128)(2,1)S(1)}, bf16[128,1024]{1,0:T(8,128)(2,1)S(1)}, u32[]{:S(2)}, u32[]{:S(2)}) %collective-permute-start.19) | collective-permute-done | bytes 262176 | tf_op jit(solution)/shard_map/ppermute | solution.py:334
  (57 shorter events, 16.3 us)
Async XLA Ops:
  23.5 6.5 %copy-start = (bf16[3,64,1024]{2,1,0:T(8,128)(2,1)S(1)}, bf16[3,64,1024]{2,1,0:T(8,128)(2,1)}, u32[]{:S(2)}) copy-start(bf16[3,64,1024]{2,1,0:T(8,128)(2,1)} %up_ref.1) | copy-start | bytes 1179652
  29.6 14.2 %collective-permute-start.9 = (bf16[128,1024]{1,0:T(8,128)(2,1)S(1)}, bf16[128,1024]{1,0:T(8,128)(2,1)S(1)}, u32[]{:S(2)}, u32[]{:S(2)}) collective-permute-start(bf16[128,1024]{1,0:T(8,128)(2,1)S(1)} %get-tuple-element.22), channel_id=1, source_target_pairs={{0,1},{1,0},{2,3},{3,2},{4,5},{5,4},{6,7},{7,6},{8,9},{9,8},{10,11... | collective-permute-start | bytes 786440 | tf_op jit(solution)/shard_map/ppermute | solution.py:334
  30.1 13.6 %collective-permute-start.11 = (bf16[3,64,512]{2,1,0:T(8,128)(2,1)S(1)}, bf16[3,64,512]{2,1,0:T(8,128)(2,1)}, u32[]{:S(2)}, u32[]{:S(2)}) collective-permute-start(bf16[3,64,512]{2,1,0:T(8,128)(2,1)S(1)} %constant_dynamic-slice_fusion), channel_id=1, source_target_pairs={{0,4},{4,8},{8,12},{12,0},{1,5},{5,9},{9,13},{13,1},{2,6},{6,10},{... | collective-permute-start | bytes 589832 | tf_op jit(solution)/shard_map/ppermute | solution.py:331
  32.7 14.9 %collective-permute-start = (bf16[80,2048]{1,0:T(8,128)(2,1)S(1)}, bf16[80,2048]{1,0:T(8,128)(2,1)S(1)}, u32[]{:S(2)}, u32[]{:S(2)}) collective-permute-start(bf16[80,2048]{1,0:T(8,128)(2,1)S(1)} %get-tuple-element.15), channel_id=1, source_target_pairs={{0,4},{4,8},{8,12},{12,0},{1,5},{5,9},{9,13},{13,1},{2,6},{6,10},{... | collective-permute-start | bytes 983048 | tf_op jit(solution)/shard_map/ppermute | solution.py:331
  34.3 27.4 %collective-permute-start.2 = (bf16[80,2048]{1,0:T(8,128)(2,1)}, bf16[80,2048]{1,0:T(8,128)(2,1)S(1)}, u32[]{:S(2)}, u32[]{:S(2)}) collective-permute-start(bf16[80,2048]{1,0:T(8,128)(2,1)} %get-tuple-element.16), channel_id=1, source_target_pairs={{0,8},{4,12},{8,0},{12,4},{1,9},{5,13},{9,1},{13,5},{2,10},{6,14},... | collective-permute-start | bytes 983048 | tf_op jit(solution)/shard_map/ppermute | solution.py:331
  35.4 37.3 %collective-permute-start.4 = (bf16[80,2048]{1,0:T(8,128)(2,1)}, bf16[80,2048]{1,0:T(8,128)(2,1)S(1)}, u32[]{:S(2)}, u32[]{:S(2)}) collective-permute-start(bf16[80,2048]{1,0:T(8,128)(2,1)} %get-tuple-element.17), channel_id=1, source_target_pairs={{0,12},{4,0},{8,4},{12,8},{1,13},{5,1},{9,5},{13,9},{2,14},{6,2},{... | collective-permute-start | bytes 983048 | tf_op jit(solution)/shard_map/ppermute | solution.py:331
  43.7 33.1 %copy-start.6 = (s32[128]{0:T(128)S(1)}, s32[128]{0:T(128)}, u32[]{:S(2)}) copy-start(s32[128]{0:T(128)} %param.20) | copy-start | bytes 1540
  43.7 38.5 %copy-start.4 = (s32[12]{0:T(128)S(1)}, s32[12]{0:T(128)}, u32[]{:S(2)}) copy-start(s32[12]{0:T(128)} %param.21) | copy-start | bytes 148
  43.8 47.5 %collective-permute-start.8 = (bf16[128,1024]{1,0:T(8,128)(2,1)}, bf16[128,1024]{1,0:T(8,128)(2,1)}, u32[]{:S(2)}, u32[]{:S(2)}) collective-permute-start(bf16[128,1024]{1,0:T(8,128)(2,1)} %get-tuple-element.20), channel_id=1, source_target_pairs={{0,1},{1,0},{2,3},{3,2},{4,5},{5,4},{6,7},{7,6},{8,9},{9,8},{10,11... | collective-permute-start | bytes 786440 | tf_op jit(solution)/shard_map/ppermute | solution.py:334
  43.8 26.6 %collective-permute-start.12 = (bf16[3,64,512]{2,1,0:T(8,128)(2,1)}, bf16[3,64,512]{2,1,0:T(8,128)(2,1)}, u32[]{:S(2)}, u32[]{:S(2)}) collective-permute-start(bf16[3,64,512]{2,1,0:T(8,128)(2,1)} %collective-permute-done.11.refs_0_), channel_id=1, source_target_pairs={{0,4},{4,8},{8,12},{12,0},{1,5},{5,9},{9,13},{13,1},{2,6},{6,10},{... | collective-permute-start | bytes 589832 | tf_op jit(solution)/shard_map/ppermute | solution.py:331
  47.7 43.6 %collective-permute-start.10 = (bf16[128,1024]{1,0:T(8,128)(2,1)}, bf16[128,1024]{1,0:T(8,128)(2,1)}, u32[]{:S(2)}, u32[]{:S(2)}) collective-permute-start(bf16[128,1024]{1,0:T(8,128)(2,1)} %add_convert_fusion), channel_id=1, source_target_pairs={{0,2},{1,3},{2,0},{3,1},{4,6},{5,7},{6,4},{7,5},{8,10},{9,11},{10,... | collective-permute-start | bytes 786440 | tf_op jit(solution)/shard_map/ppermute | solution.py:334
  61.7 13.9 %collective-permute-start.1 = (bf16[3,80,64]{2,1,0:T(8,128)(2,1)S(1)}, bf16[3,80,64]{2,1,0:T(8,128)(2,1)S(1)}, u32[]{:S(2)}, u32[]{:S(2)}) collective-permute-start(bf16[3,80,64]{2,1,0:T(8,128)(2,1)S(1)} %reduce_rows.5), channel_id=1, source_target_pairs={{0,12},{4,0},{8,4},{12,8},{1,13},{5,1},{9,5},{13,9},{2,14},{6,2},{... | collective-permute-start | bytes 92168 | tf_op jit(solution)/shard_map/ppermute | solution.py:331
  70.4 20.2 %collective-permute-start.13 = (bf16[3,64,512]{2,1,0:T(8,128)(2,1)}, bf16[3,64,512]{2,1,0:T(8,128)(2,1)S(1)}, u32[]{:S(2)}, u32[]{:S(2)}) collective-permute-start(bf16[3,64,512]{2,1,0:T(8,128)(2,1)} %collective-permute-done.12.refs_1_), channel_id=1, source_target_pairs={{0,4},{4,8},{8,12},{12,0},{1,5},{5,9},{9,13},{13,1},{2,6},{6,10},{... | collective-permute-start | bytes 589832 | tf_op jit(solution)/shard_map/ppermute | solution.py:331
  72.7 9.6 %collective-permute-start.3 = (bf16[3,80,64]{2,1,0:T(8,128)(2,1)}, bf16[3,80,64]{2,1,0:T(8,128)(2,1)S(1)}, u32[]{:S(2)}, u32[]{:S(2)}) collective-permute-start(bf16[3,80,64]{2,1,0:T(8,128)(2,1)} %reduce_rows.6), channel_id=1, source_target_pairs={{0,8},{4,12},{8,0},{12,4},{1,9},{5,13},{9,1},{13,5},{2,10},{6,14},... | collective-permute-start | bytes 92168 | tf_op jit(solution)/shard_map/ppermute | solution.py:331
  75.6 6.7 %collective-permute-start.5 = (bf16[3,80,64]{2,1,0:T(8,128)(2,1)S(1)}, bf16[3,80,64]{2,1,0:T(8,128)(2,1)S(1)}, u32[]{:S(2)}, u32[]{:S(2)}) collective-permute-start(bf16[3,80,64]{2,1,0:T(8,128)(2,1)S(1)} %reduce_rows.7), channel_id=1, source_target_pairs={{0,4},{4,8},{8,12},{12,0},{1,5},{5,9},{9,13},{13,1},{2,6},{6,10},{... | collective-permute-start | bytes 92168 | tf_op jit(solution)/shard_map/ppermute | solution.py:331
  83.5 1.3 %collective-permute-start.6 = (f32[128,64]{1,0:T(8,128)S(1)}, f32[128,64]{1,0:T(8,128)S(1)}, u32[]{:S(2)}, u32[]{:S(2)}) collective-permute-start(f32[128,64]{1,0:T(8,128)S(1)} %combine.1), channel_id=1, source_target_pairs={{0,1},{1,0},{2,3},{3,2},{4,5},{5,4},{6,7},{7,6},{8,9},{9,8},{10,11... | collective-permute-start | bytes 98312 | tf_op jit(solution)/shard_map/ppermute | solution.py:334
  84.8 4.3 %collective-permute-start.7 = (f32[128,64]{1,0:T(8,128)S(1)}, f32[128,64]{1,0:T(8,128)S(1)}, u32[]{:S(2)}, u32[]{:S(2)}) collective-permute-start(f32[128,64]{1,0:T(8,128)S(1)} %add.30), channel_id=1, source_target_pairs={{0,2},{1,3},{2,0},{3,1},{4,6},{5,7},{6,4},{7,5},{8,10},{9,11},{10,... | collective-permute-start | bytes 98312 | tf_op jit(solution)/shard_map/ppermute | solution.py:334
  86.4 8.0 %collective-permute-start.14 = (bf16[3,64,512]{2,1,0:T(8,128)(2,1)}, bf16[3,64,512]{2,1,0:T(8,128)(2,1)S(1)}, u32[]{:S(2)}, u32[]{:S(2)}) collective-permute-start(bf16[3,64,512]{2,1,0:T(8,128)(2,1)} %collective-permute-done.11.refs_0_), channel_id=1, source_target_pairs={{0,16},{16,0},{1,17},{17,1},{2,18},{18,2},{3,19},{19,3},{4,20},{20... | collective-permute-start | bytes 589832 | tf_op jit(solution)/shard_map/ppermute | solution.py:331
  89.1 9.4 %collective-permute-start.15 = (bf16[3,64,512]{2,1,0:T(8,128)(2,1)}, bf16[3,64,512]{2,1,0:T(8,128)(2,1)S(1)}, u32[]{:S(2)}, u32[]{:S(2)}) collective-permute-start(bf16[3,64,512]{2,1,0:T(8,128)(2,1)} %collective-permute-done.12.refs_1_), channel_id=1, source_target_pairs={{0,16},{16,0},{1,17},{17,1},{2,18},{18,2},{3,19},{19,3},{4,20},{20... | collective-permute-start | bytes 589832 | tf_op jit(solution)/shard_map/ppermute | solution.py:331
  90.7 11.0 %collective-permute-start.16 = (bf16[3,64,512]{2,1,0:T(8,128)(2,1)S(1)}, bf16[3,64,512]{2,1,0:T(8,128)(2,1)S(1)}, u32[]{:S(2)}, u32[]{:S(2)}) collective-permute-start(bf16[3,64,512]{2,1,0:T(8,128)(2,1)S(1)} %collective-permute-done.13.refs_2_), channel_id=1, source_target_pairs={{0,16},{16,0},{1,17},{17,1},{2,18},{18,2},{3,19},{19,3},{4,20},{20... | collective-permute-start | bytes 589832 | tf_op jit(solution)/shard_map/ppermute | solution.py:331
  103.8 7.3 %collective-permute-start.17 = (bf16[128,1024]{1,0:T(8,128)(2,1)S(1)}, bf16[128,1024]{1,0:T(8,128)(2,1)S(1)}, u32[]{:S(2)}, u32[]{:S(2)}) collective-permute-start(bf16[128,1024]{1,0:T(8,128)(2,1)S(1)} %add_delta.1), channel_id=1, source_target_pairs={{0,2},{1,3},{2,0},{3,1},{4,6},{5,7},{6,4},{7,5},{8,10},{9,11},{10,... | collective-permute-start | bytes 786440 | tf_op jit(solution)/shard_map/ppermute | solution.py:334
  104.4 6.8 %collective-permute-start.18 = (bf16[128,1024]{1,0:T(8,128)(2,1)S(1)}, bf16[128,1024]{1,0:T(8,128)(2,1)S(1)}, u32[]{:S(2)}, u32[]{:S(2)}) collective-permute-start(bf16[128,1024]{1,0:T(8,128)(2,1)S(1)} %add_delta.1), channel_id=1, source_target_pairs={{0,1},{1,0},{2,3},{3,2},{4,5},{5,4},{6,7},{7,6},{8,9},{9,8},{10,11... | collective-permute-start | bytes 786440 | tf_op jit(solution)/shard_map/ppermute | solution.py:334
  111.1 1.5 %collective-permute-start.19 = (bf16[128,1024]{1,0:T(8,128)(2,1)S(1)}, bf16[128,1024]{1,0:T(8,128)(2,1)S(1)}, u32[]{:S(2)}, u32[]{:S(2)}) collective-permute-start(bf16[128,1024]{1,0:T(8,128)(2,1)S(1)} %collective-permute-done.17), channel_id=1, source_target_pairs={{0,1},{1,0},{2,3},{3,2},{4,5},{5,4},{6,7},{7,6},{8,9},{9,8},{10,11... | collective-permute-start | bytes 786440 | tf_op jit(solution)/shard_map/ppermute | solution.py:334
  111.3 1.3 %copy-start.7 = (bf16[128,4096]{1,0:T(8,128)(2,1)}, bf16[128,4096]{1,0:T(8,128)(2,1)S(1)}, u32[]{:S(2)}) copy-start(bf16[128,4096]{1,0:T(8,128)(2,1)S(1)} %constant_dynamic-update-slice_fusion.1) | copy-start | bytes 3145732
  (4 other events, 3.4 us)

commit v2 on v0

v2 whole, which is shorter than its diff:
```python
import functools
import math

import jax
import jax.numpy as jnp
from jax import lax
from jax.experimental import pallas as pl
from jax.experimental.pallas import tpu as pltpu
from jax.sharding import PartitionSpec as P

HEAD_DIM = 128
BLOCK = 32
FREE = pl.CostEstimate(flops=0, bytes_accessed=0, transcendentals=0)
NT = (((1,), (1,)), ((), ()))


def params(mebibytes):
    return pltpu.CompilerParams(vmem_limit_bytes=mebibytes * 1024 * 1024)


def one_hot(mask):
    return mask.astype(jnp.float32).astype(jnp.bfloat16)


def iota(shape, axis):
    return lax.broadcasted_iota(jnp.int32, shape, axis)


def index_row(assign_row, home_ref, var_local, dp_count):
    rows = assign_row.shape[1]
    position = jnp.zeros((1, rows), jnp.int32)
    for v in range(var_local * dp_count):
        position = jnp.where(assign_row == v, home_ref[v], position)
    home = jnp.zeros((1, rows), jnp.int32)
    for d in range(1, dp_count):
        home = home + (position >= d * var_local).astype(jnp.int32)
    same = iota((max(16, dp_count), rows), 0) == home
    earlier = iota((rows, rows), 0) < iota((rows, rows), 1)
    before = jnp.dot(one_hot(same), one_hot(earlier), preferred_element_type=jnp.float32)
    rank = jnp.sum(jnp.where(same, before, 0.0), axis=0, keepdims=True)
    return position, home, rank.astype(jnp.int32)


def as_column(row):
    rows = row.shape[1]
    spread = jnp.where(iota((rows, rows), 0) == iota((rows, rows), 1), row.astype(jnp.float32), 0.0)
    return jnp.sum(spread, axis=1, keepdims=True).astype(jnp.int32)


def attend_kernel(
    var_local, dp_count, slots,
    q_hbm, nk_hbm, nv_hbm, k_hbm, v_hbm, len_hbm, assign_hbm, home_hbm, *rest
):
    att_ref = rest[0]
    slot_refs = rest[1 : 1 + dp_count]
    (q_buf, nk_buf, nv_buf, k_buf, v_buf, len_ref, assign_ref, home_ref, q_scr, o_scr,
     small_sem, k_sem, v_sem) = rest[1 + dp_count :]
    rows, width = q_buf.shape
    cache_len = k_buf.shape[1]
    heads, kv_local = width // HEAD_DIM, nk_buf.shape[1] // HEAD_DIM
    group = heads // kv_local
    blocks = rows // BLOCK
    scale = 1.0 / math.sqrt(HEAD_DIM)
    small = [
        pltpu.make_async_copy(source, target, small_sem.at[i])
        for i, (source, target) in enumerate((
            (q_hbm, q_buf), (nk_hbm, nk_buf), (nv_hbm, nv_buf), (len_hbm, len_ref),
            (assign_hbm, assign_ref), (home_hbm, home_ref),
        ))
    ]

    def cached(i):
        at = pl.ds(i * BLOCK, BLOCK)
        return (
            pltpu.make_async_copy(k_hbm.at[at], k_buf.at[at], k_sem.at[i]),
            pltpu.make_async_copy(v_hbm.at[at], v_buf.at[at], v_sem.at[i]),
        )

    for copy in small:
        copy.start()
    for i in range(blocks):
        for copy in cached(i):
            copy.start()
    for copy in small:
        copy.wait()
    total = BLOCK * heads
    head = iota((total, 1), 0) % heads
    own_valid = iota((total, BLOCK), 0) // heads == iota((total, BLOCK), 1)
    lane = iota((heads, cache_len), 1)

    def block(step, carry):
        at = pl.ds(pl.multiple_of(step * BLOCK, BLOCK), BLOCK)
        q = q_buf[at, :].astype(jnp.float32)
        for h in range(heads):
            q_scr[pl.ds(h, BLOCK, stride=heads), :] = q[:, h * HEAD_DIM : (h + 1) * HEAD_DIM]
        q_all = q_scr[...]
        parts = [
            jnp.where((head >= k * group) & (head < (k + 1) * group), q_all, 0.0)
            for k in range(kv_local)
        ]
        q_bd = (parts[0] if kv_local == 1 else jnp.concatenate(parts, axis=1)).astype(jnp.bfloat16)
        own = lax.dot_general(q_bd, nk_buf[at, :], NT, preferred_element_type=jnp.float32)
        own = jnp.where(own_valid, own * scale, -1e30)
        key_copy, value_copy = cached(step)
        key_copy.wait()
        scores = jnp.concatenate(
            [
                jnp.where(
                    lane < len_ref[step * BLOCK + r],
                    lax.dot_general(
                        q_bd[r * heads : (r + 1) * heads],
                        k_buf[step * BLOCK + r],
                        NT,
                        preferred_element_type=jnp.float32,
                    )
                    * scale,
                    -1e30,
                )
                for r in range(BLOCK)
            ],
            axis=0,
        )
        highest = jnp.maximum(
            jnp.max(scores, axis=1, keepdims=True), jnp.max(own, axis=1, keepdims=True)
        )
        weights = jnp.exp(scores - highest)
        own_weights = jnp.exp(own - highest)
        inverse = 1.0 / (
            jnp.sum(weights, axis=1, keepdims=True) + jnp.sum(own_weights, axis=1, keepdims=True)
        )
        weights = (weights * inverse).astype(jnp.bfloat16)
        own_weights = (own_weights * inverse).astype(jnp.bfloat16)
        own_result = jnp.dot(own_weights, nv_buf[at, :], preferred_element_type=jnp.float32)
        value_copy.wait()
        for r in range(BLOCK):
            mine = slice(r * heads, (r + 1) * heads)
            result = own_result[mine] + jnp.dot(
                weights[mine], v_buf[step * BLOCK + r], preferred_element_type=jnp.float32
            )
            picked = result[:, :HEAD_DIM]
            for k in range(1, kv_local):
                picked = jnp.where(
                    head[:heads] >= k * group, result[:, k * HEAD_DIM : (k + 1) * HEAD_DIM], picked
                )
            o_scr[mine, :] = picked
        for h in range(heads):
            att_ref[at, h * HEAD_DIM : (h + 1) * HEAD_DIM] = o_scr[
                pl.ds(h, BLOCK, stride=heads), :
            ].astype(jnp.bfloat16)
        return carry

    lax.fori_loop(0, blocks, block, 0)
    _, home, rank = index_row(assign_ref[...], home_ref, var_local, dp_count)
    slot = iota((slots, rows), 0)
    attended = att_ref[...]
    for shift in range(dp_count):
        pick = (slot == rank) & (home == lax.rem(lax.axis_index("dp") + shift, dp_count))
        slot_refs[shift][...] = jnp.dot(
            one_hot(pick), attended, preferred_element_type=jnp.float32
        ).astype(jnp.bfloat16)


def attend(
    queries, new_keys, new_values, key_cache, value_cache, lengths, assign_row, home_index,
    var_local, dp_count, slots,
):
    rows, width = queries.shape
    heads = width // HEAD_DIM
    blocks = rows // BLOCK
    vmem = pl.BlockSpec(memory_space=pltpu.VMEM)
    given = (queries, new_keys, new_values, key_cache, value_cache)
    return pl.pallas_call(
        functools.partial(attend_kernel, var_local, dp_count, slots),
        in_specs=[pl.BlockSpec(memory_space=pltpu.HBM)] * 8,
        out_specs=[vmem] * (1 + dp_count),
        out_shape=[jax.ShapeDtypeStruct((rows, width), jnp.bfloat16)]
        + [jax.ShapeDtypeStruct((slots, width), jnp.bfloat16)] * dp_count,
        scratch_shapes=[pltpu.VMEM(a.shape, a.dtype) for a in given]
        + [
            pltpu.SMEM(lengths.shape, jnp.int32),
            pltpu.VMEM(assign_row.shape, jnp.int32),
            pltpu.SMEM(home_index.shape, jnp.int32),
            pltpu.VMEM((BLOCK * heads, HEAD_DIM), jnp.float32),
            pltpu.VMEM((BLOCK * heads, HEAD_DIM), jnp.float32),
            pltpu.SemaphoreType.DMA((6,)),
            pltpu.SemaphoreType.DMA((blocks,)),
            pltpu.SemaphoreType.DMA((blocks,)),
        ],
        compiler_params=params(61),
        cost_estimate=FREE,
        name="attend",
    )(*given, lengths, assign_row, home_index)


def project_kernel(count, a_ref, w_hbm, *rest):
    outs, (w_buf, sem) = rest[:count], rest[count:]
    width = w_buf.shape[2]
    out_local = outs[0].shape[1]
    per = out_local // width
    me = lax.axis_index("tensor")
    order = [w for w in range(count) if w & 1] + [w for w in range(count) if not w & 1]

    def fetch(n):
        column = ((me ^ order[n // per]) * per + n % per) * width
        return pltpu.make_async_copy(
            w_hbm.at[:, pl.ds(pl.multiple_of(column, width), width)], w_buf.at[n], sem.at[n]
        )

    for n in range(count * per):
        fetch(n).start()
    attended = a_ref[...]
    for n in range(count * per):
        fetch(n).wait()
        at = slice(n % per * width, (n % per + 1) * width)
        outs[order[n // per]][:, at] = jnp.dot(
            attended, w_buf[n], preferred_element_type=jnp.float32
        ).astype(jnp.bfloat16)


def project(attended, out_weight, count, out_local):
    rows, depth = attended.shape
    width = min(512, out_local)
    tiles = out_weight.shape[1] // width
    vmem = pl.BlockSpec(memory_space=pltpu.VMEM)
    return pl.pallas_call(
        functools.partial(project_kernel, count),
        in_specs=[vmem, pl.BlockSpec(memory_space=pltpu.HBM)],
        out_specs=[vmem] * count,
        out_shape=[jax.ShapeDtypeStruct((rows, out_local), jnp.bfloat16)] * count,
        scratch_shapes=[
            pltpu.VMEM((tiles, depth, width), jnp.bfloat16),
            pltpu.SemaphoreType.DMA((tiles,)),
        ],
        compiler_params=params(44),
        cost_estimate=FREE,
        name="project",
    )(attended, out_weight)


def reduce_kernel(rows_ref, down_ref, o_ref):
    o_ref[...] = lax.dot_general(
        rows_ref[...], down_ref[...], NT, preferred_element_type=jnp.float32
    ).astype(o_ref.dtype)


def reduce_rows(rows, down):
    return pl.pallas_call(
        reduce_kernel,
        out_shape=jax.ShapeDtypeStruct((rows.shape[0], down.shape[0]), jnp.bfloat16),
        compiler_params=params(8),
        cost_estimate=FREE,
        name="reduce_rows",
    )(rows, down)


def combine_kernel(var_local, dp_count, assign_ref, home_ref, *refs):
    o_ref = refs[-1]
    index = index_row(assign_ref[...], home_ref, var_local, dp_count)
    position, home, rank = [as_column(part) for part in index]
    rows, rank_width = o_ref.shape
    slots, wide = refs[0].shape
    slot = iota((rows, slots), 1)
    total = jnp.zeros((rows, wide), jnp.float32)
    for shift in range(dp_count):
        pick = (slot == rank) & (home == lax.rem(lax.axis_index("dp") + shift, dp_count))
        total = total + jnp.dot(one_hot(pick), refs[shift][...], preferred_element_type=jnp.float32)
    local = position - home * var_local
    start = local * rank_width
    lane = iota((rows, wide), 1)
    total = jnp.where((lane >= start) & (lane < start + rank_width), total, 0.0)
    low = total[:, :rank_width]
    for v in range(1, var_local):
        low = low + total[:, v * rank_width : (v + 1) * rank_width]
    o_ref[...] = low


def combine(assign_row, home_index, parts, rank_width, var_local, dp_count):
    vmem = pl.BlockSpec(memory_space=pltpu.VMEM)
    return pl.pallas_call(
        functools.partial(combine_kernel, var_local, dp_count),
        in_specs=[vmem, pl.BlockSpec(memory_space=pltpu.SMEM)] + [vmem] * len(parts),
        out_specs=vmem,
        out_shape=jax.ShapeDtypeStruct((assign_row.shape[1], rank_width), jnp.float32),
        compiler_params=params(8),
        cost_estimate=FREE,
        name="combine",
    )(assign_row, home_index, *parts)


def delta_kernel(var_local, dp_count, assign_ref, home_ref, low_ref, got_ref, base_ref, add_ref, up_ref, *refs):
    o_ref = refs[-1]
    index = index_row(assign_ref[...], home_ref, var_local, dp_count)
    position = as_column(index[0])
    low = (low_ref[...] + got_ref[...]).astype(jnp.bfloat16)
    rows, rank_width = low.shape
    half = refs[0].shape[1]
    wide = up_ref.shape[0]
    spread = one_hot(iota((rank_width, wide), 1) % rank_width == iota((rank_width, wide), 0))
    low = jnp.dot(low, spread, preferred_element_type=jnp.float32)
    factor = iota((rows, wide), 1) // rank_width
    me = lax.axis_index("dp")

    def picked(shift):
        target = lax.rem(me + dp_count - shift, dp_count)
        return jnp.where(position == target * var_local + factor, low, 0.0).astype(jnp.bfloat16)

    mine = [picked(shift) for shift in range(dp_count)]
    for side in range(2):
        place = lax.rem(lax.axis_index("groups") + side, 2)
        columns = pl.ds(pl.multiple_of(place * half, half), half)
        total = jnp.dot(mine[0], up_ref[:, columns], preferred_element_type=jnp.float32)
        for shift in range(1, dp_count):
            total = total + jnp.dot(
                mine[shift],
                refs[side * (dp_count - 1) + shift - 1][...],
                preferred_element_type=jnp.float32,
            )
        base = base_ref[:, columns].astype(jnp.float32) + add_ref[:, columns].astype(jnp.float32)
        o_ref[:, columns] = (base + total).astype(jnp.bfloat16)


def add_delta(assign_row, home_index, low, got, base, add, up, near, far, var_local, dp_count):
    vmem = pl.BlockSpec(memory_space=pltpu.VMEM)
    return pl.pallas_call(
        functools.partial(delta_kernel, var_local, dp_count),
        in_specs=[vmem, pl.BlockSpec(memory_space=pltpu.SMEM)] + [vmem] * (5 + len(near) + len(far)),
        out_specs=vmem,
        out_shape=jax.ShapeDtypeStruct(base.shape, jnp.bfloat16),
        compiler_params=params(16),
        cost_estimate=FREE,
        name="add_delta",
    )(assign_row, home_index, low, got, base, add, up, *near, *far)


def per_device(
    queries, new_keys, new_values, key_cache, value_cache, lengths,
    out_weight, down_factors, up_factors, assignment, home_index,
):
    dp_count = lax.axis_size("dp")
    tensor_count = lax.axis_size("tensor")
    group_count = lax.axis_size("groups")
    t = lax.axis_index("tensor").astype(jnp.int32)
    y = lax.axis_index("groups").astype(jnp.int32)
    rows = queries.shape[0]
    var_local, _, rank_width = down_factors.shape
    variants = var_local * dp_count
    out_local = up_factors.shape[2]
    capacity = max(2, 5 * rows // (2 * variants))
    slots = min(rows, -(-var_local * capacity // 16) * 16)
    bits = tensor_count.bit_length() - 1

    def along(values, axis, count, shift):
        return lax.ppermute(values, axis, [(i, (i + shift) % count) for i in range(count)])

    def across(values, bit):
        return lax.ppermute(
            values, "tensor", [(i, i ^ (1 << bit)) for i in range(tensor_count)]
        )

    half = out_local // 2
    up = up_factors.reshape(var_local * rank_width, out_local)
    piece = lax.dynamic_slice_in_dim(up, y * half, half, axis=1)
    near, far = [], []
    for _ in range(1, dp_count):
        piece = along(piece, "dp", dp_count, 1)
        near.append(piece)
        far.append(along(piece, "groups", group_count, 1))

    assign_row = assignment[None, :]
    attended, *outgoing = attend(
        queries, new_keys, new_values, key_cache, value_cache, lengths, assign_row, home_index,
        var_local, dp_count, slots,
    )
    arrived = [outgoing[0]] + [
        along(outgoing[shift], "dp", dp_count, shift) for shift in range(1, dp_count)
    ]

    held = dict(enumerate(project(attended, out_weight, tensor_count, out_local)))
    for bit in range(bits):
        kept = {}
        for w in list(held):
            if w & (1 << bit):
                continue
            got = across(held[w | (1 << bit)], bit)
            if bit == bits - 1:
                add = got
                kept[w] = held[w]
            else:
                kept[w] = held[w].astype(jnp.float32) + got.astype(jnp.float32)
                if w:
                    kept[w] = kept[w].astype(jnp.bfloat16)
        held = kept

    down = jnp.swapaxes(down_factors, 1, 2).reshape(var_local * rank_width, -1)
    returned = []
    for shift in range(dp_count):
        part = reduce_rows(arrived[shift], down)
        returned.append(part if shift == 0 else along(part, "dp", dp_count, dp_count - shift))
    low = combine(assign_row, home_index, returned, rank_width, var_local, dp_count)
    for bit in range(bits - 1):
        low = low + across(low, bit)
    low_got = across(low, bits - 1)
    mixed = add_delta(
        assign_row, home_index, low, low_got, held[0], add, up, near, far, var_local, dp_count
    )

    pieces = {0: mixed}
    for bit in reversed(range(bits)):
        for w in list(pieces):
            pieces[w | (1 << bit)] = across(pieces[w], bit)
    whole = jnp.zeros((rows, tensor_count * out_local), jnp.bfloat16)
    for w, value in pieces.items():
        whole = lax.dynamic_update_slice(whole, value, (jnp.int32(0), (t ^ w) * out_local))
    return whole


def solution(mesh):
    placed = (
        P(("groups", "dp"), "tensor"),
        P(("groups", "dp"), "tensor"),
        P(("groups", "dp"), "tensor"),
        P(("groups", "dp"), None, "tensor"),
        P(("groups", "dp"), None, "tensor"),
        P(("groups", "dp")),
        P("tensor", None),
        P("dp", "tensor", None),
        P("dp", None, "tensor"),
        P(("groups", "dp")),
        P(),
    )
    return jax.shard_map(
        per_device, mesh=mesh, in_specs=placed, out_specs=P(("groups", "dp"), None), check_vma=False
    )
```

time: 128 us -> 86.7 us (0.68)
  waiting for transfers between devices: 55.5 us -> 29.5 us
  starting transfers between devices: 9.85 us -> 32.4 us
  Pallas kernels: 0 us -> 21.5 us
  matrix products: 20.7 us -> 0 us
  between operations: 13.6 us -> 0.18 us
  blocking collectives: 12.4 us -> 0 us
  local copies, waits for them, and re-layouts: 10.3 us -> 2.9 us
  other arithmetic: 5.02 us -> 0.13 us
    all_to_all x2 -> x0, waiting for transfers between devices: 40.5 us -> none  [the longest x1 21.9 us: per_device(): lax.all_to_all(outgoing, 'dp', split_axis=0, concat_axis=0, tiled=True)]
    ppermute x0 -> x20, starting transfers between devices: none -> 32.4 us  [the longest x12 29.4 us: along(): lax.ppermute(values, axis, [(i, (i + shift) % count) for i in range(count)])]
    ppermute x0 -> x20, waiting for transfers between devices: none -> 29.5 us  [the longest x12 21 us: along(): lax.ppermute(values, axis, [(i, (i + shift) % count) for i in range(count)])]
    pallas_call x0 -> x8, Pallas kernels: none -> 21.5 us  [the longest x1 11.3 us: attend(): pl.pallas_call(functools.partial(attend_kernel, var_local, dp_count, slot...]
    dot_general x6 -> x0, matrix products: 20.7 us -> none  [the longest x1 9.41 us: per_device(): jnp.dot(attended, out_weight, preferred_element_type=jnp.float32)]
    all_gather x1 -> x0, waiting for transfers between devices: 15 us -> none  [per_device(): delta_whole = lax.all_gather(delta_rows, 'tensor', axis=1, tiled=True)]
    psum x1 -> x0, blocking collectives: 12.4 us -> none  [per_device(): low_rank = lax.psum(low_rank, 'tensor').astype(jnp.bfloat16)]
    all_to_all x2 -> x0, starting transfers between devices: 9.8 us -> none  [the longest x1 6.32 us: per_device(): lax.all_to_all(outgoing, 'dp', split_axis=0, concat_axis=0, tiled=True)]
  transfers between devices with their start and end apart: 4 -> 20, of which waited for: 3 -> 10; matrix products, arithmetic and copies ran while one was open for 12% -> 0% of each run, Pallas kernels for 0% -> 24%
where the time goes in v2:
time: 86.7 us; the launch traced here: 86.6 us
  starting transfers between devices  32.4 us (37%)
  waiting for transfers between devices  29.5 us (34%)
  Pallas kernels  21.5 us (25%)
  local copies, waits for them, and re-layouts  2.9 us (3%)
    ppermute x12, starting transfers between devices, along(): lax.ppermute(values, axis, [(i, (i + shift) % count) for i in range(count)])  29.4 us
    ppermute x12, waiting for transfers between devices, along(): lax.ppermute(values, axis, [(i, (i + shift) % count) for i in range(count)])  21 us
    pallas_call x1, Pallas kernels, attend(): pl.pallas_call(functools.partial(attend_kernel, var_local, dp_count, slot...  11.3 us
    ppermute x8, waiting for transfers between devices, across(): lax.ppermute(values, 'tensor', [(i, i ^ 1 << bit) for i in range(tensor_c...  8.49 us
    pallas_call x1, Pallas kernels, project(): pl.pallas_call(functools.partial(project_kernel, count), in_specs=[vmem,...  6.58 us
    ppermute x8, starting transfers between devices, across(): lax.ppermute(values, 'tensor', [(i, i ^ 1 << bit) for i in range(tensor_c...  2.91 us
  transfers between devices with their start and end apart: 20, of which 10 were waited for; matrix products, arithmetic and copies ran while one was open for 0% of the time, Pallas kernels for 24%

profile of v2, /device:TPU:0, one launch (start us, length us, event | category | flops | bytes accessed | tf_op | source)
XLA Modules:
  0.0 86.6 jit_solution(12127895677795330109)
XLA Ops:
  0.9 3.1 %collective-permute-start.11 = (bf16[192,512]{1,0:T(8,128)(2,1)S(1)}, bf16[192,512]{1,0:T(8,128)(2,1)S(1)}, u32[]{:S(2)}, u32[]{:S(2)}) collective-permute-start(bf16[192,512]{1,0:T(8,128)(2,1)S(1)} %constant_dynamic-slice_fusion), channel_id=1, source_target_pairs={{0,4},{4,8},{8,12},{12,0},{1,5},{5,9},{9,13},{13,1},{2,6},{6,10},{... | collective-permute-start | bytes 589832 | tf_op jit(solution)/shard_map/ppermute | solution.py:353
  4.0 11.3 %attend.1 = (bf16[128,2048]{1,0:T(8,128)(2,1)}, bf16[80,2048]{1,0:T(8,128)(2,1)}, bf16[80,2048]{1,0:T(8,128)(2,1)}, bf16[80,2048]{1,0:T(8,128)(2,1)}, bf16[80,2048]{1,0:T(8,128)(2,1)}) custom-call(bf16[128,2048]{1,0:T(8,128)(2,1)} %q_hbm.1, bf16[128,256]{1,0:T(8,128)(2,1)} %nk_hbm.1, bf16[128,256]{1,0:T(8,128)(2,1)} %nv_hbm.1, bf16[128,96,256]{2,1,0:T(8,128)(2,1)} %k_hbm.1, ...), custom_call_target="tpu_custom_call" | custom-call | tf_op jit(solution)/shard_map/attend/pallas_call | solution.py:172
  15.3 1.6 %collective-permute-start = (bf16[80,2048]{1,0:T(8,128)(2,1)}, bf16[80,2048]{1,0:T(8,128)(2,1)S(1)}, u32[]{:S(2)}, u32[]{:S(2)}) collective-permute-start(bf16[80,2048]{1,0:T(8,128)(2,1)} %get-tuple-element.15), channel_id=1, source_target_pairs={{0,4},{4,8},{8,12},{12,0},{1,5},{5,9},{9,13},{13,1},{2,6},{6,10},{... | collective-permute-start | bytes 983048 | tf_op jit(solution)/shard_map/ppermute | solution.py:353
  16.9 1.1 %collective-permute-start.2 = (bf16[80,2048]{1,0:T(8,128)(2,1)}, bf16[80,2048]{1,0:T(8,128)(2,1)S(1)}, u32[]{:S(2)}, u32[]{:S(2)}) collective-permute-start(bf16[80,2048]{1,0:T(8,128)(2,1)} %get-tuple-element.16), channel_id=1, source_target_pairs={{0,8},{4,12},{8,0},{12,4},{1,9},{5,13},{9,1},{13,5},{2,10},{6,14},... | collective-permute-start | bytes 983048 | tf_op jit(solution)/shard_map/ppermute | solution.py:353
  18.0 2.8 %collective-permute-start.4 = (bf16[80,2048]{1,0:T(8,128)(2,1)}, bf16[80,2048]{1,0:T(8,128)(2,1)S(1)}, u32[]{:S(2)}, u32[]{:S(2)}) collective-permute-start(bf16[80,2048]{1,0:T(8,128)(2,1)} %get-tuple-element.17), channel_id=1, source_target_pairs={{0,12},{4,0},{8,4},{12,8},{1,13},{5,1},{9,5},{13,9},{2,14},{6,2},{... | collective-permute-start | bytes 983048 | tf_op jit(solution)/shard_map/ppermute | solution.py:353
  20.9 1.0 %copy-done.2 = bf16[128,2048]{1,0:T(8,128)(2,1)S(1)} copy-done((bf16[128,2048]{1,0:T(8,128)(2,1)S(1)}, bf16[128,2048]{1,0:T(8,128)(2,1)}, u32[]{:S(2)}) %copy-start.2) | copy-done | bytes 524312
  21.9 6.6 %project.1 = (bf16[128,1024]{1,0:T(8,128)(2,1)S(1)}, bf16[128,1024]{1,0:T(8,128)(2,1)S(1)}, bf16[128,1024]{1,0:T(8,128)(2,1)S(1)}, bf16[128,1024]{1,0:T(8,128)(2,1)S(1)}) custom-call(bf16[128,2048]{1,0:T(8,128)(2,1)S(1)} %copy-done.2, bf16[2048,4096]{1,0:T(8,128)(2,1)} %w_hbm.1), custom_call_target="tpu_custom_call" | custom-call | tf_op jit(solution)/shard_map/project/pallas_call | solution.py:225
  29.1 3.8 %collective-permute-start.1 = (bf16[80,192]{1,0:T(8,128)(2,1)S(1)}, bf16[80,192]{1,0:T(8,128)(2,1)S(1)}, u32[]{:S(2)}, u32[]{:S(2)}) collective-permute-start(bf16[80,192]{1,0:T(8,128)(2,1)S(1)} %reduce_rows.5), channel_id=1, source_target_pairs={{0,12},{4,0},{8,4},{12,8},{1,13},{5,1},{9,5},{13,9},{2,14},{6,2},{... | collective-permute-start | bytes 92168 | tf_op jit(solution)/shard_map/ppermute | solution.py:353
  32.9 9.3 %collective-permute-done.2.rows_ref = bf16[80,2048]{1,0:T(8,128)(2,1)S(1)} collective-permute-done((bf16[80,2048]{1,0:T(8,128)(2,1)}, bf16[80,2048]{1,0:T(8,128)(2,1)S(1)}, u32[]{:S(2)}, u32[]{:S(2)}) %collective-permute-start.2) | collective-permute-done | bytes 327712 | tf_op jit(solution)/shard_map/ppermute | solution.py:353
  42.6 1.2 %collective-permute-start.3 = (bf16[80,192]{1,0:T(8,128)(2,1)S(1)}, bf16[80,192]{1,0:T(8,128)(2,1)S(1)}, u32[]{:S(2)}, u32[]{:S(2)}) collective-permute-start(bf16[80,192]{1,0:T(8,128)(2,1)S(1)} %reduce_rows.6), channel_id=1, source_target_pairs={{0,8},{4,12},{8,0},{12,4},{1,9},{5,13},{9,1},{13,5},{2,10},{6,14},... | collective-permute-start | bytes 92168 | tf_op jit(solution)/shard_map/ppermute | solution.py:353
  44.1 9.8 %collective-permute-start.5 = (bf16[80,192]{1,0:T(8,128)(2,1)S(1)}, bf16[80,192]{1,0:T(8,128)(2,1)S(1)}, u32[]{:S(2)}, u32[]{:S(2)}) collective-permute-start(bf16[80,192]{1,0:T(8,128)(2,1)S(1)} %reduce_rows.7), channel_id=1, source_target_pairs={{0,4},{4,8},{8,12},{12,0},{1,5},{5,9},{9,13},{13,1},{2,6},{6,10},{... | collective-permute-start | bytes 92168 | tf_op jit(solution)/shard_map/ppermute | solution.py:353
  54.5 1.1 %collective-permute-done.5.refs_3_ = bf16[80,192]{1,0:T(8,128)(2,1)S(1)} collective-permute-done((bf16[80,192]{1,0:T(8,128)(2,1)S(1)}, bf16[80,192]{1,0:T(8,128)(2,1)S(1)}, u32[]{:S(2)}, u32[]{:S(2)}) %collective-permute-start.5) | collective-permute-done | bytes 30752 | tf_op jit(solution)/shard_map/ppermute | solution.py:353
  55.7 1.1 %combine.1 = f32[128,64]{1,0:T(8,128)S(1)} custom-call(s32[1,128]{1,0:T(1,128)S(1)} %bitcast.12, s32[12]{0:T(128)S(1)} %copy-done.5, bf16[80,192]{1,0:T(8,128)(2,1)S(1)} %reduce_rows.4.refs_0_, bf16[80,192]{1,0:T(8,128)(2,1)S(1)} %collective-permute-done.1.refs_1_, bf16[80,192]{1,0:T(8,128)(2,1)S(1)} %collective-permute-done.3.refs_2_, ...), custom_call_target="tpu_custom_call" | custom-call | tf_op jit(solution)/shard_map/combine/pallas_call | solution.py:279
  56.8 2.4 %collective-permute-start.13 = (bf16[192,512]{1,0:T(8,128)(2,1)S(1)}, bf16[192,512]{1,0:T(8,128)(2,1)S(1)}, u32[]{:S(2)}, u32[]{:S(2)}) collective-permute-start(bf16[192,512]{1,0:T(8,128)(2,1)S(1)} %collective-permute-done.12.refs_1_), channel_id=1, source_target_pairs={{0,4},{4,8},{8,12},{12,0},{1,5},{5,9},{9,13},{13,1},{2,6},{6,10},{... | collective-permute-start | bytes 589832 | tf_op jit(solution)/shard_map/ppermute | solution.py:353
  59.3 1.6 %collective-permute-start.10 = (bf16[128,1024]{1,0:T(8,128)(2,1)S(1)}, bf16[128,1024]{1,0:T(8,128)(2,1)S(1)}, u32[]{:S(2)}, u32[]{:S(2)}) collective-permute-start(bf16[128,1024]{1,0:T(8,128)(2,1)S(1)} %add_convert_fusion), channel_id=1, source_target_pairs={{0,2},{1,3},{2,0},{3,1},{4,6},{5,7},{6,4},{7,5},{8,10},{9,11},{10,... | collective-permute-start | bytes 786440 | tf_op jit(solution)/shard_map/ppermute | solution.py:356
  60.8 1.5 %collective-permute-start.14 = (bf16[192,512]{1,0:T(8,128)(2,1)S(1)}, bf16[192,512]{1,0:T(8,128)(2,1)S(1)}, u32[]{:S(2)}, u32[]{:S(2)}) collective-permute-start(bf16[192,512]{1,0:T(8,128)(2,1)S(1)} %collective-permute-done.11.refs_0_), channel_id=1, source_target_pairs={{0,16},{16,0},{1,17},{17,1},{2,18},{18,2},{3,19},{19,3},{4,20},{20... | collective-permute-start | bytes 589832 | tf_op jit(solution)/shard_map/ppermute | solution.py:353
  63.5 2.4 %collective-permute-done.13.refs_2_ = bf16[192,512]{1,0:T(8,128)(2,1)S(1)} collective-permute-done((bf16[192,512]{1,0:T(8,128)(2,1)S(1)}, bf16[192,512]{1,0:T(8,128)(2,1)S(1)}, u32[]{:S(2)}, u32[]{:S(2)}) %collective-permute-start.13) | collective-permute-done | bytes 196640 | tf_op jit(solution)/shard_map/ppermute | solution.py:353
  65.9 1.5 %collective-permute-start.16 = (bf16[192,512]{1,0:T(8,128)(2,1)S(1)}, bf16[192,512]{1,0:T(8,128)(2,1)S(1)}, u32[]{:S(2)}, u32[]{:S(2)}) collective-permute-start(bf16[192,512]{1,0:T(8,128)(2,1)S(1)} %collective-permute-done.13.refs_2_), channel_id=1, source_target_pairs={{0,16},{16,0},{1,17},{17,1},{2,18},{18,2},{3,19},{19,3},{4,20},{20... | collective-permute-start | bytes 589832 | tf_op jit(solution)/shard_map/ppermute | solution.py:353
  67.5 1.1 %collective-permute-done.14.refs_3_ = bf16[192,512]{1,0:T(8,128)(2,1)S(1)} collective-permute-done((bf16[192,512]{1,0:T(8,128)(2,1)S(1)}, bf16[192,512]{1,0:T(8,128)(2,1)S(1)}, u32[]{:S(2)}, u32[]{:S(2)}) %collective-permute-start.14) | collective-permute-done | bytes 196640 | tf_op jit(solution)/shard_map/ppermute | solution.py:353
  69.1 3.7 %collective-permute-done.15.refs_4_ = bf16[192,512]{1,0:T(8,128)(2,1)S(1)} collective-permute-done((bf16[192,512]{1,0:T(8,128)(2,1)S(1)}, bf16[192,512]{1,0:T(8,128)(2,1)S(1)}, u32[]{:S(2)}, u32[]{:S(2)}) %collective-permute-start.15) | collective-permute-done | bytes 196640 | tf_op jit(solution)/shard_map/ppermute | solution.py:353
  72.8 3.1 %collective-permute-done.16.refs_5_ = bf16[192,512]{1,0:T(8,128)(2,1)S(1)} collective-permute-done((bf16[192,512]{1,0:T(8,128)(2,1)S(1)}, bf16[192,512]{1,0:T(8,128)(2,1)S(1)}, u32[]{:S(2)}, u32[]{:S(2)}) %collective-permute-start.16) | collective-permute-done | bytes 196640 | tf_op jit(solution)/shard_map/ppermute | solution.py:353
  75.9 1.1 %add_delta.1 = bf16[128,1024]{1,0:T(8,128)(2,1)S(1)} custom-call(s32[1,128]{1,0:T(1,128)S(1)} %bitcast.13, s32[12]{0:T(128)S(1)} %copy-done.5, f32[128,64]{1,0:T(8,128)S(1)} %add.24.low_ref, f32[128,64]{1,0:T(8,128)S(1)} %collective-permute-done.7.got_ref, f32[128,1024]{1,0:T(8,128)S(1)} %convert_add_fusion.base_ref, ...), custom_call_target="tpu_custom_call" | custom-call | tf_op jit(solution)/shard_map/add_delta/pallas_call | solution.py:324
  77.6 6.7 %collective-permute-done.17 = bf16[128,1024]{1,0:T(8,128)(2,1)S(1)} collective-permute-done((bf16[128,1024]{1,0:T(8,128)(2,1)S(1)}, bf16[128,1024]{1,0:T(8,128)(2,1)S(1)}, u32[]{:S(2)}, u32[]{:S(2)}) %collective-permute-start.17) | collective-permute-done | bytes 262176 | tf_op jit(solution)/shard_map/ppermute | solution.py:356
  84.5 1.3 %collective-permute-done.19 = bf16[128,1024]{1,0:T(8,128)(2,1)S(1)} collective-permute-done((bf16[128,1024]{1,0:T(8,128)(2,1)S(1)}, bf16[128,1024]{1,0:T(8,128)(2,1)S(1)}, u32[]{:S(2)}, u32[]{:S(2)}) %collective-permute-start.19) | collective-permute-done | bytes 262176 | tf_op jit(solution)/shard_map/ppermute | solution.py:356
  (47 shorter events, 6.1 us)
Async XLA Ops:
  0.9 27.6 %collective-permute-start.11 = (bf16[192,512]{1,0:T(8,128)(2,1)S(1)}, bf16[192,512]{1,0:T(8,128)(2,1)S(1)}, u32[]{:S(2)}, u32[]{:S(2)}) collective-permute-start(bf16[192,512]{1,0:T(8,128)(2,1)S(1)} %constant_dynamic-slice_fusion), channel_id=1, source_target_pairs={{0,4},{4,8},{8,12},{12,0},{1,5},{5,9},{9,13},{13,1},{2,6},{6,10},{... | collective-permute-start | bytes 589832 | tf_op jit(solution)/shard_map/ppermute | solution.py:353
  15.3 13.4 %collective-permute-start = (bf16[80,2048]{1,0:T(8,128)(2,1)}, bf16[80,2048]{1,0:T(8,128)(2,1)S(1)}, u32[]{:S(2)}, u32[]{:S(2)}) collective-permute-start(bf16[80,2048]{1,0:T(8,128)(2,1)} %get-tuple-element.15), channel_id=1, source_target_pairs={{0,4},{4,8},{8,12},{12,0},{1,5},{5,9},{9,13},{13,1},{2,6},{6,10},{... | collective-permute-start | bytes 983048 | tf_op jit(solution)/shard_map/ppermute | solution.py:353
  16.9 25.3 %collective-permute-start.2 = (bf16[80,2048]{1,0:T(8,128)(2,1)}, bf16[80,2048]{1,0:T(8,128)(2,1)S(1)}, u32[]{:S(2)}, u32[]{:S(2)}) collective-permute-start(bf16[80,2048]{1,0:T(8,128)(2,1)} %get-tuple-element.16), channel_id=1, source_target_pairs={{0,8},{4,12},{8,0},{12,4},{1,9},{5,13},{9,1},{13,5},{2,10},{6,14},... | collective-permute-start | bytes 983048 | tf_op jit(solution)/shard_map/ppermute | solution.py:353
  18.0 25.8 %collective-permute-start.4 = (bf16[80,2048]{1,0:T(8,128)(2,1)}, bf16[80,2048]{1,0:T(8,128)(2,1)S(1)}, u32[]{:S(2)}, u32[]{:S(2)}) collective-permute-start(bf16[80,2048]{1,0:T(8,128)(2,1)} %get-tuple-element.17), channel_id=1, source_target_pairs={{0,12},{4,0},{8,4},{12,8},{1,13},{5,1},{9,5},{13,9},{2,14},{6,2},{... | collective-permute-start | bytes 983048 | tf_op jit(solution)/shard_map/ppermute | solution.py:353
  21.9 32.1 %copy-start.3 = (bf16[80,2048]{1,0:T(8,128)(2,1)S(1)}, bf16[80,2048]{1,0:T(8,128)(2,1)}, u32[]{:S(2)}) copy-start(bf16[80,2048]{1,0:T(8,128)(2,1)} %get-tuple-element.14.rows_ref) | copy-start | bytes 983044
  21.9 33.7 %copy-start.4 = (s32[128]{0:T(128)S(1)}, s32[128]{0:T(128)}, u32[]{:S(2)}) copy-start(s32[128]{0:T(128)} %param.20) | copy-start | bytes 1540
  21.9 33.7 %copy-start.5 = (s32[12]{0:T(128)S(1)}, s32[12]{0:T(128)}, u32[]{:S(2)}) copy-start(s32[12]{0:T(128)} %home_ref.3) | copy-start | bytes 148
  28.5 47.4 %copy-start.1 = (bf16[3,64,1024]{2,1,0:T(8,128)(2,1)S(1)}, bf16[3,64,1024]{2,1,0:T(8,128)(2,1)}, u32[]{:S(2)}) copy-start(bf16[3,64,1024]{2,1,0:T(8,128)(2,1)} %param.19) | copy-start | bytes 1179652
  28.5 30.7 %collective-permute-start.9 = (bf16[128,1024]{1,0:T(8,128)(2,1)S(1)}, bf16[128,1024]{1,0:T(8,128)(2,1)S(1)}, u32[]{:S(2)}, u32[]{:S(2)}) collective-permute-start(bf16[128,1024]{1,0:T(8,128)(2,1)S(1)} %get-tuple-element.22), channel_id=1, source_target_pairs={{0,1},{1,0},{2,3},{3,2},{4,5},{5,4},{6,7},{7,6},{8,9},{9,8},{10,11... | collective-permute-start | bytes 786440 | tf_op jit(solution)/shard_map/ppermute | solution.py:356
  28.6 28.2 %collective-permute-start.12 = (bf16[192,512]{1,0:T(8,128)(2,1)S(1)}, bf16[192,512]{1,0:T(8,128)(2,1)S(1)}, u32[]{:S(2)}, u32[]{:S(2)}) collective-permute-start(bf16[192,512]{1,0:T(8,128)(2,1)S(1)} %collective-permute-done.11.refs_0_), channel_id=1, source_target_pairs={{0,4},{4,8},{8,12},{12,0},{1,5},{5,9},{9,13},{13,1},{2,6},{6,10},{... | collective-permute-start | bytes 589832 | tf_op jit(solution)/shard_map/ppermute | solution.py:353
  29.1 24.9 %collective-permute-start.1 = (bf16[80,192]{1,0:T(8,128)(2,1)S(1)}, bf16[80,192]{1,0:T(8,128)(2,1)S(1)}, u32[]{:S(2)}, u32[]{:S(2)}) collective-permute-start(bf16[80,192]{1,0:T(8,128)(2,1)S(1)} %reduce_rows.5), channel_id=1, source_target_pairs={{0,12},{4,0},{8,4},{12,8},{1,13},{5,1},{9,5},{13,9},{2,14},{6,2},{... | collective-permute-start | bytes 92168 | tf_op jit(solution)/shard_map/ppermute | solution.py:353
  42.6 11.9 %collective-permute-start.3 = (bf16[80,192]{1,0:T(8,128)(2,1)S(1)}, bf16[80,192]{1,0:T(8,128)(2,1)S(1)}, u32[]{:S(2)}, u32[]{:S(2)}) collective-permute-start(bf16[80,192]{1,0:T(8,128)(2,1)S(1)} %reduce_rows.6), channel_id=1, source_target_pairs={{0,8},{4,12},{8,0},{12,4},{1,9},{5,13},{9,1},{13,5},{2,10},{6,14},... | collective-permute-start | bytes 92168 | tf_op jit(solution)/shard_map/ppermute | solution.py:353
  44.1 11.5 %collective-permute-start.5 = (bf16[80,192]{1,0:T(8,128)(2,1)S(1)}, bf16[80,192]{1,0:T(8,128)(2,1)S(1)}, u32[]{:S(2)}, u32[]{:S(2)}) collective-permute-start(bf16[80,192]{1,0:T(8,128)(2,1)S(1)} %reduce_rows.7), channel_id=1, source_target_pairs={{0,4},{4,8},{8,12},{12,0},{1,5},{5,9},{9,13},{13,1},{2,6},{6,10},{... | collective-permute-start | bytes 92168 | tf_op jit(solution)/shard_map/ppermute | solution.py:353
  54.0 9.0 %collective-permute-start.8 = (bf16[128,1024]{1,0:T(8,128)(2,1)S(1)}, bf16[128,1024]{1,0:T(8,128)(2,1)S(1)}, u32[]{:S(2)}, u32[]{:S(2)}) collective-permute-start(bf16[128,1024]{1,0:T(8,128)(2,1)S(1)} %get-tuple-element.20), channel_id=1, source_target_pairs={{0,1},{1,0},{2,3},{3,2},{4,5},{5,4},{6,7},{7,6},{8,9},{9,8},{10,11... | collective-permute-start | bytes 786440 | tf_op jit(solution)/shard_map/ppermute | solution.py:356
  56.7 5.6 %collective-permute-start.6 = (f32[128,64]{1,0:T(8,128)S(1)}, f32[128,64]{1,0:T(8,128)S(1)}, u32[]{:S(2)}, u32[]{:S(2)}) collective-permute-start(f32[128,64]{1,0:T(8,128)S(1)} %combine.1), channel_id=1, source_target_pairs={{0,1},{1,0},{2,3},{3,2},{4,5},{5,4},{6,7},{7,6},{8,9},{9,8},{10,11... | collective-permute-start | bytes 98312 | tf_op jit(solution)/shard_map/ppermute | solution.py:356
  56.8 9.1 %collective-permute-start.13 = (bf16[192,512]{1,0:T(8,128)(2,1)S(1)}, bf16[192,512]{1,0:T(8,128)(2,1)S(1)}, u32[]{:S(2)}, u32[]{:S(2)}) collective-permute-start(bf16[192,512]{1,0:T(8,128)(2,1)S(1)} %collective-permute-done.12.refs_1_), channel_id=1, source_target_pairs={{0,4},{4,8},{8,12},{12,0},{1,5},{5,9},{9,13},{13,1},{2,6},{6,10},{... | collective-permute-start | bytes 589832 | tf_op jit(solution)/shard_map/ppermute | solution.py:353
  59.3 9.8 %collective-permute-start.10 = (bf16[128,1024]{1,0:T(8,128)(2,1)S(1)}, bf16[128,1024]{1,0:T(8,128)(2,1)S(1)}, u32[]{:S(2)}, u32[]{:S(2)}) collective-permute-start(bf16[128,1024]{1,0:T(8,128)(2,1)S(1)} %add_convert_fusion), channel_id=1, source_target_pairs={{0,2},{1,3},{2,0},{3,1},{4,6},{5,7},{6,4},{7,5},{8,10},{9,11},{10,... | collective-permute-start | bytes 786440 | tf_op jit(solution)/shard_map/ppermute | solution.py:356
  60.8 7.8 %collective-permute-start.14 = (bf16[192,512]{1,0:T(8,128)(2,1)S(1)}, bf16[192,512]{1,0:T(8,128)(2,1)S(1)}, u32[]{:S(2)}, u32[]{:S(2)}) collective-permute-start(bf16[192,512]{1,0:T(8,128)(2,1)S(1)} %collective-permute-done.11.refs_0_), channel_id=1, source_target_pairs={{0,16},{16,0},{1,17},{17,1},{2,18},{18,2},{3,19},{19,3},{4,20},{20... | collective-permute-start | bytes 589832 | tf_op jit(solution)/shard_map/ppermute | solution.py:353
  62.4 6.7 %collective-permute-start.7 = (f32[128,64]{1,0:T(8,128)S(1)}, f32[128,64]{1,0:T(8,128)S(1)}, u32[]{:S(2)}, u32[]{:S(2)}) collective-permute-start(f32[128,64]{1,0:T(8,128)S(1)} %add.24.low_ref), channel_id=1, source_target_pairs={{0,2},{1,3},{2,0},{3,1},{4,6},{5,7},{6,4},{7,5},{8,10},{9,11},{10,... | collective-permute-start | bytes 98312 | tf_op jit(solution)/shard_map/ppermute | solution.py:356
  63.0 9.9 %collective-permute-start.15 = (bf16[192,512]{1,0:T(8,128)(2,1)S(1)}, bf16[192,512]{1,0:T(8,128)(2,1)S(1)}, u32[]{:S(2)}, u32[]{:S(2)}) collective-permute-start(bf16[192,512]{1,0:T(8,128)(2,1)S(1)} %collective-permute-done.12.refs_1_), channel_id=1, source_target_pairs={{0,16},{16,0},{1,17},{17,1},{2,18},{18,2},{3,19},{19,3},{4,20},{20... | collective-permute-start | bytes 589832 | tf_op jit(solution)/shard_map/ppermute | solution.py:353
  65.9 10.0 %collective-permute-start.16 = (bf16[192,512]{1,0:T(8,128)(2,1)S(1)}, bf16[192,512]{1,0:T(8,128)(2,1)S(1)}, u32[]{:S(2)}, u32[]{:S(2)}) collective-permute-start(bf16[192,512]{1,0:T(8,128)(2,1)S(1)} %collective-permute-done.13.refs_2_), channel_id=1, source_target_pairs={{0,16},{16,0},{1,17},{17,1},{2,18},{18,2},{3,19},{19,3},{4,20},{20... | collective-permute-start | bytes 589832 | tf_op jit(solution)/shard_map/ppermute | solution.py:353
  77.0 7.3 %collective-permute-start.17 = (bf16[128,1024]{1,0:T(8,128)(2,1)S(1)}, bf16[128,1024]{1,0:T(8,128)(2,1)S(1)}, u32[]{:S(2)}, u32[]{:S(2)}) collective-permute-start(bf16[128,1024]{1,0:T(8,128)(2,1)S(1)} %add_delta.1), channel_id=1, source_target_pairs={{0,2},{1,3},{2,0},{3,1},{4,6},{5,7},{6,4},{7,5},{8,10},{9,11},{10,... | collective-permute-start | bytes 786440 | tf_op jit(solution)/shard_map/ppermute | solution.py:356
  77.6 6.9 %collective-permute-start.18 = (bf16[128,1024]{1,0:T(8,128)(2,1)S(1)}, bf16[128,1024]{1,0:T(8,128)(2,1)S(1)}, u32[]{:S(2)}, u32[]{:S(2)}) collective-permute-start(bf16[128,1024]{1,0:T(8,128)(2,1)S(1)} %add_delta.1), channel_id=1, source_target_pairs={{0,1},{1,0},{2,3},{3,2},{4,5},{5,4},{6,7},{7,6},{8,9},{9,8},{10,11... | collective-permute-start | bytes 786440 | tf_op jit(solution)/shard_map/ppermute | solution.py:356
  84.3 1.5 %collective-permute-start.19 = (bf16[128,1024]{1,0:T(8,128)(2,1)S(1)}, bf16[128,1024]{1,0:T(8,128)(2,1)S(1)}, u32[]{:S(2)}, u32[]{:S(2)}) collective-permute-start(bf16[128,1024]{1,0:T(8,128)(2,1)S(1)} %collective-permute-done.17), channel_id=1, source_target_pairs={{0,1},{1,0},{2,3},{3,2},{4,5},{5,4},{6,7},{7,6},{8,9},{9,8},{10,11... | collective-permute-start | bytes 786440 | tf_op jit(solution)/shard_map/ppermute | solution.py:356
  (3 other events, 9.1 us)

commit v3 on v2

--- a/solution.py
+++ b/solution.py
@@ -10,6 +10,7 @@
 
 HEAD_DIM = 128
 BLOCK = 32
+FLAG = 64
 FREE = pl.CostEstimate(flops=0, bytes_accessed=0, transcendentals=0)
 NT = (((1,), (1,)), ((), ()))
 
@@ -47,14 +48,30 @@
     return jnp.sum(spread, axis=1, keepdims=True).astype(jnp.int32)
 
 
+def gate(mebibytes, values, ties):
+    hbm = pl.BlockSpec(memory_space=pl.ANY)
+    count = len(values)
+    return pl.pallas_call(
+        lambda *refs: None,
+        in_specs=[hbm] * (count + len(ties)),
+        out_specs=[hbm] * count,
+        out_shape=[jax.ShapeDtypeStruct(v.shape, v.dtype) for v in values],
+        input_output_aliases={i: i for i in range(count)},
+        compiler_params=params(mebibytes),
+        cost_estimate=FREE,
+        name="gate",
+    )(*values, *ties)
+
+
 def attend_kernel(
-    var_local, dp_count, slots,
+    var_local, dp_count,
     q_hbm, nk_hbm, nv_hbm, k_hbm, v_hbm, len_hbm, assign_hbm, home_hbm, *rest
 ):
     att_ref = rest[0]
     slot_refs = rest[1 : 1 + dp_count]
+    flag_ref = rest[1 + dp_count]
     (q_buf, nk_buf, nv_buf, k_buf, v_buf, len_ref, assign_ref, home_ref, q_scr, o_scr,
-     small_sem, k_sem, v_sem) = rest[1 + dp_count :]
+     small_sem, k_sem, v_sem) = rest[2 + dp_count :]
     rows, width = q_buf.shape
     cache_len = k_buf.shape[1]
     heads, kv_local = width // HEAD_DIM, nk_buf.shape[1] // HEAD_DIM
@@ -151,10 +168,14 @@
 
     lax.fori_loop(0, blocks, block, 0)
     _, home, rank = index_row(assign_ref[...], home_ref, var_local, dp_count)
-    slot = iota((slots, rows), 0)
+    me = lax.axis_index("dp")
+    over = (rank >= slot_refs[-1].shape[0]) & (home != me)
+    flag = jnp.max(over.astype(jnp.float32), axis=1, keepdims=True)
+    flag_ref[...] = jnp.broadcast_to(flag, flag_ref.shape).astype(jnp.bfloat16)
     attended = att_ref[...]
     for shift in range(dp_count):
-        pick = (slot == rank) & (home == lax.rem(lax.axis_index("dp") + shift, dp_count))
+        slot = iota((slot_refs[shift].shape[0], rows), 0)
+        pick = (slot == rank) & (home == lax.rem(me + shift, dp_count))
         slot_refs[shift][...] = jnp.dot(
             one_hot(pick), attended, preferred_element_type=jnp.float32
         ).astype(jnp.bfloat16)
@@ -162,19 +183,21 @@
 
 def attend(
     queries, new_keys, new_values, key_cache, value_cache, lengths, assign_row, home_index,
-    var_local, dp_count, slots,
+    var_local, slots,
 ):
     rows, width = queries.shape
+    dp_count = len(slots)
     heads = width // HEAD_DIM
     blocks = rows // BLOCK
     vmem = pl.BlockSpec(memory_space=pltpu.VMEM)
     given = (queries, new_keys, new_values, key_cache, value_cache)
     return pl.pallas_call(
-        functools.partial(attend_kernel, var_local, dp_count, slots),
+        functools.partial(attend_kernel, var_local, dp_count),
         in_specs=[pl.BlockSpec(memory_space=pltpu.HBM)] * 8,
-        out_specs=[vmem] * (1 + dp_count),
+        out_specs=[vmem] * (2 + dp_count),
         out_shape=[jax.ShapeDtypeStruct((rows, width), jnp.bfloat16)]
-        + [jax.ShapeDtypeStruct((slots, width), jnp.bfloat16)] * dp_count,
+        + [jax.ShapeDtypeStruct((count, width), jnp.bfloat16) for count in slots]
+        + [jax.ShapeDtypeStruct((16, 128), jnp.bfloat16)],
         scratch_shapes=[pltpu.VMEM(a.shape, a.dtype) for a in given]
         + [
             pltpu.SMEM(lengths.shape, jnp.int32),
@@ -237,31 +260,36 @@
     )(attended, out_weight)
 
 
-def reduce_kernel(rows_ref, down_ref, o_ref):
-    o_ref[...] = lax.dot_general(
+def reduce_kernel(rows_ref, down_ref, flag_ref, there_ref, o_ref):
+    wide = down_ref.shape[0]
+    o_ref[:, :wide] = lax.dot_general(
         rows_ref[...], down_ref[...], NT, preferred_element_type=jnp.float32
     ).astype(o_ref.dtype)
-
-
-def reduce_rows(rows, down):
+    flag = jnp.maximum(flag_ref[...].astype(jnp.float32), there_ref[...].astype(jnp.float32))
+    o_ref[:, wide:] = jnp.broadcast_to(flag[:1, :FLAG], (o_ref.shape[0], FLAG)).astype(o_ref.dtype)
+
+
+def reduce_rows(rows, down, flag, flag_there):
     return pl.pallas_call(
         reduce_kernel,
-        out_shape=jax.ShapeDtypeStruct((rows.shape[0], down.shape[0]), jnp.bfloat16),
+        out_shape=jax.ShapeDtypeStruct((rows.shape[0], down.shape[0] + FLAG), jnp.bfloat16),
         compiler_params=params(8),
         cost_estimate=FREE,
         name="reduce_rows",
-    )(rows, down)
+    )(rows, down, flag, flag_there)
 
 
 def combine_kernel(var_local, dp_count, assign_ref, home_ref, *refs):
-    o_ref = refs[-1]
+    o_ref, over_ref = refs[-2:]
     index = index_row(assign_ref[...], home_ref, var_local, dp_count)
     position, home, rank = [as_column(part) for part in index]
     rows, rank_width = o_ref.shape
-    slots, wide = refs[0].shape
-    slot = iota((rows, slots), 1)
+    wide = refs[0].shape[1]
     total = jnp.zeros((rows, wide), jnp.float32)
+    over = refs[0][:16, wide - FLAG :].astype(jnp.float32)
     for shift in range(dp_count):
+        over = jnp.maximum(over, refs[shift][:16, wide - FLAG :].astype(jnp.float32))
+        slot = iota((rows, refs[shift].shape[0]), 1)
         pick = (slot == rank) & (home == lax.rem(lax.axis_index("dp") + shift, dp_count))
         total = total + jnp.dot(one_hot(pick), refs[shift][...], preferred_element_type=jnp.float32)
     local = position - home * var_local
@@ -272,6 +300,7 @@
     for v in range(1, var_local):
         low = low + total[:, v * rank_width : (v + 1) * rank_width]
     o_ref[...] = low
+    over_ref[...] = over[:8]
 
 
 def combine(assign_row, home_index, parts, rank_width, var_local, dp_count):
@@ -279,19 +308,22 @@
     return pl.pallas_call(
         functools.partial(combine_kernel, var_local, dp_count),
         in_specs=[vmem, pl.BlockSpec(memory_space=pltpu.SMEM)] + [vmem] * len(parts),
-        out_specs=vmem,
-        out_shape=jax.ShapeDtypeStruct((assign_row.shape[1], rank_width), jnp.float32),
+        out_specs=[vmem] * 2,
+        out_shape=[
+            jax.ShapeDtypeStruct((assign_row.shape[1], rank_width), jnp.float32),
+            jax.ShapeDtypeStruct((8, FLAG), jnp.float32),
+        ],
         compiler_params=params(8),
         cost_estimate=FREE,
         name="combine",
     )(assign_row, home_index, *parts)
 
 
-def delta_kernel(var_local, dp_count, assign_ref, home_ref, low_ref, got_ref, base_ref, add_ref, up_ref, *refs):
+def delta_kernel(var_local, dp_count, assign_ref, home_ref, low_ref, base_ref, add_ref, up_ref, *refs):
     o_ref = refs[-1]
     index = index_row(assign_ref[...], home_ref, var_local, dp_count)
     position = as_column(index[0])
-    low = (low_ref[...] + got_ref[...]).astype(jnp.bfloat16)
+    low = low_ref[...].astype(jnp.bfloat16)
     rows, rank_width = low.shape
     half = refs[0].shape[1]
     wide = up_ref.shape[0]
@@ -299,6 +331,14 @@
     low = jnp.dot(low, spread, preferred_element_type=jnp.float32)
     factor = iota((rows, wide), 1) // rank_width
     me = lax.axis_index("dp")
+    last = dp_count - 1
+
+    def factors(side, shift):
+        if not side:
+            return refs[shift - 1][...]
+        if shift in (1, last):
+            return refs[last][:wide] if shift == 1 else refs[last][wide:]
+        return refs[last + shift - 1][...]
 
     def picked(shift):
         target = lax.rem(me + dp_count - shift, dp_count)
@@ -311,25 +351,23 @@
         total = jnp.dot(mine[0], up_ref[:, columns], preferred_element_type=jnp.float32)
         for shift in range(1, dp_count):
             total = total + jnp.dot(
-                mine[shift],
-                refs[side * (dp_count - 1) + shift - 1][...],
-                preferred_element_type=jnp.float32,
+                mine[shift], factors(side, shift), preferred_element_type=jnp.float32
             )
         base = base_ref[:, columns].astype(jnp.float32) + add_ref[:, columns].astype(jnp.float32)
         o_ref[:, columns] = (base + total).astype(jnp.bfloat16)
 
 
-def add_delta(assign_row, home_index, low, got, base, add, up, near, far, var_local, dp_count):
+def add_delta(assign_row, home_index, low, base, add, up, others, var_local, dp_count):
     vmem = pl.BlockSpec(memory_space=pltpu.VMEM)
     return pl.pallas_call(
         functools.partial(delta_kernel, var_local, dp_count),
-        in_specs=[vmem, pl.BlockSpec(memory_space=pltpu.SMEM)] + [vmem] * (5 + len(near) + len(far)),
+        in_specs=[vmem, pl.BlockSpec(memory_space=pltpu.SMEM)] + [vmem] * (4 + len(others)),
         out_specs=vmem,
         out_shape=jax.ShapeDtypeStruct(base.shape, jnp.bfloat16),
         compiler_params=params(16),
         cost_estimate=FREE,
         name="add_delta",
-    )(assign_row, home_index, low, got, base, add, up, *near, *far)
+    )(assign_row, home_index, low, base, add, up, *others)
 
 
 def per_device(
@@ -341,12 +379,14 @@
     group_count = lax.axis_size("groups")
     t = lax.axis_index("tensor").astype(jnp.int32)
     y = lax.axis_index("groups").astype(jnp.int32)
+    z = lax.axis_index("dp").astype(jnp.int32)
     rows = queries.shape[0]
     var_local, _, rank_width = down_factors.shape
     variants = var_local * dp_count
     out_local = up_factors.shape[2]
     capacity = max(2, 5 * rows // (2 * variants))
-    slots = min(rows, -(-var_local * capacity // 16) * 16)
+    most = min(rows, -(-var_local * capacity // 16) * 16)
+    usual = min(most, -(-7 * rows // (4 * dp_count) // 8) * 8)
     bits = tensor_count.bit_length() - 1
 
     def along(values, axis, count, shift):
@@ -360,28 +400,37 @@
     half = out_local // 2
     up = up_factors.reshape(var_local * rank_width, out_local)
     piece = lax.dynamic_slice_in_dim(up, y * half, half, axis=1)
-    near, far = [], []
-    for _ in range(1, dp_count):
-        piece = along(piece, "dp", dp_count, 1)
-        near.append(piece)
-        far.append(along(piece, "groups", group_count, 1))
+    near = {1: along(piece, "dp", dp_count, 1), dp_count - 1: along(piece, "dp", dp_count, -1)}
 
     assign_row = assignment[None, :]
-    attended, *outgoing = attend(
+    attended, *outgoing, flag = attend(
         queries, new_keys, new_values, key_cache, value_cache, lengths, assign_row, home_index,
-        var_local, dp_count, slots,
+        var_local, [most] + [usual] * (dp_count - 1),
     )
+    last = dp_count - 1
+    *outgoing[1:], flag = gate(61, outgoing[1:] + [flag], list(near.values()))
+    flag_there = along(flag, "groups", group_count, 1)
     arrived = [outgoing[0]] + [
         along(outgoing[shift], "dp", dp_count, shift) for shift in range(1, dp_count)
     ]
+    attended, near[1], near[last] = gate(
+        1, [attended, near[1], near[last]], [flag_there]
+    )
+    far = {0: along(jnp.concatenate([near[1], near[last]]), "groups", group_count, 1)}
+    for shift in range(2, last):
+        near[shift] = along(near[shift - 1], "dp", dp_count, 1)
+        far[shift] = along(near[shift], "groups", group_count, 1)
 
     held = dict(enumerate(project(attended, out_weight, tensor_count, out_local)))
+    flags = [flag] * dp_count
+    (flags[1],) = gate(1, [flag], [held[0]])
     for bit in range(bits):
         kept = {}
         for w in list(held):
             if w & (1 << bit):
                 continue
-            got = across(held[w | (1 << bit)], bit)
+            sent = held[w | (1 << bit)]
+            got = across(sent, bit)
             if bit == bits - 1:
                 add = got
                 kept[w] = held[w]
@@ -394,14 +443,48 @@
     down = jnp.swapaxes(down_factors, 1, 2).reshape(var_local * rank_width, -1)
     returned = []
     for shift in range(dp_count):
-        part = reduce_rows(arrived[shift], down)
-        returned.append(part if shift == 0 else along(part, "dp", dp_count, dp_count - shift))
-    low = combine(assign_row, home_index, returned, rank_width, var_local, dp_count)
-    for bit in range(bits - 1):
-        low = low + across(low, bit)
-    low_got = across(low, bits - 1)
+        part = reduce_rows(arrived[shift], down, flags[shift], flag_there)
+        returned.append(part if shift == 0 else along(part, "dp", dp_count, -shift))
+
+    returned[:1] = gate(1, returned[:1], [far[0], sent] + [near[shift] for shift in range(2, last)])
+
+    def over_tensor(values):
+        for bit in range(bits):
+            values = values + across(values, bit)
+        return values
+
+    def with_rest(low):
+        labels = jnp.arange(variants, dtype=jnp.int32)
+        position = jnp.sum(
+            jnp.where(assignment[:, None] == labels, home_index, 0), axis=1
+        )
+        home = position // var_local
+        same = home[:, None] == jnp.arange(dp_count, dtype=jnp.int32)
+        counted = jnp.cumsum(same.astype(jnp.int32), axis=0)
+        rank = jnp.sum(jnp.where(same, counted, 0), axis=1) - 1
+        slot = jnp.arange(most - usual, dtype=jnp.int32)[:, None] + usual
+        rest = jnp.zeros((rows, var_local * rank_width), jnp.float32)
+        for shift in range(1, dp_count):
+            pick = (slot == rank) & (home == (z + shift) % dp_count)
+            pick = pick.astype(jnp.bfloat16)
+            sent = jnp.dot(pick, attended, preferred_element_type=jnp.float32)
+            got = along(sent.astype(jnp.bfloat16), "dp", dp_count, shift)
+            part = jnp.dot(got, down.T, preferred_element_type=jnp.float32).astype(jnp.bfloat16)
+            part = along(part, "dp", dp_count, -shift)
+            rest = rest + jnp.dot(pick.T, part, preferred_element_type=jnp.float32)
+        rest = rest.reshape(rows, var_local, rank_width)
+        local = (position - home * var_local)[:, None] == jnp.arange(var_local, dtype=jnp.int32)
+        return low + over_tensor(jnp.sum(jnp.where(local[:, :, None], rest, 0.0), axis=1))
+
+    low, over = combine(assign_row, home_index, returned, rank_width, var_local, dp_count)
+    low = over_tensor(low)
+    if usual < most:
+        low = lax.cond(over[0, 0] > 0.5, with_rest, lambda low: low, low)
+    middle = range(2, last)
     mixed = add_delta(
-        assign_row, home_index, low, low_got, held[0], add, up, near, far, var_local, dp_count
+        assign_row, home_index, low, held[0], add, up,
+        [near[1]] + [near[shift] for shift in middle] + [near[last], far[0]]
+        + [far[shift] for shift in middle], var_local, dp_count,
     )
 
     pieces = {0: mixed}

time: 86.7 us -> 73.4 us (0.85)
  waiting for transfers between devices: 29.5 us -> 14 us
  local copies, waits for them, and re-layouts: 2.9 us -> 6.37 us
  starting transfers between devices: 32.4 us -> 29.3 us
  other arithmetic: 0.13 us -> 1.12 us
    ppermute x12, waiting for transfers between devices: 21 us -> 2.07 us  [along(): lax.ppermute(values, axis, [(i, (i + shift) % count) for i in range(count)])]
    ppermute x12, starting transfers between devices: 29.4 us -> 25.4 us  [along(): lax.ppermute(values, axis, [(i, (i + shift) % count) for i in range(count)])]
    ppermute x8, waiting for transfers between devices: 8.49 us -> 11.9 us  [across(): lax.ppermute(values, 'tensor', [(i, i ^ 1 << bit) for i in range(tensor_c...]
    unnamed x14 -> x30, local copies, waits for them, and re-layouts: 1.07 us -> 4.02 us
    ppermute x8, starting transfers between devices: 2.91 us -> 3.96 us  [across(): lax.ppermute(values, 'tensor', [(i, i ^ 1 << bit) for i in range(tensor_c...]
    add x1, other arithmetic: 0.06 us -> 1.01 us  [per_device(): kept[w] = held[w].astype(jnp.float32) + got.astype(jnp.float32)]
    pallas_call x1 -> x5, Pallas kernels: 11.3 us -> 11.2 us  [the longest x1 11.2 us: attend(): pl.pallas_call(functools.partial(attend_kernel, var_local, dp_count), in_...]
  transfers between devices with their start and end apart: 20 -> 20, of which waited for: 10 -> 6; matrix products, arithmetic and copies ran while one was open for 0% -> 2% of each run, Pallas kernels for 24% -> 28%
where the time goes in v3:
time: 73.4 us; the launch traced here: 73.2 us
  starting transfers between devices  29.3 us (40%)
  Pallas kernels  21.4 us (29%)
  waiting for transfers between devices  14 us (19%)
  local copies, waits for them, and re-layouts  6.37 us (9%)
  other arithmetic  1.12 us (2%)
  between operations  0.97 us (1%)
    ppermute x12, starting transfers between devices, along(): lax.ppermute(values, axis, [(i, (i + shift) % count) for i in range(count)])  25.4 us
    ppermute x8, waiting for transfers between devices, across(): lax.ppermute(values, 'tensor', [(i, i ^ 1 << bit) for i in range(tensor_c...  11.9 us
    pallas_call x1, Pallas kernels, attend(): pl.pallas_call(functools.partial(attend_kernel, var_local, dp_count), in_...  11.2 us
    pallas_call x1, Pallas kernels, project(): pl.pallas_call(functools.partial(project_kernel, count), in_specs=[vmem,...  6.6 us
    unnamed x30, local copies, waits for them, and re-layouts  4.02 us
    ppermute x8, starting transfers between devices, across(): lax.ppermute(values, 'tensor', [(i, i ^ 1 << bit) for i in range(tensor_c...  3.96 us
    ppermute x12, waiting for transfers between devices, along(): lax.ppermute(values, axis, [(i, (i + shift) % count) for i in range(count)])  2.07 us
    pallas_call x4, Pallas kernels, reduce_rows(): pl.pallas_call(reduce_kernel, out_shape=jax.ShapeDtypeStruct((rows.shape[...  1.5 us
  transfers between devices with their start and end apart: 20, of which 6 were waited for; matrix products, arithmetic and copies ran while one was open for 2% of the time, Pallas kernels for 28%

profile of v3, /device:TPU:0, one launch (start us, length us, event | category | flops | bytes accessed | tf_op | source)
XLA Modules:
  0.0 73.2 jit_solution(8150676272134623030)
XLA Ops:
  0.0 0.9 %constant_dynamic-slice_fusion = bf16[192,512]{1,0:T(8,128)(2,1)S(1)} fusion(bf16[192,1024]{1,0:T(8,128)(2,1)} %bitcast.19, s32[]{:T(128)S(6)} %select_n.64), kind=kLoop, calls=%fused_computation.53 | loop fusion | bytes 393220 | tf_op jit(solution)/shard_map/dynamic_slice | solution.py:402
  0.9 3.1 %collective-permute-start.8 = (bf16[192,512]{1,0:T(8,128)(2,1)S(1)}, bf16[192,512]{1,0:T(8,128)(2,1)S(1)}, u32[]{:S(2)}, u32[]{:S(2)}) collective-permute-start(bf16[192,512]{1,0:T(8,128)(2,1)S(1)} %constant_dynamic-slice_fusion), channel_id=1, source_target_pairs={{0,4},{4,8},{8,12},{12,0},{1,5},{5,9},{9,13},{13,1},{2,6},{6,10},{... | collective-permute-start | bytes 589832 | tf_op jit(solution)/shard_map/ppermute | solution.py:393
  4.0 2.1 %collective-permute-start.9 = (bf16[192,512]{1,0:T(8,128)(2,1)S(1)}, bf16[192,512]{1,0:T(8,128)(2,1)S(1)}, u32[]{:S(2)}, u32[]{:S(2)}) collective-permute-start(bf16[192,512]{1,0:T(8,128)(2,1)S(1)} %constant_dynamic-slice_fusion), channel_id=1, source_target_pairs={{0,12},{4,0},{8,4},{12,8},{1,13},{5,1},{9,5},{13,9},{2,14},{6,2},{... | collective-permute-start | bytes 589832 | tf_op jit(solution)/shard_map/ppermute | solution.py:393
  6.1 11.2 %attend.1 = (bf16[128,2048]{1,0:T(8,128)(2,1)S(1)}, bf16[80,2048]{1,0:T(8,128)(2,1)}, bf16[56,2048]{1,0:T(8,128)(2,1)}, bf16[56,2048]{1,0:T(8,128)(2,1)}, bf16[5...) custom-call(bf16[128,2048]{1,0:T(8,128)(2,1)} %q_hbm.1, bf16[128,256]{1,0:T(8,128)(2,1)} %nk_hbm.1, bf16[128,256]{1,0:T(8,128)(2,1)} %nv_hbm.1, ...), custom_call_target="tpu_custom_call" | custom-call | tf_op jit(solution)/shard_map/attend/pallas_call | solution.py:194
  18.1 1.0 %collective-permute-start.16 = (bf16[56,2048]{1,0:T(8,128)(2,1)}, bf16[56,2048]{1,0:T(8,128)(2,1)S(1)}, u32[]{:S(2)}, u32[]{:S(2)}) collective-permute-start(bf16[56,2048]{1,0:T(8,128)(2,1)} %get-tuple-element.60), channel_id=1, source_target_pairs={{0,8},{4,12},{8,0},{12,4},{1,9},{5,13},{9,1},{13,5},{2,10},{6,14},... | collective-permute-start | bytes 688136 | tf_op jit(solution)/shard_map/ppermute | solution.py:393
  19.0 1.5 %collective-permute-start.10 = (bf16[16,128]{1,0:T(8,128)(2,1)}, bf16[16,128]{1,0:T(8,128)(2,1)S(1)}, u32[]{:S(2)}, u32[]{:S(2)}) collective-permute-start(bf16[16,128]{1,0:T(8,128)(2,1)} %get-tuple-element.51.flag_ref.refs_0_), channel_id=1, source_target_pairs={{0,16},{16,0},{1,17},{17,1},{2,18},{18,2},{3,19},{19,3},{4,20},{20... | collective-permute-start | bytes 12296 | tf_op jit(solution)/shard_map/ppermute | solution.py:393
  20.5 1.4 %collective-permute-start.18 = (bf16[56,2048]{1,0:T(8,128)(2,1)}, bf16[56,2048]{1,0:T(8,128)(2,1)S(1)}, u32[]{:S(2)}, u32[]{:S(2)}) collective-permute-start(bf16[56,2048]{1,0:T(8,128)(2,1)} %get-tuple-element.61), channel_id=1, source_target_pairs={{0,12},{4,0},{8,4},{12,8},{1,13},{5,1},{9,5},{13,9},{2,14},{6,2},{... | collective-permute-start | bytes 688136 | tf_op jit(solution)/shard_map/ppermute | solution.py:393
  22.8 0.9 %copy-done.1 = bf16[192,512]{1,0:T(8,128)(2,1)S(1)} copy-done((bf16[192,512]{1,0:T(8,128)(2,1)S(1)}, bf16[192,512]{1,0:T(8,128)(2,1)}, u32[]{:S(2)}) %copy-start.1) | copy-done | bytes 196632
  26.1 6.6 %project.1 = (bf16[128,1024]{1,0:T(8,128)(2,1)S(1)}, bf16[128,1024]{1,0:T(8,128)(2,1)S(1)}, bf16[128,1024]{1,0:T(8,128)(2,1)S(1)}, bf16[128,1024]{1,0:T(8,128)(2,1)S(1)}) custom-call(bf16[128,2048]{1,0:T(8,128)(2,1)S(1)} %get-tuple-element.55.a_ref, bf16[2048,4096]{1,0:T(8,128)(2,1)} %w_hbm.1), custom_call_target="tpu_custom_call" | custom-call | tf_op jit(solution)/shard_map/project/pallas_call | solution.py:248
  32.8 1.6 %collective-permute-start.13 = (bf16[192,512]{1,0:T(8,128)(2,1)S(1)}, bf16[192,512]{1,0:T(8,128)(2,1)S(1)}, u32[]{:S(2)}, u32[]{:S(2)}) collective-permute-start(bf16[192,512]{1,0:T(8,128)(2,1)S(1)} %copy-done.3), channel_id=1, source_target_pairs={{0,4},{4,8},{8,12},{12,0},{1,5},{5,9},{9,13},{13,1},{2,6},{6,10},{... | collective-permute-start | bytes 589832 | tf_op jit(solution)/shard_map/ppermute | solution.py:393
  34.5 1.6 %collective-permute-start.11 = (bf16[384,512]{1,0:T(8,128)(2,1)S(1)}, bf16[384,512]{1,0:T(8,128)(2,1)S(1)}, u32[]{:S(2)}, u32[]{:S(2)}) collective-permute-start(bf16[384,512]{1,0:T(8,128)(2,1)S(1)} %pad_maximum_fusion), channel_id=1, source_target_pairs={{0,16},{16,0},{1,17},{17,1},{2,18},{18,2},{3,19},{19,3},{4,20},{20... | collective-permute-start | bytes 1179656 | tf_op jit(solution)/shard_map/ppermute | solution.py:393
  37.3 7.1 %collective-permute-start.17 = (bf16[56,256]{1,0:T(8,128)(2,1)S(1)}, bf16[56,256]{1,0:T(8,128)(2,1)S(1)}, u32[]{:S(2)}, u32[]{:S(2)}) collective-permute-start(bf16[56,256]{1,0:T(8,128)(2,1)S(1)} %reduce_rows.6), channel_id=1, source_target_pairs={{0,8},{4,12},{8,0},{12,4},{1,9},{5,13},{9,1},{13,5},{2,10},{6,14},... | collective-permute-start | bytes 86024 | tf_op jit(solution)/shard_map/ppermute | solution.py:393
  44.8 1.0 %collective-permute-start.19 = (bf16[56,256]{1,0:T(8,128)(2,1)S(1)}, bf16[56,256]{1,0:T(8,128)(2,1)S(1)}, u32[]{:S(2)}, u32[]{:S(2)}) collective-permute-start(bf16[56,256]{1,0:T(8,128)(2,1)S(1)} %reduce_rows.7), channel_id=1, source_target_pairs={{0,4},{4,8},{8,12},{12,0},{1,5},{5,9},{9,13},{13,1},{2,6},{6,10},{... | collective-permute-start | bytes 86024 | tf_op jit(solution)/shard_map/ppermute | solution.py:393
  45.8 2.9 %collective-permute-start.15 = (bf16[56,256]{1,0:T(8,128)(2,1)S(1)}, bf16[56,256]{1,0:T(8,128)(2,1)S(1)}, u32[]{:S(2)}, u32[]{:S(2)}) collective-permute-start(bf16[56,256]{1,0:T(8,128)(2,1)S(1)} %reduce_rows.5), channel_id=1, source_target_pairs={{0,12},{4,0},{8,4},{12,8},{1,13},{5,1},{9,5},{13,9},{2,14},{6,2},{... | collective-permute-start | bytes 86024 | tf_op jit(solution)/shard_map/ppermute | solution.py:393
  48.8 1.5 %collective-permute-done.15.refs_1_ = bf16[56,256]{1,0:T(8,128)(2,1)S(1)} collective-permute-done((bf16[56,256]{1,0:T(8,128)(2,1)S(1)}, bf16[56,256]{1,0:T(8,128)(2,1)S(1)}, u32[]{:S(2)}, u32[]{:S(2)}) %collective-permute-start.15) | collective-permute-done | bytes 28704 | tf_op jit(solution)/shard_map/ppermute | solution.py:393
  50.6 1.0 %combine.1 = (f32[128,64]{1,0:T(8,128)S(1)}, f32[8,64]{1,0:T(8,128)S(1)}) custom-call(s32[1,128]{1,0:T(1,128)S(1)} %bitcast.28, s32[12]{0:T(128)S(1)} %copy-done.14, bf16[80,256]{1,0:T(8,128)(2,1)S(1)} %gate.6.refs_0_, bf16[56,256]{1,0:T(8,128)(2,1)S(1)} %collective-permute-done.15.refs_1_, bf16[56,256]{1,0:T(8,128)(2,1)S(1)} %collective-permute-done.17.refs_2_, ...), custom_call_target="tpu_custom_call" | custom-call | tf_op jit(solution)/shard_map/combine/pallas_call | solution.py:308
  51.7 1.6 %collective-permute-start.23 = (bf16[128,1024]{1,0:T(8,128)(2,1)S(1)}, bf16[128,1024]{1,0:T(8,128)(2,1)S(1)}, u32[]{:S(2)}, u32[]{:S(2)}) collective-permute-start(bf16[128,1024]{1,0:T(8,128)(2,1)S(1)} %add_convert_fusion.refs_2_), channel_id=1, source_target_pairs={{0,2},{1,3},{2,0},{3,1},{4,6},{5,7},{6,4},{7,5},{8,10},{9,11},{10,... | collective-permute-start | bytes 786440 | tf_op jit(solution)/shard_map/ppermute | solution.py:396
  53.3 1.5 %collective-permute-start.24 = (bf16[192,512]{1,0:T(8,128)(2,1)S(1)}, bf16[192,512]{1,0:T(8,128)(2,1)S(1)}, u32[]{:S(2)}, u32[]{:S(2)}) collective-permute-start(bf16[192,512]{1,0:T(8,128)(2,1)S(1)} %collective-permute-done.13.refs_3_.refs_1_), channel_id=1, source_target_pairs={{0,16},{16,0},{1,17},{17,1},{2,18},{18,2},{3,19},{19,3},{4,20},{20... | collective-permute-start | bytes 589832 | tf_op jit(solution)/shard_map/ppermute | solution.py:393
  55.4 1.0 %convert_add_fusion.base_ref = f32[128,1024]{1,0:T(8,128)S(1)} fusion(bf16[128,1024]{1,0:T(8,128)(2,1)} %collective-permute-done.22, bf16[128,1024]{1,0:T(8,128)(2,1)S(1)} %get-tuple-element.59.refs_1_), kind=kLoop, calls=%fused_computation.46 | loop fusion | flops 393216 | bytes 1048576 | tf_op jit(solution)/shard_map/add | solution.py:438
  57.6 4.2 %collective-permute-done.21 = f32[128,64]{1,0:T(8,128)S(1)} collective-permute-done((f32[128,64]{1,0:T(8,128)S(1)}, f32[128,64]{1,0:T(8,128)S(1)}, u32[]{:S(2)}, u32[]{:S(2)}) %collective-permute-start.21) | collective-permute-done | bytes 32800 | tf_op jit(solution)/shard_map/ppermute | solution.py:396
  61.9 1.1 %add_delta.1 = bf16[128,1024]{1,0:T(8,128)(2,1)S(1)} custom-call(s32[1,128]{1,0:T(1,128)S(1)} %bitcast.29, s32[12]{0:T(128)S(1)} %copy-done.14, f32[128,64]{1,0:T(8,128)S(1)} %get-tuple-element.77.low_ref, f32[128,1024]{1,0:T(8,128)S(1)} %convert_add_fusion.base_ref, bf16[128,1024]{1,0:T(8,128)(2,1)S(1)} %collective-permute-done.23.add_ref, ...), custom_call_target="tpu_custom_call" | custom-call | tf_op jit(solution)/shard_map/add_delta/pallas_call | solution.py:362
  63.0 1.6 %collective-permute-start.25 = (bf16[128,1024]{1,0:T(8,128)(2,1)S(1)}, bf16[128,1024]{1,0:T(8,128)(2,1)S(1)}, u32[]{:S(2)}, u32[]{:S(2)}) collective-permute-start(bf16[128,1024]{1,0:T(8,128)(2,1)S(1)} %add_delta.1), channel_id=1, source_target_pairs={{0,2},{1,3},{2,0},{3,1},{4,6},{5,7},{6,4},{7,5},{8,10},{9,11},{10,... | collective-permute-start | bytes 786440 | tf_op jit(solution)/shard_map/ppermute | solution.py:396
  64.6 6.4 %collective-permute-done.25 = bf16[128,1024]{1,0:T(8,128)(2,1)S(1)} collective-permute-done((bf16[128,1024]{1,0:T(8,128)(2,1)S(1)}, bf16[128,1024]{1,0:T(8,128)(2,1)S(1)}, u32[]{:S(2)}, u32[]{:S(2)}) %collective-permute-start.25) | collective-permute-done | bytes 262176 | tf_op jit(solution)/shard_map/ppermute | solution.py:396
  71.2 1.3 %collective-permute-done.27 = bf16[128,1024]{1,0:T(8,128)(2,1)S(1)} collective-permute-done((bf16[128,1024]{1,0:T(8,128)(2,1)S(1)}, bf16[128,1024]{1,0:T(8,128)(2,1)S(1)}, u32[]{:S(2)}, u32[]{:S(2)}) %collective-permute-start.27) | collective-permute-done | bytes 262176 | tf_op jit(solution)/shard_map/ppermute | solution.py:396
  (71 shorter events, 8.2 us)
Async XLA Ops:
  0.9 16.3 %collective-permute-start.8 = (bf16[192,512]{1,0:T(8,128)(2,1)S(1)}, bf16[192,512]{1,0:T(8,128)(2,1)S(1)}, u32[]{:S(2)}, u32[]{:S(2)}) collective-permute-start(bf16[192,512]{1,0:T(8,128)(2,1)S(1)} %constant_dynamic-slice_fusion), channel_id=1, source_target_pairs={{0,4},{4,8},{8,12},{12,0},{1,5},{5,9},{9,13},{13,1},{2,6},{6,10},{... | collective-permute-start | bytes 589832 | tf_op jit(solution)/shard_map/ppermute | solution.py:393
  4.0 13.3 %collective-permute-start.9 = (bf16[192,512]{1,0:T(8,128)(2,1)S(1)}, bf16[192,512]{1,0:T(8,128)(2,1)S(1)}, u32[]{:S(2)}, u32[]{:S(2)}) collective-permute-start(bf16[192,512]{1,0:T(8,128)(2,1)S(1)} %constant_dynamic-slice_fusion), channel_id=1, source_target_pairs={{0,12},{4,0},{8,4},{12,8},{1,13},{5,1},{9,5},{13,9},{2,14},{6,2},{... | collective-permute-start | bytes 589832 | tf_op jit(solution)/shard_map/ppermute | solution.py:393
  18.1 16.4 %collective-permute-start.16 = (bf16[56,2048]{1,0:T(8,128)(2,1)}, bf16[56,2048]{1,0:T(8,128)(2,1)S(1)}, u32[]{:S(2)}, u32[]{:S(2)}) collective-permute-start(bf16[56,2048]{1,0:T(8,128)(2,1)} %get-tuple-element.60), channel_id=1, source_target_pairs={{0,8},{4,12},{8,0},{12,4},{1,9},{5,13},{9,1},{13,5},{2,10},{6,14},... | collective-permute-start | bytes 688136 | tf_op jit(solution)/shard_map/ppermute | solution.py:393
  19.0 3.8 %collective-permute-start.10 = (bf16[16,128]{1,0:T(8,128)(2,1)}, bf16[16,128]{1,0:T(8,128)(2,1)S(1)}, u32[]{:S(2)}, u32[]{:S(2)}) collective-permute-start(bf16[16,128]{1,0:T(8,128)(2,1)} %get-tuple-element.51.flag_ref.refs_0_), channel_id=1, source_target_pairs={{0,16},{16,0},{1,17},{17,1},{2,18},{18,2},{3,19},{19,3},{4,20},{20... | collective-permute-start | bytes 12296 | tf_op jit(solution)/shard_map/ppermute | solution.py:393
  20.5 16.3 %collective-permute-start.18 = (bf16[56,2048]{1,0:T(8,128)(2,1)}, bf16[56,2048]{1,0:T(8,128)(2,1)S(1)}, u32[]{:S(2)}, u32[]{:S(2)}) collective-permute-start(bf16[56,2048]{1,0:T(8,128)(2,1)} %get-tuple-element.61), channel_id=1, source_target_pairs={{0,12},{4,0},{8,4},{12,8},{1,13},{5,1},{9,5},{13,9},{2,14},{6,2},{... | collective-permute-start | bytes 688136 | tf_op jit(solution)/shard_map/ppermute | solution.py:393
  21.9 15.4 %collective-permute-start.14 = (bf16[56,2048]{1,0:T(8,128)(2,1)}, bf16[56,2048]{1,0:T(8,128)(2,1)S(1)}, u32[]{:S(2)}, u32[]{:S(2)}) collective-permute-start(bf16[56,2048]{1,0:T(8,128)(2,1)} %get-tuple-element.58), channel_id=1, source_target_pairs={{0,4},{4,8},{8,12},{12,0},{1,5},{5,9},{9,13},{13,1},{2,6},{6,10},{... | collective-permute-start | bytes 688136 | tf_op jit(solution)/shard_map/ppermute | solution.py:393
  26.1 10.0 %copy-start.10 = (bf16[16,128]{1,0:T(8,128)(2,1)S(1)}, bf16[16,128]{1,0:T(8,128)(2,1)}, u32[]{:S(2)}) copy-start(bf16[16,128]{1,0:T(8,128)(2,1)} %get-tuple-element.51.flag_ref.refs_0_) | copy-start | bytes 12292
  32.7 17.9 %copy-start.13 = (s32[128]{0:T(128)S(1)}, s32[128]{0:T(128)}, u32[]{:S(2)}) copy-start(s32[128]{0:T(128)} %param.22) | copy-start | bytes 1540
  32.7 17.9 %copy-start.14 = (s32[12]{0:T(128)S(1)}, s32[12]{0:T(128)}, u32[]{:S(2)}) copy-start(s32[12]{0:T(128)} %home_ref.3) | copy-start | bytes 148
  32.7 13.1 %collective-permute-start.12 = (bf16[128,1024]{1,0:T(8,128)(2,1)S(1)}, bf16[128,1024]{1,0:T(8,128)(2,1)S(1)}, u32[]{:S(2)}, u32[]{:S(2)}) collective-permute-start(bf16[128,1024]{1,0:T(8,128)(2,1)S(1)} %get-tuple-element.57), channel_id=1, source_target_pairs={{0,1},{1,0},{2,3},{3,2},{4,5},{5,4},{6,7},{7,6},{8,9},{9,8},{10,11... | collective-permute-start | bytes 786440 | tf_op jit(solution)/shard_map/ppermute | solution.py:396
  32.8 12.0 %collective-permute-start.13 = (bf16[192,512]{1,0:T(8,128)(2,1)S(1)}, bf16[192,512]{1,0:T(8,128)(2,1)S(1)}, u32[]{:S(2)}, u32[]{:S(2)}) collective-permute-start(bf16[192,512]{1,0:T(8,128)(2,1)S(1)} %copy-done.3), channel_id=1, source_target_pairs={{0,4},{4,8},{8,12},{12,0},{1,5},{5,9},{9,13},{13,1},{2,6},{6,10},{... | collective-permute-start | bytes 589832 | tf_op jit(solution)/shard_map/ppermute | solution.py:393
  34.5 14.3 %collective-permute-start.11 = (bf16[384,512]{1,0:T(8,128)(2,1)S(1)}, bf16[384,512]{1,0:T(8,128)(2,1)S(1)}, u32[]{:S(2)}, u32[]{:S(2)}) collective-permute-start(bf16[384,512]{1,0:T(8,128)(2,1)S(1)} %pad_maximum_fusion), channel_id=1, source_target_pairs={{0,16},{16,0},{1,17},{17,1},{2,18},{18,2},{3,19},{19,3},{4,20},{20... | collective-permute-start | bytes 1179656 | tf_op jit(solution)/shard_map/ppermute | solution.py:393
  36.5 25.4 %copy-start.8 = (bf16[3,64,1024]{2,1,0:T(8,128)(2,1)S(1)}, bf16[3,64,1024]{2,1,0:T(8,128)(2,1)}, u32[]{:S(2)}) copy-start(bf16[3,64,1024]{2,1,0:T(8,128)(2,1)} %param.21) | copy-start | bytes 1179652
  36.9 18.6 %collective-permute-start.22 = (bf16[128,1024]{1,0:T(8,128)(2,1)S(1)}, bf16[128,1024]{1,0:T(8,128)(2,1)}, u32[]{:S(2)}, u32[]{:S(2)}) collective-permute-start(bf16[128,1024]{1,0:T(8,128)(2,1)S(1)} %get-tuple-element.64), channel_id=1, source_target_pairs={{0,1},{1,0},{2,3},{3,2},{4,5},{5,4},{6,7},{7,6},{8,9},{9,8},{10,11... | collective-permute-start | bytes 786440 | tf_op jit(solution)/shard_map/ppermute | solution.py:396
  37.3 12.9 %collective-permute-start.17 = (bf16[56,256]{1,0:T(8,128)(2,1)S(1)}, bf16[56,256]{1,0:T(8,128)(2,1)S(1)}, u32[]{:S(2)}, u32[]{:S(2)}) collective-permute-start(bf16[56,256]{1,0:T(8,128)(2,1)S(1)} %reduce_rows.6), channel_id=1, source_target_pairs={{0,8},{4,12},{8,0},{12,4},{1,9},{5,13},{9,1},{13,5},{2,10},{6,14},... | collective-permute-start | bytes 86024 | tf_op jit(solution)/shard_map/ppermute | solution.py:393
  44.8 5.7 %collective-permute-start.19 = (bf16[56,256]{1,0:T(8,128)(2,1)S(1)}, bf16[56,256]{1,0:T(8,128)(2,1)S(1)}, u32[]{:S(2)}, u32[]{:S(2)}) collective-permute-start(bf16[56,256]{1,0:T(8,128)(2,1)S(1)} %reduce_rows.7), channel_id=1, source_target_pairs={{0,4},{4,8},{8,12},{12,0},{1,5},{5,9},{9,13},{13,1},{2,6},{6,10},{... | collective-permute-start | bytes 86024 | tf_op jit(solution)/shard_map/ppermute | solution.py:393
  45.8 4.5 %collective-permute-start.15 = (bf16[56,256]{1,0:T(8,128)(2,1)S(1)}, bf16[56,256]{1,0:T(8,128)(2,1)S(1)}, u32[]{:S(2)}, u32[]{:S(2)}) collective-permute-start(bf16[56,256]{1,0:T(8,128)(2,1)S(1)} %reduce_rows.5), channel_id=1, source_target_pairs={{0,12},{4,0},{8,4},{12,8},{1,13},{5,1},{9,5},{13,9},{2,14},{6,2},{... | collective-permute-start | bytes 86024 | tf_op jit(solution)/shard_map/ppermute | solution.py:393
  51.6 3.2 %collective-permute-start.20 = (f32[128,64]{1,0:T(8,128)S(1)}, f32[128,64]{1,0:T(8,128)S(1)}, u32[]{:S(2)}, u32[]{:S(2)}) collective-permute-start(f32[128,64]{1,0:T(8,128)S(1)} %get-tuple-element.63), channel_id=1, source_target_pairs={{0,1},{1,0},{2,3},{3,2},{4,5},{5,4},{6,7},{7,6},{8,9},{9,8},{10,11... | collective-permute-start | bytes 98312 | tf_op jit(solution)/shard_map/ppermute | solution.py:396
  51.7 10.2 %collective-permute-start.23 = (bf16[128,1024]{1,0:T(8,128)(2,1)S(1)}, bf16[128,1024]{1,0:T(8,128)(2,1)S(1)}, u32[]{:S(2)}, u32[]{:S(2)}) collective-permute-start(bf16[128,1024]{1,0:T(8,128)(2,1)S(1)} %add_convert_fusion.refs_2_), channel_id=1, source_target_pairs={{0,2},{1,3},{2,0},{3,1},{4,6},{5,7},{6,4},{7,5},{8,10},{9,11},{10,... | collective-permute-start | bytes 786440 | tf_op jit(solution)/shard_map/ppermute | solution.py:396
  53.3 8.6 %collective-permute-start.24 = (bf16[192,512]{1,0:T(8,128)(2,1)S(1)}, bf16[192,512]{1,0:T(8,128)(2,1)S(1)}, u32[]{:S(2)}, u32[]{:S(2)}) collective-permute-start(bf16[192,512]{1,0:T(8,128)(2,1)S(1)} %collective-permute-done.13.refs_3_.refs_1_), channel_id=1, source_target_pairs={{0,16},{16,0},{1,17},{17,1},{2,18},{18,2},{3,19},{19,3},{4,20},{20... | collective-permute-start | bytes 589832 | tf_op jit(solution)/shard_map/ppermute | solution.py:393
  54.8 7.0 %collective-permute-start.21 = (f32[128,64]{1,0:T(8,128)S(1)}, f32[128,64]{1,0:T(8,128)S(1)}, u32[]{:S(2)}, u32[]{:S(2)}) collective-permute-start(f32[128,64]{1,0:T(8,128)S(1)} %add.97), channel_id=1, source_target_pairs={{0,2},{1,3},{2,0},{3,1},{4,6},{5,7},{6,4},{7,5},{8,10},{9,11},{10,... | collective-permute-start | bytes 98312 | tf_op jit(solution)/shard_map/ppermute | solution.py:396
  63.0 7.9 %collective-permute-start.25 = (bf16[128,1024]{1,0:T(8,128)(2,1)S(1)}, bf16[128,1024]{1,0:T(8,128)(2,1)S(1)}, u32[]{:S(2)}, u32[]{:S(2)}) collective-permute-start(bf16[128,1024]{1,0:T(8,128)(2,1)S(1)} %add_delta.1), channel_id=1, source_target_pairs={{0,2},{1,3},{2,0},{3,1},{4,6},{5,7},{6,4},{7,5},{8,10},{9,11},{10,... | collective-permute-start | bytes 786440 | tf_op jit(solution)/shard_map/ppermute | solution.py:396
  64.6 6.5 %collective-permute-start.26 = (bf16[128,1024]{1,0:T(8,128)(2,1)S(1)}, bf16[128,1024]{1,0:T(8,128)(2,1)S(1)}, u32[]{:S(2)}, u32[]{:S(2)}) collective-permute-start(bf16[128,1024]{1,0:T(8,128)(2,1)S(1)} %add_delta.1), channel_id=1, source_target_pairs={{0,1},{1,0},{2,3},{3,2},{4,5},{5,4},{6,7},{7,6},{8,9},{9,8},{10,11... | collective-permute-start | bytes 786440 | tf_op jit(solution)/shard_map/ppermute | solution.py:396
  71.0 1.5 %collective-permute-start.27 = (bf16[128,1024]{1,0:T(8,128)(2,1)S(1)}, bf16[128,1024]{1,0:T(8,128)(2,1)S(1)}, u32[]{:S(2)}, u32[]{:S(2)}) collective-permute-start(bf16[128,1024]{1,0:T(8,128)(2,1)S(1)} %collective-permute-done.25), channel_id=1, source_target_pairs={{0,1},{1,0},{2,3},{3,2},{4,5},{5,4},{6,7},{7,6},{8,9},{9,8},{10,11... | collective-permute-start | bytes 786440 | tf_op jit(solution)/shard_map/ppermute | solution.py:396
  (11 other events, 41.1 us)

commit v4 on v3

--- a/solution.py
+++ b/solution.py
@@ -221,7 +221,7 @@
     out_local = outs[0].shape[1]
     per = out_local // width
     me = lax.axis_index("tensor")
-    order = [w for w in range(count) if w & 1] + [w for w in range(count) if not w & 1]
+    order = list(reversed(range(count)))
 
     def fetch(n):
         column = ((me ^ order[n // per]) * per + n % per) * width
@@ -424,14 +424,14 @@
     held = dict(enumerate(project(attended, out_weight, tensor_count, out_local)))
     flags = [flag] * dp_count
     (flags[1],) = gate(1, [flag], [held[0]])
-    for bit in range(bits):
+    for bit in reversed(range(bits)):
         kept = {}
         for w in list(held):
             if w & (1 << bit):
                 continue
             sent = held[w | (1 << bit)]
             got = across(sent, bit)
-            if bit == bits - 1:
+            if bit == 0:
                 add = got
                 kept[w] = held[w]
             else:

time: 73.4 us -> 71.7 us (0.977)
  starting transfers between devices: 29.3 us -> 28.2 us
    ppermute x12, starting transfers between devices: 25.4 us -> 23.1 us  [along(): lax.ppermute(values, axis, [(i, (i + shift) % count) for i in range(count)])]
    ppermute x8, waiting for transfers between devices: 11.9 us -> 9.78 us  [across(): lax.ppermute(values, 'tensor', [(i, i ^ 1 << bit) for i in range(tensor_c...]
    ppermute x12, waiting for transfers between devices: 2.07 us -> 3.62 us  [along(): lax.ppermute(values, axis, [(i, (i + shift) % count) for i in range(count)])]
    ppermute x8, starting transfers between devices: 3.96 us -> 5.17 us  [across(): lax.ppermute(values, 'tensor', [(i, i ^ 1 << bit) for i in range(tensor_c...]
  transfers between devices with their start and end apart: 20 -> 20, of which waited for: 6 -> 8; matrix products, arithmetic and copies ran while one was open for 2% -> 3% of each run, Pallas kernels for 28% -> 28%
where the time goes in v4:
time: 71.7 us; the launch traced here: 71.5 us
  starting transfers between devices  28.2 us (39%)
  Pallas kernels  21.4 us (30%)
  waiting for transfers between devices  13.4 us (19%)
  local copies, waits for them, and re-layouts  6.37 us (9%)
  other arithmetic  1.12 us (2%)
  between operations  0.92 us (1%)
    ppermute x12, starting transfers between devices, along(): lax.ppermute(values, axis, [(i, (i + shift) % count) for i in range(count)])  23.1 us
    pallas_call x1, Pallas kernels, attend(): pl.pallas_call(functools.partial(attend_kernel, var_local, dp_count), in_...  11.2 us
    ppermute x8, waiting for transfers between devices, across(): lax.ppermute(values, 'tensor', [(i, i ^ 1 << bit) for i in range(tensor_c...  9.78 us
    pallas_call x1, Pallas kernels, project(): pl.pallas_call(functools.partial(project_kernel, count), in_specs=[vmem,...  6.6 us
    ppermute x8, starting transfers between devices, across(): lax.ppermute(values, 'tensor', [(i, i ^ 1 << bit) for i in range(tensor_c...  5.17 us
    unnamed x30, local copies, waits for them, and re-layouts  4.02 us
    ppermute x12, waiting for transfers between devices, along(): lax.ppermute(values, axis, [(i, (i + shift) % count) for i in range(count)])  3.62 us
    pallas_call x4, Pallas kernels, reduce_rows(): pl.pallas_call(reduce_kernel, out_shape=jax.ShapeDtypeStruct((rows.shape[...  1.5 us
  transfers between devices with their start and end apart: 20, of which 8 were waited for; matrix products, arithmetic and copies ran while one was open for 3% of the time, Pallas kernels for 28%

profile of v4, /device:TPU:0, one launch (start us, length us, event | category | flops | bytes accessed | tf_op | source)
XLA Modules:
  0.0 71.5 jit_solution(5805621490603341025)
XLA Ops:
  0.0 0.9 %constant_dynamic-slice_fusion = bf16[192,512]{1,0:T(8,128)(2,1)S(1)} fusion(bf16[192,1024]{1,0:T(8,128)(2,1)} %bitcast.19, s32[]{:T(128)S(6)} %select_n.64), kind=kLoop, calls=%fused_computation.53 | loop fusion | bytes 393220 | tf_op jit(solution)/shard_map/dynamic_slice | solution.py:402
  0.9 3.1 %collective-permute-start.8 = (bf16[192,512]{1,0:T(8,128)(2,1)S(1)}, bf16[192,512]{1,0:T(8,128)(2,1)S(1)}, u32[]{:S(2)}, u32[]{:S(2)}) collective-permute-start(bf16[192,512]{1,0:T(8,128)(2,1)S(1)} %constant_dynamic-slice_fusion), channel_id=1, source_target_pairs={{0,4},{4,8},{8,12},{12,0},{1,5},{5,9},{9,13},{13,1},{2,6},{6,10},{... | collective-permute-start | bytes 589832 | tf_op jit(solution)/shard_map/ppermute | solution.py:393
  4.0 2.1 %collective-permute-start.9 = (bf16[192,512]{1,0:T(8,128)(2,1)S(1)}, bf16[192,512]{1,0:T(8,128)(2,1)S(1)}, u32[]{:S(2)}, u32[]{:S(2)}) collective-permute-start(bf16[192,512]{1,0:T(8,128)(2,1)S(1)} %constant_dynamic-slice_fusion), channel_id=1, source_target_pairs={{0,12},{4,0},{8,4},{12,8},{1,13},{5,1},{9,5},{13,9},{2,14},{6,2},{... | collective-permute-start | bytes 589832 | tf_op jit(solution)/shard_map/ppermute | solution.py:393
  6.1 11.2 %attend.1 = (bf16[128,2048]{1,0:T(8,128)(2,1)S(1)}, bf16[80,2048]{1,0:T(8,128)(2,1)}, bf16[56,2048]{1,0:T(8,128)(2,1)}, bf16[56,2048]{1,0:T(8,128)(2,1)}, bf16[5...) custom-call(bf16[128,2048]{1,0:T(8,128)(2,1)} %q_hbm.1, bf16[128,256]{1,0:T(8,128)(2,1)} %nk_hbm.1, bf16[128,256]{1,0:T(8,128)(2,1)} %nv_hbm.1, ...), custom_call_target="tpu_custom_call" | custom-call | tf_op jit(solution)/shard_map/attend/pallas_call | solution.py:194
  18.1 1.0 %collective-permute-start.16 = (bf16[56,2048]{1,0:T(8,128)(2,1)}, bf16[56,2048]{1,0:T(8,128)(2,1)S(1)}, u32[]{:S(2)}, u32[]{:S(2)}) collective-permute-start(bf16[56,2048]{1,0:T(8,128)(2,1)} %get-tuple-element.60), channel_id=1, source_target_pairs={{0,8},{4,12},{8,0},{12,4},{1,9},{5,13},{9,1},{13,5},{2,10},{6,14},... | collective-permute-start | bytes 688136 | tf_op jit(solution)/shard_map/ppermute | solution.py:393
  19.0 1.5 %collective-permute-start.10 = (bf16[16,128]{1,0:T(8,128)(2,1)}, bf16[16,128]{1,0:T(8,128)(2,1)S(1)}, u32[]{:S(2)}, u32[]{:S(2)}) collective-permute-start(bf16[16,128]{1,0:T(8,128)(2,1)} %get-tuple-element.51.flag_ref.refs_0_), channel_id=1, source_target_pairs={{0,16},{16,0},{1,17},{17,1},{2,18},{18,2},{3,19},{19,3},{4,20},{20... | collective-permute-start | bytes 12296 | tf_op jit(solution)/shard_map/ppermute | solution.py:393
  20.5 1.4 %collective-permute-start.18 = (bf16[56,2048]{1,0:T(8,128)(2,1)}, bf16[56,2048]{1,0:T(8,128)(2,1)S(1)}, u32[]{:S(2)}, u32[]{:S(2)}) collective-permute-start(bf16[56,2048]{1,0:T(8,128)(2,1)} %get-tuple-element.61), channel_id=1, source_target_pairs={{0,12},{4,0},{8,4},{12,8},{1,13},{5,1},{9,5},{13,9},{2,14},{6,2},{... | collective-permute-start | bytes 688136 | tf_op jit(solution)/shard_map/ppermute | solution.py:393
  26.1 6.6 %project.1 = (bf16[128,1024]{1,0:T(8,128)(2,1)S(1)}, bf16[128,1024]{1,0:T(8,128)(2,1)S(1)}, bf16[128,1024]{1,0:T(8,128)(2,1)S(1)}, bf16[128,1024]{1,0:T(8,128)(2,1)S(1)}) custom-call(bf16[128,2048]{1,0:T(8,128)(2,1)S(1)} %get-tuple-element.55.a_ref, bf16[2048,4096]{1,0:T(8,128)(2,1)} %w_hbm.1), custom_call_target="tpu_custom_call" | custom-call | tf_op jit(solution)/shard_map/project/pallas_call | solution.py:248
  32.7 1.6 %collective-permute-start.12 = (bf16[128,1024]{1,0:T(8,128)(2,1)S(1)}, bf16[128,1024]{1,0:T(8,128)(2,1)S(1)}, u32[]{:S(2)}, u32[]{:S(2)}) collective-permute-start(bf16[128,1024]{1,0:T(8,128)(2,1)S(1)} %get-tuple-element.57), channel_id=1, source_target_pairs={{0,2},{1,3},{2,0},{3,1},{4,6},{5,7},{6,4},{7,5},{8,10},{9,11},{10,... | collective-permute-start | bytes 786440 | tf_op jit(solution)/shard_map/ppermute | solution.py:396
  34.3 1.6 %collective-permute-start.13 = (bf16[192,512]{1,0:T(8,128)(2,1)S(1)}, bf16[192,512]{1,0:T(8,128)(2,1)S(1)}, u32[]{:S(2)}, u32[]{:S(2)}) collective-permute-start(bf16[192,512]{1,0:T(8,128)(2,1)S(1)} %copy-done.3), channel_id=1, source_target_pairs={{0,4},{4,8},{8,12},{12,0},{1,5},{5,9},{9,13},{13,1},{2,6},{6,10},{... | collective-permute-start | bytes 589832 | tf_op jit(solution)/shard_map/ppermute | solution.py:393
  35.9 1.6 %collective-permute-start.11 = (bf16[384,512]{1,0:T(8,128)(2,1)S(1)}, bf16[384,512]{1,0:T(8,128)(2,1)S(1)}, u32[]{:S(2)}, u32[]{:S(2)}) collective-permute-start(bf16[384,512]{1,0:T(8,128)(2,1)S(1)} %pad_maximum_fusion), channel_id=1, source_target_pairs={{0,16},{16,0},{1,17},{17,1},{2,18},{18,2},{3,19},{19,3},{4,20},{20... | collective-permute-start | bytes 1179656 | tf_op jit(solution)/shard_map/ppermute | solution.py:393
  38.8 1.8 %collective-permute-start.22 = (bf16[128,1024]{1,0:T(8,128)(2,1)S(1)}, bf16[128,1024]{1,0:T(8,128)(2,1)}, u32[]{:S(2)}, u32[]{:S(2)}) collective-permute-start(bf16[128,1024]{1,0:T(8,128)(2,1)S(1)} %get-tuple-element.64), channel_id=1, source_target_pairs={{0,2},{1,3},{2,0},{3,1},{4,6},{5,7},{6,4},{7,5},{8,10},{9,11},{10,... | collective-permute-start | bytes 786440 | tf_op jit(solution)/shard_map/ppermute | solution.py:396
  41.1 4.9 %collective-permute-start.17 = (bf16[56,256]{1,0:T(8,128)(2,1)S(1)}, bf16[56,256]{1,0:T(8,128)(2,1)S(1)}, u32[]{:S(2)}, u32[]{:S(2)}) collective-permute-start(bf16[56,256]{1,0:T(8,128)(2,1)S(1)} %reduce_rows.6), channel_id=1, source_target_pairs={{0,8},{4,12},{8,0},{12,4},{1,9},{5,13},{9,1},{13,5},{2,10},{6,14},... | collective-permute-start | bytes 86024 | tf_op jit(solution)/shard_map/ppermute | solution.py:393
  46.3 1.0 %collective-permute-start.19 = (bf16[56,256]{1,0:T(8,128)(2,1)S(1)}, bf16[56,256]{1,0:T(8,128)(2,1)S(1)}, u32[]{:S(2)}, u32[]{:S(2)}) collective-permute-start(bf16[56,256]{1,0:T(8,128)(2,1)S(1)} %reduce_rows.7), channel_id=1, source_target_pairs={{0,4},{4,8},{8,12},{12,0},{1,5},{5,9},{9,13},{13,1},{2,6},{6,10},{... | collective-permute-start | bytes 86024 | tf_op jit(solution)/shard_map/ppermute | solution.py:393
  47.3 2.9 %collective-permute-start.15 = (bf16[56,256]{1,0:T(8,128)(2,1)S(1)}, bf16[56,256]{1,0:T(8,128)(2,1)S(1)}, u32[]{:S(2)}, u32[]{:S(2)}) collective-permute-start(bf16[56,256]{1,0:T(8,128)(2,1)S(1)} %reduce_rows.5), channel_id=1, source_target_pairs={{0,12},{4,0},{8,4},{12,8},{1,13},{5,1},{9,5},{13,9},{2,14},{6,2},{... | collective-permute-start | bytes 86024 | tf_op jit(solution)/shard_map/ppermute | solution.py:393
  50.3 1.5 %collective-permute-done.15.refs_1_ = bf16[56,256]{1,0:T(8,128)(2,1)S(1)} collective-permute-done((bf16[56,256]{1,0:T(8,128)(2,1)S(1)}, bf16[56,256]{1,0:T(8,128)(2,1)S(1)}, u32[]{:S(2)}, u32[]{:S(2)}) %collective-permute-start.15) | collective-permute-done | bytes 28704 | tf_op jit(solution)/shard_map/ppermute | solution.py:393
  52.1 1.0 %combine.1 = (f32[128,64]{1,0:T(8,128)S(1)}, f32[8,64]{1,0:T(8,128)S(1)}) custom-call(s32[1,128]{1,0:T(1,128)S(1)} %bitcast.28, s32[12]{0:T(128)S(1)} %copy-done.14, bf16[80,256]{1,0:T(8,128)(2,1)S(1)} %gate.6.refs_0_, bf16[56,256]{1,0:T(8,128)(2,1)S(1)} %collective-permute-done.15.refs_1_, bf16[56,256]{1,0:T(8,128)(2,1)S(1)} %collective-permute-done.17.refs_2_, ...), custom_call_target="tpu_custom_call" | custom-call | tf_op jit(solution)/shard_map/combine/pallas_call | solution.py:308
  53.7 1.5 %collective-permute-start.24 = (bf16[192,512]{1,0:T(8,128)(2,1)S(1)}, bf16[192,512]{1,0:T(8,128)(2,1)S(1)}, u32[]{:S(2)}, u32[]{:S(2)}) collective-permute-start(bf16[192,512]{1,0:T(8,128)(2,1)S(1)} %collective-permute-done.13.refs_3_.refs_1_), channel_id=1, source_target_pairs={{0,16},{16,0},{1,17},{17,1},{2,18},{18,2},{3,19},{19,3},{4,20},{20... | collective-permute-start | bytes 589832 | tf_op jit(solution)/shard_map/ppermute | solution.py:393
  55.8 1.0 %convert_add_fusion.base_ref = f32[128,1024]{1,0:T(8,128)S(1)} fusion(bf16[128,1024]{1,0:T(8,128)(2,1)} %collective-permute-done.22, bf16[128,1024]{1,0:T(8,128)(2,1)S(1)} %get-tuple-element.59.refs_1_), kind=kLoop, calls=%fused_computation.46 | loop fusion | flops 393216 | bytes 1048576 | tf_op jit(solution)/shard_map/add | solution.py:438
  58.0 1.5 %collective-permute-done.21 = f32[128,64]{1,0:T(8,128)S(1)} collective-permute-done((f32[128,64]{1,0:T(8,128)S(1)}, f32[128,64]{1,0:T(8,128)S(1)}, u32[]{:S(2)}, u32[]{:S(2)}) %collective-permute-start.21) | collective-permute-done | bytes 32800 | tf_op jit(solution)/shard_map/ppermute | solution.py:396
  59.6 1.0 %collective-permute-done.24.refs_4_ = bf16[192,512]{1,0:T(8,128)(2,1)S(1)} collective-permute-done((bf16[192,512]{1,0:T(8,128)(2,1)S(1)}, bf16[192,512]{1,0:T(8,128)(2,1)S(1)}, u32[]{:S(2)}, u32[]{:S(2)}) %collective-permute-start.24) | collective-permute-done | bytes 196640 | tf_op jit(solution)/shard_map/ppermute | solution.py:393
  60.6 1.1 %add_delta.1 = bf16[128,1024]{1,0:T(8,128)(2,1)S(1)} custom-call(s32[1,128]{1,0:T(1,128)S(1)} %bitcast.29, s32[12]{0:T(128)S(1)} %copy-done.14, f32[128,64]{1,0:T(8,128)S(1)} %get-tuple-element.77.low_ref, f32[128,1024]{1,0:T(8,128)S(1)} %convert_add_fusion.base_ref, bf16[128,1024]{1,0:T(8,128)(2,1)S(1)} %collective-permute-done.23.add_ref, ...), custom_call_target="tpu_custom_call" | custom-call | tf_op jit(solution)/shard_map/add_delta/pallas_call | solution.py:362
  62.3 6.9 %collective-permute-done.25 = bf16[128,1024]{1,0:T(8,128)(2,1)S(1)} collective-permute-done((bf16[128,1024]{1,0:T(8,128)(2,1)S(1)}, bf16[128,1024]{1,0:T(8,128)(2,1)S(1)}, u32[]{:S(2)}, u32[]{:S(2)}) %collective-permute-start.25) | collective-permute-done | bytes 262176 | tf_op jit(solution)/shard_map/ppermute | solution.py:396
  69.4 1.3 %collective-permute-done.27 = bf16[128,1024]{1,0:T(8,128)(2,1)S(1)} collective-permute-done((bf16[128,1024]{1,0:T(8,128)(2,1)S(1)}, bf16[128,1024]{1,0:T(8,128)(2,1)S(1)}, u32[]{:S(2)}, u32[]{:S(2)}) %collective-permute-start.27) | collective-permute-done | bytes 262176 | tf_op jit(solution)/shard_map/ppermute | solution.py:396
  (71 shorter events, 10.7 us)
Async XLA Ops:
  0.9 16.3 %collective-permute-start.8 = (bf16[192,512]{1,0:T(8,128)(2,1)S(1)}, bf16[192,512]{1,0:T(8,128)(2,1)S(1)}, u32[]{:S(2)}, u32[]{:S(2)}) collective-permute-start(bf16[192,512]{1,0:T(8,128)(2,1)S(1)} %constant_dynamic-slice_fusion), channel_id=1, source_target_pairs={{0,4},{4,8},{8,12},{12,0},{1,5},{5,9},{9,13},{13,1},{2,6},{6,10},{... | collective-permute-start | bytes 589832 | tf_op jit(solution)/shard_map/ppermute | solution.py:393
  4.0 13.3 %collective-permute-start.9 = (bf16[192,512]{1,0:T(8,128)(2,1)S(1)}, bf16[192,512]{1,0:T(8,128)(2,1)S(1)}, u32[]{:S(2)}, u32[]{:S(2)}) collective-permute-start(bf16[192,512]{1,0:T(8,128)(2,1)S(1)} %constant_dynamic-slice_fusion), channel_id=1, source_target_pairs={{0,12},{4,0},{8,4},{12,8},{1,13},{5,1},{9,5},{13,9},{2,14},{6,2},{... | collective-permute-start | bytes 589832 | tf_op jit(solution)/shard_map/ppermute | solution.py:393
  18.1 17.8 %collective-permute-start.16 = (bf16[56,2048]{1,0:T(8,128)(2,1)}, bf16[56,2048]{1,0:T(8,128)(2,1)S(1)}, u32[]{:S(2)}, u32[]{:S(2)}) collective-permute-start(bf16[56,2048]{1,0:T(8,128)(2,1)} %get-tuple-element.60), channel_id=1, source_target_pairs={{0,8},{4,12},{8,0},{12,4},{1,9},{5,13},{9,1},{13,5},{2,10},{6,14},... | collective-permute-start | bytes 688136 | tf_op jit(solution)/shard_map/ppermute | solution.py:393
  19.0 3.8 %collective-permute-start.10 = (bf16[16,128]{1,0:T(8,128)(2,1)}, bf16[16,128]{1,0:T(8,128)(2,1)S(1)}, u32[]{:S(2)}, u32[]{:S(2)}) collective-permute-start(bf16[16,128]{1,0:T(8,128)(2,1)} %get-tuple-element.51.flag_ref.refs_0_), channel_id=1, source_target_pairs={{0,16},{16,0},{1,17},{17,1},{2,18},{18,2},{3,19},{19,3},{4,20},{20... | collective-permute-start | bytes 12296 | tf_op jit(solution)/shard_map/ppermute | solution.py:393
  20.5 18.3 %collective-permute-start.18 = (bf16[56,2048]{1,0:T(8,128)(2,1)}, bf16[56,2048]{1,0:T(8,128)(2,1)S(1)}, u32[]{:S(2)}, u32[]{:S(2)}) collective-permute-start(bf16[56,2048]{1,0:T(8,128)(2,1)} %get-tuple-element.61), channel_id=1, source_target_pairs={{0,12},{4,0},{8,4},{12,8},{1,13},{5,1},{9,5},{13,9},{2,14},{6,2},{... | collective-permute-start | bytes 688136 | tf_op jit(solution)/shard_map/ppermute | solution.py:393
  21.9 19.2 %collective-permute-start.14 = (bf16[56,2048]{1,0:T(8,128)(2,1)}, bf16[56,2048]{1,0:T(8,128)(2,1)S(1)}, u32[]{:S(2)}, u32[]{:S(2)}) collective-permute-start(bf16[56,2048]{1,0:T(8,128)(2,1)} %get-tuple-element.58), channel_id=1, source_target_pairs={{0,4},{4,8},{8,12},{12,0},{1,5},{5,9},{9,13},{13,1},{2,6},{6,10},{... | collective-permute-start | bytes 688136 | tf_op jit(solution)/shard_map/ppermute | solution.py:393
  26.1 11.4 %copy-start.10 = (bf16[16,128]{1,0:T(8,128)(2,1)S(1)}, bf16[16,128]{1,0:T(8,128)(2,1)}, u32[]{:S(2)}) copy-start(bf16[16,128]{1,0:T(8,128)(2,1)} %get-tuple-element.51.flag_ref.refs_0_) | copy-start | bytes 12292
  32.7 19.4 %copy-start.13 = (s32[128]{0:T(128)S(1)}, s32[128]{0:T(128)}, u32[]{:S(2)}) copy-start(s32[128]{0:T(128)} %param.22) | copy-start | bytes 1540
  32.7 19.4 %copy-start.14 = (s32[12]{0:T(128)S(1)}, s32[12]{0:T(128)}, u32[]{:S(2)}) copy-start(s32[12]{0:T(128)} %home_ref.3) | copy-start | bytes 148
  32.7 14.6 %collective-permute-start.12 = (bf16[128,1024]{1,0:T(8,128)(2,1)S(1)}, bf16[128,1024]{1,0:T(8,128)(2,1)S(1)}, u32[]{:S(2)}, u32[]{:S(2)}) collective-permute-start(bf16[128,1024]{1,0:T(8,128)(2,1)S(1)} %get-tuple-element.57), channel_id=1, source_target_pairs={{0,2},{1,3},{2,0},{3,1},{4,6},{5,7},{6,4},{7,5},{8,10},{9,11},{10,... | collective-permute-start | bytes 786440 | tf_op jit(solution)/shard_map/ppermute | solution.py:396
  34.3 12.0 %collective-permute-start.13 = (bf16[192,512]{1,0:T(8,128)(2,1)S(1)}, bf16[192,512]{1,0:T(8,128)(2,1)S(1)}, u32[]{:S(2)}, u32[]{:S(2)}) collective-permute-start(bf16[192,512]{1,0:T(8,128)(2,1)S(1)} %copy-done.3), channel_id=1, source_target_pairs={{0,4},{4,8},{8,12},{12,0},{1,5},{5,9},{9,13},{13,1},{2,6},{6,10},{... | collective-permute-start | bytes 589832 | tf_op jit(solution)/shard_map/ppermute | solution.py:393
  35.9 14.4 %collective-permute-start.11 = (bf16[384,512]{1,0:T(8,128)(2,1)S(1)}, bf16[384,512]{1,0:T(8,128)(2,1)S(1)}, u32[]{:S(2)}, u32[]{:S(2)}) collective-permute-start(bf16[384,512]{1,0:T(8,128)(2,1)S(1)} %pad_maximum_fusion), channel_id=1, source_target_pairs={{0,16},{16,0},{1,17},{17,1},{2,18},{18,2},{3,19},{19,3},{4,20},{20... | collective-permute-start | bytes 1179656 | tf_op jit(solution)/shard_map/ppermute | solution.py:393
  37.9 22.7 %copy-start.8 = (bf16[3,64,1024]{2,1,0:T(8,128)(2,1)S(1)}, bf16[3,64,1024]{2,1,0:T(8,128)(2,1)}, u32[]{:S(2)}) copy-start(bf16[3,64,1024]{2,1,0:T(8,128)(2,1)} %param.21) | copy-start | bytes 1179652
  38.8 17.0 %collective-permute-start.22 = (bf16[128,1024]{1,0:T(8,128)(2,1)S(1)}, bf16[128,1024]{1,0:T(8,128)(2,1)}, u32[]{:S(2)}, u32[]{:S(2)}) collective-permute-start(bf16[128,1024]{1,0:T(8,128)(2,1)S(1)} %get-tuple-element.64), channel_id=1, source_target_pairs={{0,2},{1,3},{2,0},{3,1},{4,6},{5,7},{6,4},{7,5},{8,10},{9,11},{10,... | collective-permute-start | bytes 786440 | tf_op jit(solution)/shard_map/ppermute | solution.py:396
  41.1 10.7 %collective-permute-start.17 = (bf16[56,256]{1,0:T(8,128)(2,1)S(1)}, bf16[56,256]{1,0:T(8,128)(2,1)S(1)}, u32[]{:S(2)}, u32[]{:S(2)}) collective-permute-start(bf16[56,256]{1,0:T(8,128)(2,1)S(1)} %reduce_rows.6), channel_id=1, source_target_pairs={{0,8},{4,12},{8,0},{12,4},{1,9},{5,13},{9,1},{13,5},{2,10},{6,14},... | collective-permute-start | bytes 86024 | tf_op jit(solution)/shard_map/ppermute | solution.py:393
  46.3 5.7 %collective-permute-start.19 = (bf16[56,256]{1,0:T(8,128)(2,1)S(1)}, bf16[56,256]{1,0:T(8,128)(2,1)S(1)}, u32[]{:S(2)}, u32[]{:S(2)}) collective-permute-start(bf16[56,256]{1,0:T(8,128)(2,1)S(1)} %reduce_rows.7), channel_id=1, source_target_pairs={{0,4},{4,8},{8,12},{12,0},{1,5},{5,9},{9,13},{13,1},{2,6},{6,10},{... | collective-permute-start | bytes 86024 | tf_op jit(solution)/shard_map/ppermute | solution.py:393
  47.3 4.5 %collective-permute-start.15 = (bf16[56,256]{1,0:T(8,128)(2,1)S(1)}, bf16[56,256]{1,0:T(8,128)(2,1)S(1)}, u32[]{:S(2)}, u32[]{:S(2)}) collective-permute-start(bf16[56,256]{1,0:T(8,128)(2,1)S(1)} %reduce_rows.5), channel_id=1, source_target_pairs={{0,12},{4,0},{8,4},{12,8},{1,13},{5,1},{9,5},{13,9},{2,14},{6,2},{... | collective-permute-start | bytes 86024 | tf_op jit(solution)/shard_map/ppermute | solution.py:393
  53.1 2.1 %collective-permute-start.20 = (f32[128,64]{1,0:T(8,128)S(1)}, f32[128,64]{1,0:T(8,128)S(1)}, u32[]{:S(2)}, u32[]{:S(2)}) collective-permute-start(f32[128,64]{1,0:T(8,128)S(1)} %get-tuple-element.63), channel_id=1, source_target_pairs={{0,1},{1,0},{2,3},{3,2},{4,5},{5,4},{6,7},{7,6},{8,9},{9,8},{10,11... | collective-permute-start | bytes 98312 | tf_op jit(solution)/shard_map/ppermute | solution.py:396
  53.2 7.4 %collective-permute-start.23 = (bf16[128,1024]{1,0:T(8,128)(2,1)S(1)}, bf16[128,1024]{1,0:T(8,128)(2,1)S(1)}, u32[]{:S(2)}, u32[]{:S(2)}) collective-permute-start(bf16[128,1024]{1,0:T(8,128)(2,1)S(1)} %add_convert_fusion.refs_2_), channel_id=1, source_target_pairs={{0,1},{1,0},{2,3},{3,2},{4,5},{5,4},{6,7},{7,6},{8,9},{9,8},{10,11... | collective-permute-start | bytes 786440 | tf_op jit(solution)/shard_map/ppermute | solution.py:396
  53.7 6.9 %collective-permute-start.24 = (bf16[192,512]{1,0:T(8,128)(2,1)S(1)}, bf16[192,512]{1,0:T(8,128)(2,1)S(1)}, u32[]{:S(2)}, u32[]{:S(2)}) collective-permute-start(bf16[192,512]{1,0:T(8,128)(2,1)S(1)} %collective-permute-done.13.refs_3_.refs_1_), channel_id=1, source_target_pairs={{0,16},{16,0},{1,17},{17,1},{2,18},{18,2},{3,19},{19,3},{4,20},{20... | collective-permute-start | bytes 589832 | tf_op jit(solution)/shard_map/ppermute | solution.py:393
  55.2 4.3 %collective-permute-start.21 = (f32[128,64]{1,0:T(8,128)S(1)}, f32[128,64]{1,0:T(8,128)S(1)}, u32[]{:S(2)}, u32[]{:S(2)}) collective-permute-start(f32[128,64]{1,0:T(8,128)S(1)} %add.97), channel_id=1, source_target_pairs={{0,2},{1,3},{2,0},{3,1},{4,6},{5,7},{6,4},{7,5},{8,10},{9,11},{10,... | collective-permute-start | bytes 98312 | tf_op jit(solution)/shard_map/ppermute | solution.py:396
  61.7 7.5 %collective-permute-start.25 = (bf16[128,1024]{1,0:T(8,128)(2,1)S(1)}, bf16[128,1024]{1,0:T(8,128)(2,1)S(1)}, u32[]{:S(2)}, u32[]{:S(2)}) collective-permute-start(bf16[128,1024]{1,0:T(8,128)(2,1)S(1)} %add_delta.1), channel_id=1, source_target_pairs={{0,2},{1,3},{2,0},{3,1},{4,6},{5,7},{6,4},{7,5},{8,10},{9,11},{10,... | collective-permute-start | bytes 786440 | tf_op jit(solution)/shard_map/ppermute | solution.py:396
  62.3 7.1 %collective-permute-start.26 = (bf16[128,1024]{1,0:T(8,128)(2,1)S(1)}, bf16[128,1024]{1,0:T(8,128)(2,1)S(1)}, u32[]{:S(2)}, u32[]{:S(2)}) collective-permute-start(bf16[128,1024]{1,0:T(8,128)(2,1)S(1)} %add_delta.1), channel_id=1, source_target_pairs={{0,1},{1,0},{2,3},{3,2},{4,5},{5,4},{6,7},{7,6},{8,9},{9,8},{10,11... | collective-permute-start | bytes 786440 | tf_op jit(solution)/shard_map/ppermute | solution.py:396
  69.2 1.5 %collective-permute-start.27 = (bf16[128,1024]{1,0:T(8,128)(2,1)S(1)}, bf16[128,1024]{1,0:T(8,128)(2,1)S(1)}, u32[]{:S(2)}, u32[]{:S(2)}) collective-permute-start(bf16[128,1024]{1,0:T(8,128)(2,1)S(1)} %collective-permute-done.25), channel_id=1, source_target_pairs={{0,1},{1,0},{2,3},{3,2},{4,5},{5,4},{6,7},{7,6},{8,9},{9,8},{10,11... | collective-permute-start | bytes 786440 | tf_op jit(solution)/shard_map/ppermute | solution.py:396
  (11 other events, 46.8 us)

commit v5 on v4

--- a/solution.py
+++ b/solution.py
@@ -279,21 +279,47 @@
     )(rows, down, flag, flag_there)
 
 
-def combine_kernel(var_local, dp_count, assign_ref, home_ref, *refs):
-    o_ref, over_ref = refs[-2:]
+def reduce_own_kernel(
+    var_local, dp_count, rows_ref, down_ref, flag_ref, there_ref, assign_ref, home_ref,
+    o_ref, position_ref, local_ref, *pick_refs
+):
+    reduce_kernel(rows_ref, down_ref, flag_ref, there_ref, o_ref)
     index = index_row(assign_ref[...], home_ref, var_local, dp_count)
     position, home, rank = [as_column(part) for part in index]
+    position_ref[...] = jnp.broadcast_to(position, position_ref.shape)
+    local_ref[...] = jnp.broadcast_to(position - home * var_local, local_ref.shape)
+    for shift, pick_ref in enumerate(pick_refs):
+        target = lax.rem(lax.axis_index("dp") + shift, dp_count)
+        pick_ref[...] = one_hot((iota(pick_ref.shape, 1) == rank) & (home == target))
+
+
+def reduce_own(rows, down, flag, flag_there, assign_row, home_index, var_local, slots):
+    vmem = pl.BlockSpec(memory_space=pltpu.VMEM)
+    requests = assign_row.shape[1]
+    return pl.pallas_call(
+        functools.partial(reduce_own_kernel, var_local, len(slots)),
+        in_specs=[vmem] * 5 + [pl.BlockSpec(memory_space=pltpu.SMEM)],
+        out_specs=[vmem] * (3 + len(slots)),
+        out_shape=[jax.ShapeDtypeStruct((rows.shape[0], down.shape[0] + FLAG), jnp.bfloat16)]
+        + [jax.ShapeDtypeStruct((requests, 128), jnp.int32)] * 2
+        + [jax.ShapeDtypeStruct((requests, count), jnp.bfloat16) for count in slots],
+        compiler_params=params(8),
+        cost_estimate=FREE,
+        name="reduce_own",
+    )(rows, down, flag, flag_there, assign_row, home_index)
+
+
+def combine_kernel(var_local, dp_count, local_ref, *refs):
+    o_ref, over_ref = refs[-2:]
+    pick_refs, part_refs = refs[:dp_count], refs[dp_count:-2]
     rows, rank_width = o_ref.shape
-    wide = refs[0].shape[1]
+    wide = part_refs[0].shape[1]
     total = jnp.zeros((rows, wide), jnp.float32)
-    over = refs[0][:16, wide - FLAG :].astype(jnp.float32)
-    for shift in range(dp_count):
-        over = jnp.maximum(over, refs[shift][:16, wide - FLAG :].astype(jnp.float32))
-        slot = iota((rows, refs[shift].shape[0]), 1)
-        pick = (slot == rank) & (home == lax.rem(lax.axis_index("dp") + shift, dp_count))
-        total = total + jnp.dot(one_hot(pick), refs[shift][...], preferred_element_type=jnp.float32)
-    local = position - home * var_local
-    start = local * rank_width
+    over = part_refs[0][:16, wide - FLAG :].astype(jnp.float32)
+    for pick_ref, part_ref in zip(pick_refs, part_refs):
+        over = jnp.maximum(over, part_ref[:16, wide - FLAG :].astype(jnp.float32))
+        total = total + jnp.dot(pick_ref[...], part_ref[...], preferred_element_type=jnp.float32)
+    start = local_ref[:, :1] * rank_width
     lane = iota((rows, wide), 1)
     total = jnp.where((lane >= start) & (lane < start + rank_width), total, 0.0)
     low = total[:, :rank_width]
@@ -303,26 +329,25 @@
     over_ref[...] = over[:8]
 
 
-def combine(assign_row, home_index, parts, rank_width, var_local, dp_count):
+def combine(local, picks, parts, rank_width, var_local):
     vmem = pl.BlockSpec(memory_space=pltpu.VMEM)
     return pl.pallas_call(
-        functools.partial(combine_kernel, var_local, dp_count),
-        in_specs=[vmem, pl.BlockSpec(memory_space=pltpu.SMEM)] + [vmem] * len(parts),
+        functools.partial(combine_kernel, var_local, len(parts)),
+        in_specs=[vmem] * (1 + 2 * len(parts)),
         out_specs=[vmem] * 2,
         out_shape=[
-            jax.ShapeDtypeStruct((assign_row.shape[1], rank_width), jnp.float32),
+            jax.ShapeDtypeStruct((local.shape[0], rank_width), jnp.float32),
             jax.ShapeDtypeStruct((8, FLAG), jnp.float32),
         ],
         compiler_params=params(8),
         cost_estimate=FREE,
         name="combine",
-    )(assign_row, home_index, *parts)
-
-
-def delta_kernel(var_local, dp_count, assign_ref, home_ref, low_ref, base_ref, add_ref, up_ref, *refs):
+    )(local, *picks, *parts)
+
+
+def delta_kernel(var_local, dp_count, position_ref, low_ref, base_ref, add_ref, up_ref, *refs):
     o_ref = refs[-1]
-    index = index_row(assign_ref[...], home_ref, var_local, dp_count)
-    position = as_column(index[0])
+    position = position_ref[:, :1]
     low = low_ref[...].astype(jnp.bfloat16)
     rows, rank_width = low.shape
     half = refs[0].shape[1]
@@ -357,17 +382,17 @@
         o_ref[:, columns] = (base + total).astype(jnp.bfloat16)
 
 
-def add_delta(assign_row, home_index, low, base, add, up, others, var_local, dp_count):
+def add_delta(position, low, base, add, up, others, var_local, dp_count):
     vmem = pl.BlockSpec(memory_space=pltpu.VMEM)
     return pl.pallas_call(
         functools.partial(delta_kernel, var_local, dp_count),
-        in_specs=[vmem, pl.BlockSpec(memory_space=pltpu.SMEM)] + [vmem] * (4 + len(others)),
+        in_specs=[vmem] * (5 + len(others)),
         out_specs=vmem,
         out_shape=jax.ShapeDtypeStruct(base.shape, jnp.bfloat16),
         compiler_params=params(16),
         cost_estimate=FREE,
         name="add_delta",
-    )(assign_row, home_index, low, base, add, up, *others)
+    )(position, low, base, add, up, *others)
 
 
 def per_device(
@@ -387,6 +412,7 @@
     capacity = max(2, 5 * rows // (2 * variants))
     most = min(rows, -(-var_local * capacity // 16) * 16)
     usual = min(most, -(-7 * rows // (4 * dp_count) // 8) * 8)
+    slots = [most] + [usual] * (dp_count - 1)
     bits = tensor_count.bit_length() - 1
 
     def along(values, axis, count, shift):
@@ -405,7 +431,7 @@
     assign_row = assignment[None, :]
     attended, *outgoing, flag = attend(
         queries, new_keys, new_values, key_cache, value_cache, lengths, assign_row, home_index,
-        var_local, [most] + [usual] * (dp_count - 1),
+        var_local, slots,
     )
     last = dp_count - 1
     *outgoing[1:], flag = gate(61, outgoing[1:] + [flag], list(near.values()))
@@ -441,11 +467,13 @@
         held = kept
 
     down = jnp.swapaxes(down_factors, 1, 2).reshape(var_local * rank_width, -1)
-    returned = []
-    for shift in range(dp_count):
-        part = reduce_rows(arrived[shift], down, flags[shift], flag_there)
-        returned.append(part if shift == 0 else along(part, "dp", dp_count, -shift))
-
+    own, position, local, *picks = reduce_own(
+        arrived[0], down, flags[0], flag_there, assign_row, home_index, var_local, slots
+    )
+    returned = [own] + [
+        along(reduce_rows(arrived[shift], down, flags[shift], flag_there), "dp", dp_count, -shift)
+        for shift in range(1, dp_count)
+    ]
     returned[:1] = gate(1, returned[:1], [far[0], sent] + [near[shift] for shift in range(2, last)])
 
     def over_tensor(values):
@@ -476,13 +504,13 @@
         local = (position - home * var_local)[:, None] == jnp.arange(var_local, dtype=jnp.int32)
         return low + over_tensor(jnp.sum(jnp.where(local[:, :, None], rest, 0.0), axis=1))
 
-    low, over = combine(assign_row, home_index, returned, rank_width, var_local, dp_count)
+    low, over = combine(local, picks, returned, rank_width, var_local)
     low = over_tensor(low)
     if usual < most:
         low = lax.cond(over[0, 0] > 0.5, with_rest, lambda low: low, low)
     middle = range(2, last)
     mixed = add_delta(
-        assign_row, home_index, low, held[0], add, up,
+        position, low, held[0], add, up,
         [near[1]] + [near[shift] for shift in middle] + [near[last], far[0]]
         + [far[shift] for shift in middle], var_local, dp_count,
     )

time: 71.7 us -> 70.4 us (0.982)
    ppermute x12, starting transfers between devices: 23.1 us -> 21.3 us  [along(): lax.ppermute(values, axis, [(i, (i + shift) % count) for i in range(count)])]
    ppermute x8, starting transfers between devices: 5.17 us -> 6.83 us  [across(): lax.ppermute(values, 'tensor', [(i, i ^ 1 << bit) for i in range(tensor_c...]
    pallas_call x4 -> x3, Pallas kernels: 1.5 us -> 1.11 us  [reduce_rows(): pl.pallas_call(reduce_kernel, out_shape=jax.ShapeDtypeStruct((rows.shape[...]
  transfers between devices with their start and end apart: 20 -> 20, of which waited for: 8 -> 7; matrix products, arithmetic and copies ran while one was open for 3% -> 3% of each run, Pallas kernels for 28% -> 29%
where the time goes in v5:
time: 70.4 us; the launch traced here: 70.2 us
  starting transfers between devices  28.2 us (40%)
  Pallas kernels  20.7 us (29%)
  waiting for transfers between devices  12.8 us (18%)
  local copies, waits for them, and re-layouts  6.34 us (9%)
  other arithmetic  1.12 us (2%)
  between operations  0.95 us (1%)
    ppermute x12, starting transfers between devices, along(): lax.ppermute(values, axis, [(i, (i + shift) % count) for i in range(count)])  21.3 us
    pallas_call x1, Pallas kernels, attend(): pl.pallas_call(functools.partial(attend_kernel, var_local, dp_count), in_...  11.2 us
    ppermute x8, waiting for transfers between devices, across(): lax.ppermute(values, 'tensor', [(i, i ^ 1 << bit) for i in range(tensor_c...  9.77 us
    ppermute x8, starting transfers between devices, across(): lax.ppermute(values, 'tensor', [(i, i ^ 1 << bit) for i in range(tensor_c...  6.83 us
    pallas_call x1, Pallas kernels, project(): pl.pallas_call(functools.partial(project_kernel, count), in_specs=[vmem,...  6.59 us
    unnamed x30, local copies, waits for them, and re-layouts  3.99 us
    ppermute x12, waiting for transfers between devices, along(): lax.ppermute(values, axis, [(i, (i + shift) % count) for i in range(count)])  3.05 us
  transfers between devices with their start and end apart: 20, of which 7 were waited for; matrix products, arithmetic and copies ran while one was open for 3% of the time, Pallas kernels for 29%

profile of v5, /device:TPU:0, one launch (start us, length us, event | category | flops | bytes accessed | tf_op | source)
XLA Modules:
  0.0 70.2 jit_solution(15899220777839570371)
XLA Ops:
  0.0 0.9 %constant_dynamic-slice_fusion = bf16[192,512]{1,0:T(8,128)(2,1)S(1)} fusion(bf16[192,1024]{1,0:T(8,128)(2,1)} %bitcast.19, s32[]{:T(128)S(6)} %select_n.64), kind=kLoop, calls=%fused_computation.53 | loop fusion | bytes 393220 | tf_op jit(solution)/shard_map/dynamic_slice | solution.py:428
  0.9 3.1 %collective-permute-start.8 = (bf16[192,512]{1,0:T(8,128)(2,1)S(1)}, bf16[192,512]{1,0:T(8,128)(2,1)S(1)}, u32[]{:S(2)}, u32[]{:S(2)}) collective-permute-start(bf16[192,512]{1,0:T(8,128)(2,1)S(1)} %constant_dynamic-slice_fusion), channel_id=1, source_target_pairs={{0,4},{4,8},{8,12},{12,0},{1,5},{5,9},{9,13},{13,1},{2,6},{6,10},{... | collective-permute-start | bytes 589832 | tf_op jit(solution)/shard_map/ppermute | solution.py:419
  4.0 2.1 %collective-permute-start.9 = (bf16[192,512]{1,0:T(8,128)(2,1)S(1)}, bf16[192,512]{1,0:T(8,128)(2,1)S(1)}, u32[]{:S(2)}, u32[]{:S(2)}) collective-permute-start(bf16[192,512]{1,0:T(8,128)(2,1)S(1)} %constant_dynamic-slice_fusion), channel_id=1, source_target_pairs={{0,12},{4,0},{8,4},{12,8},{1,13},{5,1},{9,5},{13,9},{2,14},{6,2},{... | collective-permute-start | bytes 589832 | tf_op jit(solution)/shard_map/ppermute | solution.py:419
  6.1 11.2 %attend.1 = (bf16[128,2048]{1,0:T(8,128)(2,1)S(1)}, bf16[80,2048]{1,0:T(8,128)(2,1)}, bf16[56,2048]{1,0:T(8,128)(2,1)}, bf16[56,2048]{1,0:T(8,128)(2,1)}, bf16[5...) custom-call(bf16[128,2048]{1,0:T(8,128)(2,1)} %q_hbm.1, bf16[128,256]{1,0:T(8,128)(2,1)} %nk_hbm.1, bf16[128,256]{1,0:T(8,128)(2,1)} %nv_hbm.1, ...), custom_call_target="tpu_custom_call" | custom-call | tf_op jit(solution)/shard_map/attend/pallas_call | solution.py:194
  18.0 1.0 %collective-permute-start.16 = (bf16[56,2048]{1,0:T(8,128)(2,1)}, bf16[56,2048]{1,0:T(8,128)(2,1)S(1)}, u32[]{:S(2)}, u32[]{:S(2)}) collective-permute-start(bf16[56,2048]{1,0:T(8,128)(2,1)} %get-tuple-element.74), channel_id=1, source_target_pairs={{0,8},{4,12},{8,0},{12,4},{1,9},{5,13},{9,1},{13,5},{2,10},{6,14},... | collective-permute-start | bytes 688136 | tf_op jit(solution)/shard_map/ppermute | solution.py:419
  19.0 1.5 %collective-permute-start.10 = (bf16[16,128]{1,0:T(8,128)(2,1)}, bf16[16,128]{1,0:T(8,128)(2,1)S(1)}, u32[]{:S(2)}, u32[]{:S(2)}) collective-permute-start(bf16[16,128]{1,0:T(8,128)(2,1)} %get-tuple-element.58.flag_ref.refs_0_), channel_id=1, source_target_pairs={{0,16},{16,0},{1,17},{17,1},{2,18},{18,2},{3,19},{19,3},{4,20},{20... | collective-permute-start | bytes 12296 | tf_op jit(solution)/shard_map/ppermute | solution.py:419
  20.5 1.4 %collective-permute-start.18 = (bf16[56,2048]{1,0:T(8,128)(2,1)}, bf16[56,2048]{1,0:T(8,128)(2,1)S(1)}, u32[]{:S(2)}, u32[]{:S(2)}) collective-permute-start(bf16[56,2048]{1,0:T(8,128)(2,1)} %get-tuple-element.75), channel_id=1, source_target_pairs={{0,12},{4,0},{8,4},{12,8},{1,13},{5,1},{9,5},{13,9},{2,14},{6,2},{... | collective-permute-start | bytes 688136 | tf_op jit(solution)/shard_map/ppermute | solution.py:419
  22.8 0.9 %copy-done.1 = bf16[192,512]{1,0:T(8,128)(2,1)S(1)} copy-done((bf16[192,512]{1,0:T(8,128)(2,1)S(1)}, bf16[192,512]{1,0:T(8,128)(2,1)}, u32[]{:S(2)}) %copy-start.1) | copy-done | bytes 196632
  26.1 6.6 %project.1 = (bf16[128,1024]{1,0:T(8,128)(2,1)S(1)}, bf16[128,1024]{1,0:T(8,128)(2,1)S(1)}, bf16[128,1024]{1,0:T(8,128)(2,1)S(1)}, bf16[128,1024]{1,0:T(8,128)(2,1)S(1)}) custom-call(bf16[128,2048]{1,0:T(8,128)(2,1)S(1)} %get-tuple-element.69.a_ref, bf16[2048,4096]{1,0:T(8,128)(2,1)} %w_hbm.1), custom_call_target="tpu_custom_call" | custom-call | tf_op jit(solution)/shard_map/project/pallas_call | solution.py:248
  32.7 1.6 %collective-permute-start.12 = (bf16[128,1024]{1,0:T(8,128)(2,1)S(1)}, bf16[128,1024]{1,0:T(8,128)(2,1)S(1)}, u32[]{:S(2)}, u32[]{:S(2)}) collective-permute-start(bf16[128,1024]{1,0:T(8,128)(2,1)S(1)} %get-tuple-element.71), channel_id=1, source_target_pairs={{0,2},{1,3},{2,0},{3,1},{4,6},{5,7},{6,4},{7,5},{8,10},{9,11},{10,... | collective-permute-start | bytes 786440 | tf_op jit(solution)/shard_map/ppermute | solution.py:422
  34.2 1.6 %collective-permute-start.13 = (bf16[192,512]{1,0:T(8,128)(2,1)S(1)}, bf16[192,512]{1,0:T(8,128)(2,1)S(1)}, u32[]{:S(2)}, u32[]{:S(2)}) collective-permute-start(bf16[192,512]{1,0:T(8,128)(2,1)S(1)} %copy-done.3), channel_id=1, source_target_pairs={{0,4},{4,8},{8,12},{12,0},{1,5},{5,9},{9,13},{13,1},{2,6},{6,10},{... | collective-permute-start | bytes 589832 | tf_op jit(solution)/shard_map/ppermute | solution.py:419
  35.9 1.6 %collective-permute-start.11 = (bf16[384,512]{1,0:T(8,128)(2,1)S(1)}, bf16[384,512]{1,0:T(8,128)(2,1)S(1)}, u32[]{:S(2)}, u32[]{:S(2)}) collective-permute-start(bf16[384,512]{1,0:T(8,128)(2,1)S(1)} %pad_maximum_fusion), channel_id=1, source_target_pairs={{0,16},{16,0},{1,17},{17,1},{2,18},{18,2},{3,19},{19,3},{4,20},{20... | collective-permute-start | bytes 1179656 | tf_op jit(solution)/shard_map/ppermute | solution.py:419
  37.5 1.0 %reduce_own.1 = (bf16[80,256]{1,0:T(8,128)(2,1)S(1)}, s32[128,128]{1,0:T(8,128)S(1)}, s32[128,128]{1,0:T(8,128)S(1)}, bf16[128,80]{1,0:T(8,128)(2,1)S(1)}, bf16[...) custom-call(bf16[80,2048]{1,0:T(8,128)(2,1)S(1)} %copy-done.9, ...), custom_call_target="tpu_custom_call" | custom-call | tf_op jit(solution)/shard_map/reduce_own/pallas_call | solution.py:299
  38.9 3.5 %collective-permute-start.22 = (bf16[128,1024]{1,0:T(8,128)(2,1)S(1)}, bf16[128,1024]{1,0:T(8,128)(2,1)}, u32[]{:S(2)}, u32[]{:S(2)}) collective-permute-start(bf16[128,1024]{1,0:T(8,128)(2,1)S(1)} %get-tuple-element.78), channel_id=1, source_target_pairs={{0,2},{1,3},{2,0},{3,1},{4,6},{5,7},{6,4},{7,5},{8,10},{9,11},{10,... | collective-permute-start | bytes 786440 | tf_op jit(solution)/shard_map/ppermute | solution.py:422
  42.8 3.1 %collective-permute-start.17 = (bf16[56,256]{1,0:T(8,128)(2,1)S(1)}, bf16[56,256]{1,0:T(8,128)(2,1)S(1)}, u32[]{:S(2)}, u32[]{:S(2)}) collective-permute-start(bf16[56,256]{1,0:T(8,128)(2,1)S(1)} %reduce_rows.4), channel_id=1, source_target_pairs={{0,8},{4,12},{8,0},{12,4},{1,9},{5,13},{9,1},{13,5},{2,10},{6,14},... | collective-permute-start | bytes 86024 | tf_op jit(solution)/shard_map/ppermute | solution.py:419
  46.3 1.0 %collective-permute-start.19 = (bf16[56,256]{1,0:T(8,128)(2,1)S(1)}, bf16[56,256]{1,0:T(8,128)(2,1)S(1)}, u32[]{:S(2)}, u32[]{:S(2)}) collective-permute-start(bf16[56,256]{1,0:T(8,128)(2,1)S(1)} %reduce_rows.5), channel_id=1, source_target_pairs={{0,4},{4,8},{8,12},{12,0},{1,5},{5,9},{9,13},{13,1},{2,6},{6,10},{... | collective-permute-start | bytes 86024 | tf_op jit(solution)/shard_map/ppermute | solution.py:419
  47.3 2.9 %collective-permute-start.15 = (bf16[56,256]{1,0:T(8,128)(2,1)S(1)}, bf16[56,256]{1,0:T(8,128)(2,1)S(1)}, u32[]{:S(2)}, u32[]{:S(2)}) collective-permute-start(bf16[56,256]{1,0:T(8,128)(2,1)S(1)} %reduce_rows.3), channel_id=1, source_target_pairs={{0,12},{4,0},{8,4},{12,8},{1,13},{5,1},{9,5},{13,9},{2,14},{6,2},{... | collective-permute-start | bytes 86024 | tf_op jit(solution)/shard_map/ppermute | solution.py:419
  50.3 1.5 %collective-permute-done.15.refs_5_ = bf16[56,256]{1,0:T(8,128)(2,1)S(1)} collective-permute-done((bf16[56,256]{1,0:T(8,128)(2,1)S(1)}, bf16[56,256]{1,0:T(8,128)(2,1)S(1)}, u32[]{:S(2)}, u32[]{:S(2)}) %collective-permute-start.15) | collective-permute-done | bytes 28704 | tf_op jit(solution)/shard_map/ppermute | solution.py:419
  52.9 1.5 %collective-permute-start.24 = (bf16[192,512]{1,0:T(8,128)(2,1)S(1)}, bf16[192,512]{1,0:T(8,128)(2,1)S(1)}, u32[]{:S(2)}, u32[]{:S(2)}) collective-permute-start(bf16[192,512]{1,0:T(8,128)(2,1)S(1)} %collective-permute-done.13.refs_3_.refs_1_), channel_id=1, source_target_pairs={{0,16},{16,0},{1,17},{17,1},{2,18},{18,2},{3,19},{19,3},{4,20},{20... | collective-permute-start | bytes 589832 | tf_op jit(solution)/shard_map/ppermute | solution.py:419
  55.1 1.0 %convert_add_fusion.base_ref = f32[128,1024]{1,0:T(8,128)S(1)} fusion(bf16[128,1024]{1,0:T(8,128)(2,1)} %collective-permute-done.22, bf16[128,1024]{1,0:T(8,128)(2,1)S(1)} %get-tuple-element.73.refs_1_), kind=kLoop, calls=%fused_computation.46 | loop fusion | flops 393216 | bytes 1048576 | tf_op jit(solution)/shard_map/add | solution.py:464
  57.2 1.5 %collective-permute-done.21 = f32[128,64]{1,0:T(8,128)S(1)} collective-permute-done((f32[128,64]{1,0:T(8,128)S(1)}, f32[128,64]{1,0:T(8,128)S(1)}, u32[]{:S(2)}, u32[]{:S(2)}) %collective-permute-start.21) | collective-permute-done | bytes 32800 | tf_op jit(solution)/shard_map/ppermute | solution.py:422
  58.8 1.0 %collective-permute-done.24.refs_4_ = bf16[192,512]{1,0:T(8,128)(2,1)S(1)} collective-permute-done((bf16[192,512]{1,0:T(8,128)(2,1)S(1)}, bf16[192,512]{1,0:T(8,128)(2,1)S(1)}, u32[]{:S(2)}, u32[]{:S(2)}) %collective-permute-start.24) | collective-permute-done | bytes 196640 | tf_op jit(solution)/shard_map/ppermute | solution.py:419
  61.0 6.9 %collective-permute-done.25 = bf16[128,1024]{1,0:T(8,128)(2,1)S(1)} collective-permute-done((bf16[128,1024]{1,0:T(8,128)(2,1)S(1)}, bf16[128,1024]{1,0:T(8,128)(2,1)S(1)}, u32[]{:S(2)}, u32[]{:S(2)}) %collective-permute-start.25) | collective-permute-done | bytes 262176 | tf_op jit(solution)/shard_map/ppermute | solution.py:422
  68.1 1.3 %collective-permute-done.27 = bf16[128,1024]{1,0:T(8,128)(2,1)S(1)} collective-permute-done((bf16[128,1024]{1,0:T(8,128)(2,1)S(1)}, bf16[128,1024]{1,0:T(8,128)(2,1)S(1)}, u32[]{:S(2)}, u32[]{:S(2)}) %collective-permute-start.27) | collective-permute-done | bytes 262176 | tf_op jit(solution)/shard_map/ppermute | solution.py:422
  (71 shorter events, 9.6 us)
Async XLA Ops:
  0.9 16.3 %collective-permute-start.8 = (bf16[192,512]{1,0:T(8,128)(2,1)S(1)}, bf16[192,512]{1,0:T(8,128)(2,1)S(1)}, u32[]{:S(2)}, u32[]{:S(2)}) collective-permute-start(bf16[192,512]{1,0:T(8,128)(2,1)S(1)} %constant_dynamic-slice_fusion), channel_id=1, source_target_pairs={{0,4},{4,8},{8,12},{12,0},{1,5},{5,9},{9,13},{13,1},{2,6},{6,10},{... | collective-permute-start | bytes 589832 | tf_op jit(solution)/shard_map/ppermute | solution.py:419
  4.0 13.3 %collective-permute-start.9 = (bf16[192,512]{1,0:T(8,128)(2,1)S(1)}, bf16[192,512]{1,0:T(8,128)(2,1)S(1)}, u32[]{:S(2)}, u32[]{:S(2)}) collective-permute-start(bf16[192,512]{1,0:T(8,128)(2,1)S(1)} %constant_dynamic-slice_fusion), channel_id=1, source_target_pairs={{0,12},{4,0},{8,4},{12,8},{1,13},{5,1},{9,5},{13,9},{2,14},{6,2},{... | collective-permute-start | bytes 589832 | tf_op jit(solution)/shard_map/ppermute | solution.py:419
  18.0 17.8 %collective-permute-start.16 = (bf16[56,2048]{1,0:T(8,128)(2,1)}, bf16[56,2048]{1,0:T(8,128)(2,1)S(1)}, u32[]{:S(2)}, u32[]{:S(2)}) collective-permute-start(bf16[56,2048]{1,0:T(8,128)(2,1)} %get-tuple-element.74), channel_id=1, source_target_pairs={{0,8},{4,12},{8,0},{12,4},{1,9},{5,13},{9,1},{13,5},{2,10},{6,14},... | collective-permute-start | bytes 688136 | tf_op jit(solution)/shard_map/ppermute | solution.py:419
  19.0 3.8 %collective-permute-start.10 = (bf16[16,128]{1,0:T(8,128)(2,1)}, bf16[16,128]{1,0:T(8,128)(2,1)S(1)}, u32[]{:S(2)}, u32[]{:S(2)}) collective-permute-start(bf16[16,128]{1,0:T(8,128)(2,1)} %get-tuple-element.58.flag_ref.refs_0_), channel_id=1, source_target_pairs={{0,16},{16,0},{1,17},{17,1},{2,18},{18,2},{3,19},{19,3},{4,20},{20... | collective-permute-start | bytes 12296 | tf_op jit(solution)/shard_map/ppermute | solution.py:419
  20.5 18.4 %collective-permute-start.18 = (bf16[56,2048]{1,0:T(8,128)(2,1)}, bf16[56,2048]{1,0:T(8,128)(2,1)S(1)}, u32[]{:S(2)}, u32[]{:S(2)}) collective-permute-start(bf16[56,2048]{1,0:T(8,128)(2,1)} %get-tuple-element.75), channel_id=1, source_target_pairs={{0,12},{4,0},{8,4},{12,8},{1,13},{5,1},{9,5},{13,9},{2,14},{6,2},{... | collective-permute-start | bytes 688136 | tf_op jit(solution)/shard_map/ppermute | solution.py:419
  21.9 20.9 %collective-permute-start.14 = (bf16[56,2048]{1,0:T(8,128)(2,1)}, bf16[56,2048]{1,0:T(8,128)(2,1)S(1)}, u32[]{:S(2)}, u32[]{:S(2)}) collective-permute-start(bf16[56,2048]{1,0:T(8,128)(2,1)} %get-tuple-element.72), channel_id=1, source_target_pairs={{0,4},{4,8},{8,12},{12,0},{1,5},{5,9},{9,13},{13,1},{2,6},{6,10},{... | collective-permute-start | bytes 688136 | tf_op jit(solution)/shard_map/ppermute | solution.py:419
  26.0 11.4 %copy-start.9 = (bf16[80,2048]{1,0:T(8,128)(2,1)S(1)}, bf16[80,2048]{1,0:T(8,128)(2,1)}, u32[]{:S(2)}) copy-start(bf16[80,2048]{1,0:T(8,128)(2,1)} %get-tuple-element.53.rows_ref) | copy-start | bytes 983044
  26.0 11.4 %copy-start.10 = (bf16[16,128]{1,0:T(8,128)(2,1)S(1)}, bf16[16,128]{1,0:T(8,128)(2,1)}, u32[]{:S(2)}) copy-start(bf16[16,128]{1,0:T(8,128)(2,1)} %get-tuple-element.58.flag_ref.refs_0_) | copy-start | bytes 12292
  26.0 11.4 %copy-start.11 = (bf16[3,2048,64]{1,2,0:T(8,128)(2,1)S(1)}, bf16[3,2048,64]{1,2,0:T(8,128)(2,1)}, u32[]{:S(2)}) copy-start(bf16[3,2048,64]{1,2,0:T(8,128)(2,1)} %param.20) | copy-start | bytes 2359300
  32.7 14.6 %collective-permute-start.12 = (bf16[128,1024]{1,0:T(8,128)(2,1)S(1)}, bf16[128,1024]{1,0:T(8,128)(2,1)S(1)}, u32[]{:S(2)}, u32[]{:S(2)}) collective-permute-start(bf16[128,1024]{1,0:T(8,128)(2,1)S(1)} %get-tuple-element.71), channel_id=1, source_target_pairs={{0,2},{1,3},{2,0},{3,1},{4,6},{5,7},{6,4},{7,5},{8,10},{9,11},{10,... | collective-permute-start | bytes 786440 | tf_op jit(solution)/shard_map/ppermute | solution.py:422
  34.2 12.1 %collective-permute-start.13 = (bf16[192,512]{1,0:T(8,128)(2,1)S(1)}, bf16[192,512]{1,0:T(8,128)(2,1)S(1)}, u32[]{:S(2)}, u32[]{:S(2)}) collective-permute-start(bf16[192,512]{1,0:T(8,128)(2,1)S(1)} %copy-done.3), channel_id=1, source_target_pairs={{0,4},{4,8},{8,12},{12,0},{1,5},{5,9},{9,13},{13,1},{2,6},{6,10},{... | collective-permute-start | bytes 589832 | tf_op jit(solution)/shard_map/ppermute | solution.py:419
  35.9 14.4 %collective-permute-start.11 = (bf16[384,512]{1,0:T(8,128)(2,1)S(1)}, bf16[384,512]{1,0:T(8,128)(2,1)S(1)}, u32[]{:S(2)}, u32[]{:S(2)}) collective-permute-start(bf16[384,512]{1,0:T(8,128)(2,1)S(1)} %pad_maximum_fusion), channel_id=1, source_target_pairs={{0,16},{16,0},{1,17},{17,1},{2,18},{18,2},{3,19},{19,3},{4,20},{20... | collective-permute-start | bytes 1179656 | tf_op jit(solution)/shard_map/ppermute | solution.py:419
  38.5 21.3 %copy-start.8 = (bf16[3,64,1024]{2,1,0:T(8,128)(2,1)S(1)}, bf16[3,64,1024]{2,1,0:T(8,128)(2,1)}, u32[]{:S(2)}) copy-start(bf16[3,64,1024]{2,1,0:T(8,128)(2,1)} %param.21) | copy-start | bytes 1179652
  38.9 16.1 %collective-permute-start.22 = (bf16[128,1024]{1,0:T(8,128)(2,1)S(1)}, bf16[128,1024]{1,0:T(8,128)(2,1)}, u32[]{:S(2)}, u32[]{:S(2)}) collective-permute-start(bf16[128,1024]{1,0:T(8,128)(2,1)S(1)} %get-tuple-element.78), channel_id=1, source_target_pairs={{0,2},{1,3},{2,0},{3,1},{4,6},{5,7},{6,4},{7,5},{8,10},{9,11},{10,... | collective-permute-start | bytes 786440 | tf_op jit(solution)/shard_map/ppermute | solution.py:422
  42.8 8.9 %collective-permute-start.17 = (bf16[56,256]{1,0:T(8,128)(2,1)S(1)}, bf16[56,256]{1,0:T(8,128)(2,1)S(1)}, u32[]{:S(2)}, u32[]{:S(2)}) collective-permute-start(bf16[56,256]{1,0:T(8,128)(2,1)S(1)} %reduce_rows.4), channel_id=1, source_target_pairs={{0,8},{4,12},{8,0},{12,4},{1,9},{5,13},{9,1},{13,5},{2,10},{6,14},... | collective-permute-start | bytes 86024 | tf_op jit(solution)/shard_map/ppermute | solution.py:419
  46.3 5.7 %collective-permute-start.19 = (bf16[56,256]{1,0:T(8,128)(2,1)S(1)}, bf16[56,256]{1,0:T(8,128)(2,1)S(1)}, u32[]{:S(2)}, u32[]{:S(2)}) collective-permute-start(bf16[56,256]{1,0:T(8,128)(2,1)S(1)} %reduce_rows.5), channel_id=1, source_target_pairs={{0,4},{4,8},{8,12},{12,0},{1,5},{5,9},{9,13},{13,1},{2,6},{6,10},{... | collective-permute-start | bytes 86024 | tf_op jit(solution)/shard_map/ppermute | solution.py:419
  47.3 4.5 %collective-permute-start.15 = (bf16[56,256]{1,0:T(8,128)(2,1)S(1)}, bf16[56,256]{1,0:T(8,128)(2,1)S(1)}, u32[]{:S(2)}, u32[]{:S(2)}) collective-permute-start(bf16[56,256]{1,0:T(8,128)(2,1)S(1)} %reduce_rows.3), channel_id=1, source_target_pairs={{0,12},{4,0},{8,4},{12,8},{1,13},{5,1},{9,5},{13,9},{2,14},{6,2},{... | collective-permute-start | bytes 86024 | tf_op jit(solution)/shard_map/ppermute | solution.py:419
  52.3 2.1 %collective-permute-start.20 = (f32[128,64]{1,0:T(8,128)S(1)}, f32[128,64]{1,0:T(8,128)S(1)}, u32[]{:S(2)}, u32[]{:S(2)}) collective-permute-start(f32[128,64]{1,0:T(8,128)S(1)} %get-tuple-element.77), channel_id=1, source_target_pairs={{0,1},{1,0},{2,3},{3,2},{4,5},{5,4},{6,7},{7,6},{8,9},{9,8},{10,11... | collective-permute-start | bytes 98312 | tf_op jit(solution)/shard_map/ppermute | solution.py:422
  52.4 7.4 %collective-permute-start.23 = (bf16[128,1024]{1,0:T(8,128)(2,1)S(1)}, bf16[128,1024]{1,0:T(8,128)(2,1)S(1)}, u32[]{:S(2)}, u32[]{:S(2)}) collective-permute-start(bf16[128,1024]{1,0:T(8,128)(2,1)S(1)} %add_convert_fusion.refs_2_), channel_id=1, source_target_pairs={{0,1},{1,0},{2,3},{3,2},{4,5},{5,4},{6,7},{7,6},{8,9},{9,8},{10,11... | collective-permute-start | bytes 786440 | tf_op jit(solution)/shard_map/ppermute | solution.py:422
  52.9 6.9 %collective-permute-start.24 = (bf16[192,512]{1,0:T(8,128)(2,1)S(1)}, bf16[192,512]{1,0:T(8,128)(2,1)S(1)}, u32[]{:S(2)}, u32[]{:S(2)}) collective-permute-start(bf16[192,512]{1,0:T(8,128)(2,1)S(1)} %collective-permute-done.13.refs_3_.refs_1_), channel_id=1, source_target_pairs={{0,16},{16,0},{1,17},{17,1},{2,18},{18,2},{3,19},{19,3},{4,20},{20... | collective-permute-start | bytes 589832 | tf_op jit(solution)/shard_map/ppermute | solution.py:419
  54.5 4.3 %collective-permute-start.21 = (f32[128,64]{1,0:T(8,128)S(1)}, f32[128,64]{1,0:T(8,128)S(1)}, u32[]{:S(2)}, u32[]{:S(2)}) collective-permute-start(f32[128,64]{1,0:T(8,128)S(1)} %add.97), channel_id=1, source_target_pairs={{0,2},{1,3},{2,0},{3,1},{4,6},{5,7},{6,4},{7,5},{8,10},{9,11},{10,... | collective-permute-start | bytes 98312 | tf_op jit(solution)/shard_map/ppermute | solution.py:422
  60.4 7.5 %collective-permute-start.25 = (bf16[128,1024]{1,0:T(8,128)(2,1)S(1)}, bf16[128,1024]{1,0:T(8,128)(2,1)S(1)}, u32[]{:S(2)}, u32[]{:S(2)}) collective-permute-start(bf16[128,1024]{1,0:T(8,128)(2,1)S(1)} %add_delta.1), channel_id=1, source_target_pairs={{0,2},{1,3},{2,0},{3,1},{4,6},{5,7},{6,4},{7,5},{8,10},{9,11},{10,... | collective-permute-start | bytes 786440 | tf_op jit(solution)/shard_map/ppermute | solution.py:422
  61.0 7.1 %collective-permute-start.26 = (bf16[128,1024]{1,0:T(8,128)(2,1)S(1)}, bf16[128,1024]{1,0:T(8,128)(2,1)S(1)}, u32[]{:S(2)}, u32[]{:S(2)}) collective-permute-start(bf16[128,1024]{1,0:T(8,128)(2,1)S(1)} %add_delta.1), channel_id=1, source_target_pairs={{0,1},{1,0},{2,3},{3,2},{4,5},{5,4},{6,7},{7,6},{8,9},{9,8},{10,11... | collective-permute-start | bytes 786440 | tf_op jit(solution)/shard_map/ppermute | solution.py:422
  67.9 1.5 %collective-permute-start.27 = (bf16[128,1024]{1,0:T(8,128)(2,1)S(1)}, bf16[128,1024]{1,0:T(8,128)(2,1)S(1)}, u32[]{:S(2)}, u32[]{:S(2)}) collective-permute-start(bf16[128,1024]{1,0:T(8,128)(2,1)S(1)} %collective-permute-done.25), channel_id=1, source_target_pairs={{0,1},{1,0},{2,3},{3,2},{4,5},{5,4},{6,7},{7,6},{8,9},{9,8},{10,11... | collective-permute-start | bytes 786440 | tf_op jit(solution)/shard_map/ppermute | solution.py:422
  (11 other events, 46.8 us)
